TPU v7x, 256 devices: a whole 4x4x8 slice. The times are simulated.
256 devices in a mesh: dp: 4 (over y), ep: 64 (over z, x, core).
Axes of the slice: x: 4, y: 4, z: 8, core: 2. Of those that a mesh axis runs over, the one named last changes fastest.
Arguments:
- queries: bfloat16 [2048, 4096], P(('dp', 'ep')), may hold values from -12 to 12
- key_cache: bfloat16 [2048, 64, 256], P(('dp', 'ep')), may hold values from -6 to 6
- value_cache: bfloat16 [2048, 64, 256], P(('dp', 'ep')), may hold values from -6 to 6
- new_keys: bfloat16 [2048, 256], P(('dp', 'ep')), may hold values from -6 to 6
- new_values: bfloat16 [2048, 256], P(('dp', 'ep')), may hold values from -6 to 6
- cache_lengths: int32 [2048], P(('dp', 'ep')), may hold values from 2 to 63, as said below
- residual: bfloat16 [2048, 4096], P(('dp', 'ep')), may hold values from -6 to 6
- move_plan: int32 [2048, 2], P(('dp', 'ep')), may hold values from 0 to 2047, as said below
- norm_gain: float32 [4096], replicated, may hold values from 0.5 to 1.5
- expert_ids: int32 [2048, 8], P(('dp', 'ep')), may hold values from 0 to 63, all different within a row; in each aligned block of 8 rows (0 to 7, 8 to 15, ...) at most 2 rows name the same one
- gate_weights: float32 [2048, 8], P(('dp', 'ep')), may hold values from 0.1 to 1
- w_gate: bfloat16 [64, 4096, 1536], P('ep', None, 'dp'), may hold values from -0.09375 to 0.09375
- w_up: bfloat16 [64, 4096, 1536], P('ep', None, 'dp'), may hold values from -0.09375 to 0.09375
- w_down: bfloat16 [64, 1536, 4096], P('ep', 'dp'), may hold values from -0.15625 to 0.15625
Outputs:
- layer_out: bfloat16 [2048, 4096], P(('dp', 'ep'))
- keys_out: bfloat16 [2048, 64, 256], P(('dp', 'ep'))
- values_out: bfloat16 [2048, 64, 256], P(('dp', 'ep'))
Inputs may be any that keep to these rules, and one draw needn't show every extreme that they name: `move_plan`: requests move only between devices of the same index of dp. Exactly 2 requests leave each device: for each d < 2, one goes to the device 1 + d * 31 indices further along ep (wrapping around), and exactly 2 arrive at each device, one from each of the devices that many indices before it, into the slots that it vacates. Column 0 names the slot whose request a slot holds after the move (itself if it stays), column 1 the slot that its own request moves to (itself if it stays). `cache_lengths`: every device's 8 requests include one of length 63. `expert_ids`: within the 8 rows of one device no expert is named by more than 2 rows, a bound that some block reaches.
All inputs are finite; a program needn't handle non-finite values.
Results may differ from a plain program's by a relative error of at most 0.011.
Values may be sent and summed in bfloat16 or wider, within the bound.
No kernel may reach another device: no remote copies, remote signals or barrier semaphores. Data moves between devices by JAX's collectives and lax.ppermute only.
A program may use at most 128 MiB of HBM per device.

v0:
```python
import math

import jax
import jax.numpy as jnp
from jax import lax
from jax.sharding import PartitionSpec as P

HD = 128
TOP = 8


def pick_floats(selection, arrays):
    selector = selection.astype(jnp.bfloat16)
    return tuple(
        (
            jnp.dot(selector, member, preferred_element_type=jnp.float32).astype(jnp.bfloat16)
            for member in arrays
        )
    )


def pick_ints(selection, member):
    return jnp.sum(jnp.where(selection, member[None, :], 0), axis=1).astype(jnp.int32)


def expert_terms(row_block, w_gate, w_up, w_down):
    gate_proj = jnp.dot(row_block, w_gate[0], preferred_element_type=jnp.float32)
    up_proj = jnp.dot(row_block, w_up[0], preferred_element_type=jnp.float32)
    hidden = (jax.nn.silu(gate_proj) * up_proj).astype(jnp.bfloat16)
    return jnp.dot(hidden, w_down[0], preferred_element_type=jnp.float32)


def local(
    queries,
    key_cache,
    value_cache,
    new_keys,
    new_values,
    cache_lengths,
    residual,
    move_plan,
    norm_gain,
    expert_ids,
    gate_weights,
    w_gate,
    w_up,
    w_down,
):
    per_device = queries.shape[0]
    model_width = queries.shape[1]
    slot_count = key_cache.shape[1]
    kv_width = key_cache.shape[2]
    ep_count = lax.axis_size("ep")
    own_rank = lax.axis_index("ep")
    own_slots = (lax.axis_index("dp") * ep_count + own_rank) * per_device + jnp.arange(
        per_device, dtype=jnp.int32
    )
    source = move_plan[:, 0]
    target = move_plan[:, 1]
    arriving = source != own_slots
    leaving = target != own_slots
    flat_keys = key_cache.reshape(per_device, slot_count * kv_width)
    flat_values = value_cache.reshape(per_device, slot_count * kv_width)
    resident = (flat_keys, flat_values, queries, residual, new_keys, new_values)
    target_rank = target // per_device % ep_count
    addressed = (jnp.arange(ep_count, dtype=jnp.int32)[:, None] == target_rank[None, :]) & leaving[
        None, :
    ]
    send_keys, send_values, send_queries, send_residual, send_new_keys, send_new_values = (
        pick_floats(addressed, resident)
    )
    send_lengths = pick_ints(addressed, cache_lengths)
    received = (
        lax.all_to_all(send_keys, "ep", split_axis=0, concat_axis=0, tiled=True),
        lax.all_to_all(send_values, "ep", split_axis=0, concat_axis=0, tiled=True),
        lax.all_to_all(send_queries, "ep", split_axis=0, concat_axis=0, tiled=True),
        lax.all_to_all(send_residual, "ep", split_axis=0, concat_axis=0, tiled=True),
        lax.all_to_all(send_new_keys, "ep", split_axis=0, concat_axis=0, tiled=True),
        lax.all_to_all(send_new_values, "ep", split_axis=0, concat_axis=0, tiled=True),
        lax.all_to_all(send_lengths, "ep", split_axis=0, concat_axis=0, tiled=True),
    )
    anchor_rank = source // per_device % ep_count
    take_mask = (anchor_rank[:, None] == jnp.arange(ep_count, dtype=jnp.int32)[None, :]) & arriving[
        :, None
    ]
    incoming = pick_floats(take_mask, received[:6])
    floats_now = tuple(
        (
            jnp.where(arriving[:, None], new_member, old_member)
            for new_member, old_member in zip(incoming, resident)
        )
    )
    arrived = floats_now + (jnp.where(arriving, pick_ints(take_mask, received[6]), cache_lengths),)
    moved_keys, moved_values, moved_queries, moved_residual, fresh_keys, fresh_values, lengths = (
        arrived
    )
    position_ids = jnp.arange(slot_count, dtype=jnp.int32)
    newest = (position_ids[None, :] == lengths[:, None])[:, :, None]
    keys_out = jnp.where(
        newest, fresh_keys[:, None, :], moved_keys.reshape(per_device, slot_count, kv_width)
    )
    values_out = jnp.where(
        newest, fresh_values[:, None, :], moved_values.reshape(per_device, slot_count, kv_width)
    )
    kv_heads = kv_width // HD
    groups = model_width // HD // kv_heads
    query_heads = moved_queries.reshape(per_device, kv_heads, groups, HD)
    scores = jnp.einsum(
        "rkgd,rpkd->rkgp",
        query_heads,
        keys_out.reshape(per_device, slot_count, kv_heads, HD),
        preferred_element_type=jnp.float32,
    ) * (1.0 / math.sqrt(HD))
    visible = (position_ids[None, :] <= lengths[:, None])[:, None, None, :]
    scores = jnp.where(visible, scores, -jnp.inf)
    highest = jnp.max(scores, axis=-1, keepdims=True)
    weights = jnp.exp(scores - highest)
    probabilities = (weights / jnp.sum(weights, axis=-1, keepdims=True)).astype(jnp.bfloat16)
    attended = jnp.einsum(
        "rkgp,rpkd->rkgd",
        probabilities,
        values_out.reshape(per_device, slot_count, kv_heads, HD),
        preferred_element_type=jnp.float32,
    ).reshape(per_device, model_width)
    summed = moved_residual.astype(jnp.float32) + attended
    normed = (
        summed * lax.rsqrt(jnp.mean(summed * summed, axis=-1, keepdims=True) + 1e-06) * norm_gain
    ).astype(jnp.bfloat16)
    route_flat = expert_ids.reshape(-1)
    most_rows = max(2, min(per_device, per_device * TOP // ep_count + 1))
    buffer_rows = ep_count * most_rows
    route_marks = (route_flat[:, None] == jnp.arange(ep_count, dtype=jnp.int32)[None, :]).astype(
        jnp.int32
    )
    before = jnp.cumsum(route_marks, axis=0) - route_marks
    route_place = jnp.sum(before * route_marks, axis=1)
    slot_index = route_flat * most_rows + route_place
    placing = jnp.arange(buffer_rows, dtype=jnp.int32)[:, None] == slot_index[None, :]
    placing = jnp.any(placing.reshape(buffer_rows, per_device, TOP), axis=2)
    outgoing = jnp.dot(
        placing.astype(jnp.bfloat16), normed, preferred_element_type=jnp.float32
    ).astype(jnp.bfloat16)
    arrived_rows = lax.all_to_all(
        outgoing.reshape(ep_count, most_rows, model_width),
        "ep",
        split_axis=0,
        concat_axis=0,
        tiled=True,
    )
    everyone = lax.all_gather(
        arrived_rows.reshape(buffer_rows, model_width), "dp", axis=0, tiled=True
    )
    combined = lax.psum_scatter(
        expert_terms(everyone, w_gate, w_up, w_down).astype(jnp.bfloat16),
        "dp",
        scatter_dimension=0,
        tiled=True,
    )
    results = combined.reshape(ep_count, most_rows, model_width)
    returned_rows = lax.all_to_all(results, "ep", split_axis=0, concat_axis=0, tiled=True).reshape(
        buffer_rows, model_width
    )
    picked = returned_rows[slot_index].astype(jnp.float32).reshape(per_device, TOP, model_width)
    mixture = jnp.sum(picked * gate_weights[:, :, None], axis=1)
    layer_out = (summed + mixture).astype(jnp.bfloat16)
    return (layer_out, keys_out, values_out)


def solution(mesh):
    placed = (
        P(("dp", "ep"), None),
        P(("dp", "ep"), None, None),
        P(("dp", "ep"), None, None),
        P(("dp", "ep"), None),
        P(("dp", "ep"), None),
        P(("dp", "ep")),
        P(("dp", "ep"), None),
        P(("dp", "ep"), None),
        P(),
        P(("dp", "ep"), None),
        P(("dp", "ep"), None),
        P("ep", None, "dp"),
        P("ep", None, "dp"),
        P("ep", "dp", None),
    )
    return jax.shard_map(
        local,
        mesh=mesh,
        in_specs=placed,
        out_specs=(P(("dp", "ep"), None), P(("dp", "ep"), None, None), P(("dp", "ep"), None, None)),
        check_vma=False,
    )
```

profile of v0, /device:TPU:1, one launch (start us, length us, event | category | flops | bytes accessed | tf_op | source)
XLA Modules:
  0.0 454.4 jit_solution(3129565528432223180)
XLA Ops:
  7.2 0.9 and_select_fusion
  8.1 0.8 bitcast_compare_fusion
  10.3 13.0 %all-to-all-start.1 = ((s32[64,1,1]{2,1,0:T(1,128)}), s32[64,1,1]{2,1,0:T(1,128)S(1)}, u32[]{:S(2)}, u32[]{:S(2)}) async-start(s32[64,1,1]{2,1,0:T(1,128)} %copy.53), calls=%async_computation.1 | async-start | bytes 65536 | tf_op jit(solution)/shard_map/all_to_all | solution.py:80
  23.3 1.0 fusion.29
  26.0 6.6 %all-to-all-done.1 = s32[64,1,1]{2,1,0:T(1,128)S(1)} async-done(((s32[64,1,1]{2,1,0:T(1,128)}), s32[64,1,1]{2,1,0:T(1,128)S(1)}, u32[]{:S(2)}, u32[]{:S(2)}) %all-to-all-start.1) | async-done | bytes 288 | tf_op jit(solution)/shard_map/all_to_all | solution.py:80
  33.2 4.7 %all-to-all-start.3 = ((bf16[64,2,128]{2,1,0:T(2,128)(2,1)}), bf16[64,2,128]{2,1,0:T(2,128)(2,1)S(1)}, u32[]{:S(2)}, u32[]{:S(2)}) async-start(bf16[64,2,128]{2,1,0:T(2,128)(2,1)} %reshape.251), calls=%async_computation.3 | async-start | bytes 65536 | tf_op jit(solution)/shard_map/all_to_all | solution.py:78
  37.9 1.0 fusion.30
  40.1 7.2 %all-to-all-done.3 = bf16[64,2,128]{2,1,0:T(2,128)(2,1)S(1)} async-done(((bf16[64,2,128]{2,1,0:T(2,128)(2,1)}), bf16[64,2,128]{2,1,0:T(2,128)(2,1)S(1)}, u32[]{:S(2)}, u32[]{:S(2)}) %all-to-all-start.3) | async-done | bytes 32800 | tf_op jit(solution)/shard_map/all_to_all | solution.py:78
  47.3 4.7 %all-to-all-start.5 = ((bf16[64,2,128]{2,1,0:T(2,128)(2,1)}), bf16[64,2,128]{2,1,0:T(2,128)(2,1)S(1)}, u32[]{:S(2)}, u32[]{:S(2)}) async-start(bf16[64,2,128]{2,1,0:T(2,128)(2,1)} %reshape.247), calls=%async_computation.5 | async-start | bytes 65536 | tf_op jit(solution)/shard_map/all_to_all | solution.py:79
  52.0 2.0 fusion.6
  54.1 2.6 reduce.5
  56.7 2.2 reshape.253
  58.9 2.5 all-to-all-done.5
  61.5 8.1 %all-to-all-start.2 = ((bf16[64,2,2048]{2,1,0:T(2,128)(2,1)}), bf16[64,2,2048]{2,1,0:T(2,128)(2,1)}, u32[]{:S(2)}, u32[]{:S(2)}) async-start(bf16[64,2,2048]{2,1,0:T(2,128)(2,1)} %reshape.253), calls=%async_computation.2 | async-start | bytes 1048576 | tf_op jit(solution)/shard_map/all_to_all | solution.py:76
  69.6 1.2 fusion.5
  70.8 2.6 reduce.6
  73.5 2.2 reshape.243
  75.7 11.5 %all-to-all-done.2 = bf16[64,2,2048]{2,1,0:T(2,128)(2,1)} async-done(((bf16[64,2,2048]{2,1,0:T(2,128)(2,1)}), bf16[64,2,2048]{2,1,0:T(2,128)(2,1)}, u32[]{:S(2)}, u32[]{:S(2)}) %all-to-all-start.2) | async-done | bytes 524320 | tf_op jit(solution)/shard_map/all_to_all | solution.py:76
  87.2 5.9 %all-to-all-start = ((bf16[64,2,2048]{2,1,0:T(2,128)(2,1)}), bf16[64,2,2048]{2,1,0:T(2,128)(2,1)}, u32[]{:S(2)}, u32[]{:S(2)}) async-start(bf16[64,2,2048]{2,1,0:T(2,128)(2,1)} %reshape.243), calls=%async_computation | async-start | bytes 1048576 | tf_op jit(solution)/shard_map/all_to_all | solution.py:77
  93.1 1.1 copy.72
  94.2 2.2 fusion.1
  96.4 4.4 reduce.3
  100.8 4.5 reshape.249
  105.3 5.5 %all-to-all-done = bf16[64,2,2048]{2,1,0:T(2,128)(2,1)} async-done(((bf16[64,2,2048]{2,1,0:T(2,128)(2,1)}), bf16[64,2,2048]{2,1,0:T(2,128)(2,1)}, u32[]{:S(2)}, u32[]{:S(2)}) %all-to-all-start) | async-done | bytes 524320 | tf_op jit(solution)/shard_map/all_to_all | solution.py:77
  110.7 5.9 %all-to-all-start.4 = ((bf16[64,2,8192]{2,1,0:T(2,128)(2,1)}), bf16[64,2,8192]{2,1,0:T(2,128)(2,1)}, u32[]{:S(2)}, u32[]{:S(2)}) async-start(bf16[64,2,8192]{2,1,0:T(2,128)(2,1)} %reshape.249), calls=%async_computation.4 | async-start | bytes 4194304 | tf_op jit(solution)/shard_map/all_to_all | solution.py:74
  116.7 1.1 copy.73
  118.5 2.2 fusion.2
  120.7 4.4 reduce.1
  125.1 4.5 reshape.245
  129.6 36.7 %all-to-all-done.4 = bf16[64,2,8192]{2,1,0:T(2,128)(2,1)} async-done(((bf16[64,2,8192]{2,1,0:T(2,128)(2,1)}), bf16[64,2,8192]{2,1,0:T(2,128)(2,1)}, u32[]{:S(2)}, u32[]{:S(2)}) %all-to-all-start.4) | async-done | bytes 2097184 | tf_op jit(solution)/shard_map/all_to_all | solution.py:74
  166.3 7.2 %all-to-all-start.6 = ((bf16[64,2,8192]{2,1,0:T(2,128)(2,1)}), bf16[64,2,8192]{2,1,0:T(2,128)(2,1)}, u32[]{:S(2)}, u32[]{:S(2)}) async-start(bf16[64,2,8192]{2,1,0:T(2,128)(2,1)} %reshape.245), calls=%async_computation.6 | async-start | bytes 4194304 | tf_op jit(solution)/shard_map/all_to_all | solution.py:75
  174.3 1.4 reduce_window_sum.11
  175.7 0.9 select_reduce_fusion
  179.4 2.0 reduce
  182.9 1.4 reshape.252
  184.3 1.0 fusion.31
  186.0 1.4 reshape.248
  187.4 1.0 fusion.32
  189.0 4.5 reshape.254
  193.4 4.4 reshape.244
  197.9 2.5 fusion.10
  200.4 10.5 %reshape.250 = bf16[64,1,16384]{2,1,0:T(2,128)(2,1)} reshape(bf16[64,2,8192]{2,1,0:T(2,128)(2,1)} %all-to-all-done.4) | data formatting | bytes 4194304
  210.9 4.5 fusion.3
  215.4 1.0 fusion.28
  217.3 5.8 %all-to-all-done.6 = bf16[64,2,8192]{2,1,0:T(2,128)(2,1)} async-done(((bf16[64,2,8192]{2,1,0:T(2,128)(2,1)}), bf16[64,2,8192]{2,1,0:T(2,128)(2,1)}, u32[]{:S(2)}, u32[]{:S(2)}) %all-to-all-start.6) | async-done | bytes 2097184 | tf_op jit(solution)/shard_map/all_to_all | solution.py:75
  223.1 10.4 %reshape.246 = bf16[64,1,16384]{2,1,0:T(2,128)(2,1)} reshape(bf16[64,2,8192]{2,1,0:T(2,128)(2,1)} %all-to-all-done.6) | data formatting | bytes 4194304
  233.5 5.2 %fusion.4 = bf16[8,16384]{1,0:T(8,128)(2,1)} fusion(bf16[8,16384]{1,0:T(8,128)(2,1)S(1)} %bitcast.103, bf16[64,1,16384]{2,1,0:T(2,128)(2,1)} %reshape.246, pred[8]{0:T(512)(128)(4,1)S(1)} %compare_bitcast_fusion, s32[8]{0:T(128)S(1)} %copy-done.15), kind=kOutput, calls=%fused_computation.9 | convolution fusion | flops 17040384 | bytes 2621480 | tf_op jit(solution)/shard_map/dot_general | solution.py:16
  238.8 1.7 fusion.41
  240.5 2.0 multiply_reduce_fusion
  242.5 1.5 convolution_convert_fusion.5
  244.0 2.5 reshape.227
  246.6 35.1 %all_to_all.91 = bf16[64,2,4096]{2,1,0:T(2,128)(2,1)} all-to-all(bf16[64,2,4096]{2,1,0:T(2,128)(2,1)} %reshape.227), channel_id=1, replica_groups=mesh['dp'=4,'ep'=64] {'ep'}, dimensions={0} | all-to-all | bytes 2097152 | tf_op jit(solution)/shard_map/all_to_all | solution.py:143
  281.7 2.3 reshape.228
  284.2 48.0 %all-gather.2.cloned.1.call-done = bf16[512,4096]{1,0:T(8,128)(2,1)} async-done(((bf16[128,4096]{1,0:T(8,128)(2,1)}), bf16[512,4096]{1,0:T(8,128)(2,1)}) %all-gather.2.cloned.1.call-update) | async-done | bytes 4194320 | tf_op jit(solution)/shard_map/all_gather | solution.py:150
  332.2 6.4 %fusion.14 = f32[512,384]{1,0:T(8,128)} fusion(bf16[512,4096]{1,0:T(8,128)(2,1)} %all-gather.2.cloned.1.call-done, bf16[1,4096,384]{2,1,0:T(8,128)(2,1)} %param.25), kind=kOutput, calls=%fused_computation.25 | convolution fusion | flops 1610612736 | bytes 8126464 | tf_op jit(solution)/shard_map/dot_general | solution.py:27
  338.7 9.8 %convolution_convert_fusion.4 = bf16[512,4096]{1,0:T(8,128)(2,1)} fusion(bf16[1,384,4096]{2,1,0:T(8,128)(2,1)S(1)} %copy-done, bf16[512,4096]{1,0:T(8,128)(2,1)} %all-gather.2.cloned.1.call-done, bf16[1,4096,384]{2,1,0:T(8,128)(2,1)} %param.26, f32[512,384]{1,0:T(8,128)} %fusion.14), kind=kOutput, calls=%fused_computation.10 | convolution fusion | flops 3224502272 | bytes 15466496 | tf_op jit(solution)/shard_map/dot_general | solution.py:30
  348.5 49.9 %reduce-scatter.2.cloned.1.call-done = bf16[128,4096]{1,0:T(8,128)(2,1)} async-done(((bf16[512,4096]{1,0:T(8,128)(2,1)}), bf16[128,4096]{1,0:T(8,128)(2,1)}) %reduce-scatter.2.cloned.1.call-update) | async-done | bytes 1048592 | tf_op jit(solution)/shard_map/reduce_scatter | solution.py:153
  398.4 2.5 reshape.229
  400.9 10.8 %all-to-all-start.8 = ((bf16[64,2,4096]{2,1,0:T(2,128)(2,1)}), bf16[64,2,4096]{2,1,0:T(2,128)(2,1)}, u32[]{:S(2)}, u32[]{:S(2)}) async-start(bf16[64,2,4096]{2,1,0:T(2,128)(2,1)} %reshape.229), calls=%async_computation.9 | async-start | bytes 2097152 | tf_op jit(solution)/shard_map/all_to_all | solution.py:160
  413.0 1.9 copy_select_fusion
  414.9 24.7 %all-to-all-done.8 = bf16[64,2,4096]{2,1,0:T(2,128)(2,1)} async-done(((bf16[64,2,4096]{2,1,0:T(2,128)(2,1)}), bf16[64,2,4096]{2,1,0:T(2,128)(2,1)}, u32[]{:S(2)}, u32[]{:S(2)}) %all-to-all-start.8) | async-done | bytes 1048608 | tf_op jit(solution)/shard_map/all_to_all | solution.py:160
  439.6 2.3 reshape.230
  441.9 3.5 gather_fusion
  445.4 1.5 fusion.33
  (73 shorter events, 15.0 us)
Async XLA Ops:
  7.2 331.5 %copy-start = (bf16[1,384,4096]{2,1,0:T(8,128)(2,1)S(1)}, bf16[1,384,4096]{2,1,0:T(8,128)(2,1)}, u32[]{:S(2)}) copy-start(bf16[1,384,4096]{2,1,0:T(8,128)(2,1)} %param.27) | copy-start | bytes 9437188
  7.2 62.4 %copy-start.6 = (bf16[8,4096]{1,0:T(8,128)(2,1)S(1)}, bf16[8,4096]{1,0:T(8,128)(2,1)}, u32[]{:S(2)}) copy-start(bf16[8,4096]{1,0:T(8,128)(2,1)} %param.20) | copy-start | bytes 196612
  10.3 22.3 %all-to-all-start.1 = ((s32[64,1,1]{2,1,0:T(1,128)}), s32[64,1,1]{2,1,0:T(1,128)S(1)}, u32[]{:S(2)}, u32[]{:S(2)}) async-start(s32[64,1,1]{2,1,0:T(1,128)} %copy.53), calls=%async_computation.1 | async-start | bytes 65536 | tf_op jit(solution)/shard_map/all_to_all | solution.py:80
  32.6 0.6 copy-start.10
  33.2 14.1 %all-to-all-start.3 = ((bf16[64,2,128]{2,1,0:T(2,128)(2,1)}), bf16[64,2,128]{2,1,0:T(2,128)(2,1)S(1)}, u32[]{:S(2)}, u32[]{:S(2)}) async-start(bf16[64,2,128]{2,1,0:T(2,128)(2,1)} %reshape.251), calls=%async_computation.3 | async-start | bytes 65536 | tf_op jit(solution)/shard_map/all_to_all | solution.py:78
  47.3 28.4 %copy-start.7 = (bf16[64,2,128]{2,1,0:T(2,128)(2,1)}, bf16[64,2,128]{2,1,0:T(2,128)(2,1)S(1)}, u32[]{:S(2)}) copy-start(bf16[64,2,128]{2,1,0:T(2,128)(2,1)S(1)} %all-to-all-done.3) | copy-start | bytes 98308
  47.3 14.1 %all-to-all-start.5 = ((bf16[64,2,128]{2,1,0:T(2,128)(2,1)}), bf16[64,2,128]{2,1,0:T(2,128)(2,1)S(1)}, u32[]{:S(2)}, u32[]{:S(2)}) async-start(bf16[64,2,128]{2,1,0:T(2,128)(2,1)} %reshape.247), calls=%async_computation.5 | async-start | bytes 65536 | tf_op jit(solution)/shard_map/all_to_all | solution.py:79
  61.5 31.7 %copy-start.8 = (bf16[64,2,128]{2,1,0:T(2,128)(2,1)}, bf16[64,2,128]{2,1,0:T(2,128)(2,1)S(1)}, u32[]{:S(2)}) copy-start(bf16[64,2,128]{2,1,0:T(2,128)(2,1)S(1)} %all-to-all-done.5) | copy-start | bytes 98308
  61.5 25.7 %all-to-all-start.2 = ((bf16[64,2,2048]{2,1,0:T(2,128)(2,1)}), bf16[64,2,2048]{2,1,0:T(2,128)(2,1)}, u32[]{:S(2)}, u32[]{:S(2)}) async-start(bf16[64,2,2048]{2,1,0:T(2,128)(2,1)} %reshape.253), calls=%async_computation.2 | async-start | bytes 1048576 | tf_op jit(solution)/shard_map/all_to_all | solution.py:76
  87.2 23.6 %all-to-all-start = ((bf16[64,2,2048]{2,1,0:T(2,128)(2,1)}), bf16[64,2,2048]{2,1,0:T(2,128)(2,1)}, u32[]{:S(2)}, u32[]{:S(2)}) async-start(bf16[64,2,2048]{2,1,0:T(2,128)(2,1)} %reshape.243), calls=%async_computation | async-start | bytes 1048576 | tf_op jit(solution)/shard_map/all_to_all | solution.py:77
  110.7 55.5 %all-to-all-start.4 = ((bf16[64,2,8192]{2,1,0:T(2,128)(2,1)}), bf16[64,2,8192]{2,1,0:T(2,128)(2,1)}, u32[]{:S(2)}, u32[]{:S(2)}) async-start(bf16[64,2,8192]{2,1,0:T(2,128)(2,1)} %reshape.249), calls=%async_computation.4 | async-start | bytes 4194304 | tf_op jit(solution)/shard_map/all_to_all | solution.py:74
  117.8 0.7 copy-start.1
  129.6 44.0 %copy-start.13 = (s32[8,8]{1,0:T(8,128)S(1)}, s32[8,8]{1,0:T(8,128)}, u32[]{:S(2)}) copy-start(s32[8,8]{1,0:T(8,128)} %param.23) | copy-start | bytes 772
  129.6 68.3 %copy-start.5 = (bf16[8,4096]{1,0:T(8,128)(2,1)S(1)}, bf16[8,4096]{1,0:T(8,128)(2,1)}, u32[]{:S(2)}) copy-start(bf16[8,4096]{1,0:T(8,128)(2,1)} %param.14) | copy-start | bytes 196612
  166.3 56.8 %all-to-all-start.6 = ((bf16[64,2,8192]{2,1,0:T(2,128)(2,1)}), bf16[64,2,8192]{2,1,0:T(2,128)(2,1)}, u32[]{:S(2)}, u32[]{:S(2)}) async-start(bf16[64,2,8192]{2,1,0:T(2,128)(2,1)} %reshape.245), calls=%async_computation.6 | async-start | bytes 4194304 | tf_op jit(solution)/shard_map/all_to_all | solution.py:75
  173.5 158.8 %all-gather.2.cloned.1.call-start = ((), (), s32[]{:S(2)}) async-start(), calls=%async_computation.10 | async-start | bytes 5242880 | tf_op jit(solution)/shard_map/all_gather | solution.py:150
  176.7 0.5 copy-start.21
  179.4 6.6 %copy-start.14 = (s32[8]{0:T(128)}, s32[8]{0:T(128)S(1)}, u32[]{:S(2)}) copy-start(s32[8]{0:T(128)S(1)} %fusion.94) | copy-start | bytes 100
  200.4 15.0 %copy-start.11 = (bf16[8,4096]{1,0:T(8,128)(2,1)S(1)}, bf16[8,4096]{1,0:T(8,128)(2,1)}, u32[]{:S(2)}) copy-start(bf16[8,4096]{1,0:T(8,128)(2,1)} %fusion.10) | copy-start | bytes 196612
  215.4 1.0 copy-start.3
  216.4 0.7 copy-start.9
  217.2 16.3 %copy-start.2 = (bf16[1,8,64,256]{3,1,2,0:T(8,128)(2,1)S(1)}, bf16[1,8,64,256]{3,1,2,0:T(8,128)(2,1)}, u32[]{:S(2)}) copy-start(bf16[1,8,64,256]{3,1,2,0:T(8,128)(2,1)} %copy-done.1) | copy-start | bytes 786436
  217.2 16.3 %copy-start.15 = (s32[8]{0:T(128)S(1)}, s32[8]{0:T(128)}, u32[]{:S(2)}) copy-start(s32[8]{0:T(128)} %copy-done.14) | copy-start | bytes 100
  217.3 21.5 %copy-start.18 = (pred[8,64]{1,0:T(8,128)(4,1)S(1)}, pred[8,64]{1,0:T(8,128)(4,1)}, u32[]{:S(2)}) copy-start(pred[8,64]{1,0:T(8,128)(4,1)} %get-tuple-element.8) | copy-start | bytes 1540
  217.3 21.5 %copy-start.20 = (bf16[8,2,128]{2,1,0:T(2,128)(2,1)S(1)}, bf16[8,2,128]{2,1,0:T(2,128)(2,1)}, u32[]{:S(2)}) copy-start(bf16[8,2,128]{2,1,0:T(2,128)(2,1)} %copy.61) | copy-start | bytes 12292
  233.5 9.0 %copy-start.12 = (f32[4096]{0:T(1024)S(1)}, f32[4096]{0:T(1024)}, u32[]{:S(2)}) copy-start(f32[4096]{0:T(1024)} %param.22) | copy-start | bytes 49156
  233.5 9.0 %copy-start.17 = (pred[128,8]{0,1:T(8,128)(4,1)S(1)}, pred[128,8]{0,1:T(8,128)(4,1)}, u32[]{:S(2)}) copy-start(pred[128,8]{0,1:T(8,128)(4,1)} %fusion.55) | copy-start | bytes 3076
  284.0 114.4 %reduce-scatter.2.cloned.1.call-start = ((), (), s32[]{:S(2)}) async-start(), calls=%async_computation.11 | async-start | bytes 5242880 | tf_op jit(solution)/shard_map/reduce_scatter | solution.py:153
  348.5 64.5 %copy-start.4 = (bf16[8,16384]{1,0:T(8,128)(2,1)S(1)}, bf16[8,16384]{1,0:T(8,128)(2,1)}, u32[]{:S(2)}) copy-start(bf16[8,16384]{1,0:T(8,128)(2,1)} %copy-done.3) | copy-start | bytes 786436
  348.5 64.5 %copy-start.19 = (pred[8,64]{1,0:T(8,128)(4,1)S(1)}, pred[8,64]{1,0:T(8,128)(4,1)}, u32[]{:S(2)}) copy-start(pred[8,64]{1,0:T(8,128)(4,1)} %get-tuple-element.8) | copy-start | bytes 1540
  400.9 38.7 %all-to-all-start.8 = ((bf16[64,2,4096]{2,1,0:T(2,128)(2,1)}), bf16[64,2,4096]{2,1,0:T(2,128)(2,1)}, u32[]{:S(2)}, u32[]{:S(2)}) async-start(bf16[64,2,4096]{2,1,0:T(2,128)(2,1)} %reshape.229), calls=%async_computation.9 | async-start | bytes 2097152 | tf_op jit(solution)/shard_map/all_to_all | solution.py:160
  414.9 30.5 %copy-start.16 = (f32[8,8]{1,0:T(8,128)S(1)}, f32[8,8]{1,0:T(8,128)}, u32[]{:S(2)}) copy-start(f32[8,8]{1,0:T(8,128)} %param.24) | copy-start | bytes 772
Sparse Core Ops, SparseCore 0:
  284.1 48.1 all-gather.1
  348.6 49.7 reduce-scatter.1
where the time goes:
time: 457 us; the launch traced here: 454 us
  waiting for transfers between devices  198 us (43%)
  local copies, waits for them, and re-layouts  68.4 us (15%)
  starting transfers between devices  60.6 us (13%)
  matrix products  46.2 us (10%)
  blocking collectives  35.1 us (8%)
  other arithmetic  31.2 us (7%)
  between operations  14.4 us (3%)
    unnamed x58, local copies, waits for them, and re-layouts  52.1 us
    reduce_scatter x1, waiting for transfers between devices, local(): lax.psum_scatter(expert_terms(everyone, w_gate, w_up, w_down).astype(jnp....  49.9 us
    all_gather x1, waiting for transfers between devices, local(): lax.all_gather(arrived_rows.reshape(buffer_rows, model_width), 'dp', axis...  48 us
    all_to_all x1, waiting for transfers between devices, local(): lax.all_to_all(send_keys, 'ep', split_axis=0, concat_axis=0, tiled=True)  36.7 us
    all_to_all x1, blocking collectives, local(): lax.all_to_all(outgoing.reshape(ep_count, most_rows, model_width), 'ep',...  35.1 us
    dot_general x12, matrix products, pick_floats(): jnp.dot(selector, member, preferred_element_type=jnp.float32)  25.8 us
    all_to_all x1, waiting for transfers between devices, local(): lax.all_to_all(results, 'ep', split_axis=0, concat_axis=0, tiled=True)  24.7 us
    all_to_all x1, starting transfers between devices, local(): lax.all_to_all(send_lengths, 'ep', split_axis=0, concat_axis=0, tiled=True)  13 us
  transfers between devices with their start and end apart: 10, of which 10 were waited for; matrix products, arithmetic and copies ran while one was open for 19% of the time, Pallas kernels for 0%

commit v1 on v0

v1 whole, which is shorter than its diff:
```python
import math

import jax
import jax.numpy as jnp
from jax import lax
from jax.experimental import pallas as pl
from jax.experimental.pallas import tpu as pltpu
from jax.sharding import PartitionSpec as P

HD = 128
TOP = 8
MIG = 2
MOST = 2
COLS = 8
STEP = 512
F32 = jnp.float32
BF16 = jnp.bfloat16
VMEM = pl.BlockSpec(memory_space=pltpu.VMEM)
HBM = pl.BlockSpec(memory_space=pltpu.HBM)


def iota(shape, dim):
    return lax.broadcasted_iota(jnp.int32, shape, dim)


def one_hot(condition):
    return jnp.where(condition, 1.0, 0.0).astype(BF16)


def distances(ep_count):
    return tuple(1 + d * (ep_count // 2 - 1) for d in range(MIG))


def find_slot(plan_ref, column, rank, per_device, ep_count):
    found = jnp.int32(0)
    for r in range(per_device):
        other = lax.rem(lax.div(plan_ref[column, r], per_device), ep_count)
        found = jnp.where(other == rank, jnp.int32(r), found)
    return found


def attend_kernel(
    ep_count,
    lengths_ref,
    plan_ref,
    queries_ref,
    keys_ref,
    values_ref,
    new_keys_ref,
    new_values_ref,
    residual_ref,
    ids_ref,
    gain_ref,
    keys_out_ref,
    values_out_ref,
    carry_ref,
    row0_ref,
    row1_ref,
    cache0_ref,
    cache1_ref,
):
    requests, slots, width = keys_ref.shape
    heads = queries_ref.shape[1] // HD
    kv_heads = width // HD
    groups = heads // kv_heads
    fresh_keys = new_keys_ref[...].astype(F32)
    fresh_values = new_values_ref[...].astype(F32)
    position = iota((slots, width), 0)
    for r in range(requests):
        newest = position == lengths_ref[r]
        keys_out_ref[r] = jnp.where(
            newest, fresh_keys[r : r + 1], keys_ref[r].astype(F32)
        ).astype(BF16)
        values_out_ref[r] = jnp.where(
            newest, fresh_values[r : r + 1], values_ref[r].astype(F32)
        ).astype(BF16)
    total = requests * slots
    column = iota((groups * requests, total), 1)
    holder = lax.div(column, slots)
    limit = jnp.zeros_like(column)
    for r in range(requests):
        limit = jnp.where(holder == r, lengths_ref[r], limit)
    own_row = lax.rem(iota((groups * requests, total), 0), requests)
    visible = (holder == own_row) & (lax.rem(column, slots) <= limit)
    queries = queries_ref[...].astype(F32)
    residual = residual_ref[...].astype(F32)
    all_keys = keys_out_ref[...].reshape(total, width)
    all_values = values_out_ref[...].reshape(total, width)
    for k in range(kv_heads):
        stacked = jnp.concatenate(
            [
                queries[:, (k * groups + h) * HD : (k * groups + h + 1) * HD]
                for h in range(groups)
            ],
            axis=0,
        ).astype(BF16)
        scores = lax.dot_general(
            stacked,
            all_keys[:, k * HD : (k + 1) * HD],
            (((1,), (1,)), ((), ())),
            preferred_element_type=F32,
        ) * (1.0 / math.sqrt(HD))
        scores = jnp.where(visible, scores, -jnp.inf)
        weights = jnp.exp(scores - jnp.max(scores, axis=1, keepdims=True))
        probabilities = (weights / jnp.sum(weights, axis=1, keepdims=True)).astype(BF16)
        attended = jnp.dot(
            probabilities, all_values[:, k * HD : (k + 1) * HD], preferred_element_type=F32
        )
        for h in range(groups):
            place = slice((k * groups + h) * HD, (k * groups + h + 1) * HD)
            carry_ref[0:requests, place] = (
                residual[:, place] + attended[h * requests : (h + 1) * requests]
            )
    rank = lax.axis_index("ep")
    summed = carry_ref[0:requests]
    row_number = iota(summed.shape, 0)
    for d, (distance, row_ref, cache_ref) in enumerate(
        zip(distances(ep_count), (row0_ref, row1_ref), (cache0_ref, cache1_ref))
    ):
        slot = find_slot(plan_ref, 1, lax.rem(rank + distance, ep_count), requests, ep_count)
        row_ref[...] = jnp.sum(jnp.where(row_number == slot, summed, 0.0), axis=0, keepdims=True)
        cache_ref[0:slots] = keys_out_ref[slot]
        cache_ref[slots : 2 * slots] = values_out_ref[slot]
        origin = lax.rem(rank + ep_count - distance, ep_count)
        arrival = find_slot(plan_ref, 0, origin, requests, ep_count)
        carry_ref[2 * requests : 3 * requests, (2 + d) * HD : (3 + d) * HD] = jnp.where(
            iota((requests, HD), 0) == arrival, 1.0, 0.0
        )
    carry_ref[requests : 2 * requests] = jnp.broadcast_to(gain_ref[...], summed.shape)
    chosen, _, earlier = routes(ids_ref[...], None, ep_count)
    carry_ref[2 * requests : 3 * requests, 0:ep_count] = chosen
    carry_ref[2 * requests : 3 * requests, HD : HD + ep_count] = earlier


def routes(ids, gates, experts):
    rows = ids.shape[0]
    expert = iota((rows, experts), 1)
    chosen = jnp.zeros((rows, experts), F32)
    weight = jnp.zeros((rows, experts), F32)
    for k in range(TOP):
        same = ids[:, k : k + 1] == expert
        chosen = jnp.where(same, 1.0, chosen)
        if gates is not None:
            weight = jnp.where(same, gates[:, k : k + 1], weight)
    earlier = []
    running = jnp.zeros((1, experts), F32)
    for r in range(rows):
        earlier.append(running)
        running = running + chosen[r : r + 1]
    return chosen, weight, jnp.concatenate(earlier, axis=0)


def place_kernel(ep_count, carry_ref, row0_ref, row1_ref, summed_out_ref, slots_ref):
    rows, model_width = summed_out_ref.shape
    summed = carry_ref[0:rows]
    notes = slice(2 * rows, 3 * rows)
    for d, row_ref in enumerate((row0_ref, row1_ref)):
        arrival = carry_ref[notes, (2 + d) * HD : (2 + d) * HD + 1]
        summed = jnp.where(arrival > 0.5, row_ref[...], summed)
    summed_out_ref[...] = summed
    scale = lax.rsqrt(jnp.mean(summed * summed, axis=1, keepdims=True) + 1e-06)
    normed = summed * scale * carry_ref[rows : 2 * rows]
    part = model_width // COLS
    pieces = jnp.concatenate(
        [normed[:, c * part : (c + 1) * part] for c in range(COLS)], axis=0
    ).astype(BF16)
    chosen = carry_ref[notes, 0:ep_count]
    earlier = carry_ref[notes, HD : HD + ep_count]
    deep = MOST * COLS
    wide = (ep_count * deep, ep_count)
    spread = one_hot(lax.div(iota(wide, 0), deep) == iota(wide, 1))
    repeat_shape = (rows, COLS * rows)
    repeat = one_hot(iota(repeat_shape, 0) == lax.rem(iota(repeat_shape, 1), rows))
    pick_shape = (ep_count * deep, COLS * rows)
    row_here = iota(pick_shape, 0)
    same_part = lax.rem(row_here, COLS) == lax.div(iota(pick_shape, 1), rows)
    slot_here = lax.rem(lax.div(row_here, COLS), MOST)
    pick = jnp.zeros(pick_shape, F32)
    for s in range(MOST):
        placed = jnp.where(earlier == float(s), chosen, 0.0).astype(BF16)
        by_expert = lax.dot_general(
            placed, repeat, (((0,), (0,)), ((), ())), preferred_element_type=F32
        ).astype(BF16)
        by_piece = jnp.dot(spread, by_expert, preferred_element_type=F32)
        pick = jnp.where(same_part & (slot_here == s), by_piece, pick)
    slots_ref[...] = jnp.dot(pick.astype(BF16), pieces, preferred_element_type=F32).astype(BF16)


def regroup(rows):
    shape = (rows, rows)
    count = rows // COLS
    first = iota(shape, 0)
    return one_hot(
        iota(shape, 1) == lax.rem(first, count) * COLS + lax.div(first, count)
    )


def expert_kernel(n_pieces, n_blocks, *refs):
    piece_refs = refs[:n_pieces]
    gate_ref, up_ref, down_ref = refs[n_pieces : n_pieces + 3]
    out_refs = refs[n_pieces + 3 : n_pieces + 3 + n_blocks]
    rows_ref = refs[-1]
    model_width, hidden_width = gate_ref.shape[1:]
    count = STEP // COLS
    part = model_width // COLS
    order = regroup(STEP)
    n = 0
    for ref in piece_refs:
        for m in range(ref.shape[0] // STEP):
            sorted_rows = jnp.dot(
                order, ref[m * STEP : (m + 1) * STEP], preferred_element_type=F32
            ).astype(BF16)
            for c in range(COLS):
                rows_ref[n * count : (n + 1) * count, c * part : (c + 1) * part] = sorted_rows[
                    c * count : (c + 1) * count
                ]
            n += 1
    rows = rows_ref[...]
    gate_proj = jnp.dot(rows, gate_ref[0], preferred_element_type=F32)
    up_proj = jnp.dot(rows, up_ref[0], preferred_element_type=F32)
    hidden = (gate_proj / (1.0 + jnp.exp(-gate_proj)) * up_proj).astype(BF16)
    for c in range(COLS):
        term = jnp.dot(
            hidden, down_ref[0, :, c * part : (c + 1) * part], preferred_element_type=F32
        ).astype(BF16)
        for n in range(n_blocks):
            out_refs[n][c * count : (c + 1) * count] = term[n * count : (n + 1) * count]


def relay_kernel(right_ref, left_ref, from_left_ref, from_right_ref, to_right_ref, to_left_ref):
    to_right_ref[...] = (right_ref[...].astype(F32) + from_left_ref[...].astype(F32)).astype(BF16)
    to_left_ref[...] = (left_ref[...].astype(F32) + from_right_ref[...].astype(F32)).astype(BF16)


def gather_kernel(
    own_top_ref,
    own_bottom_ref,
    left_top_ref,
    left_bottom_ref,
    right_top_ref,
    right_bottom_ref,
    out_ref,
):
    order = regroup(STEP)
    for i, refs in enumerate(
        (
            (own_top_ref, left_top_ref, right_top_ref),
            (own_bottom_ref, left_bottom_ref, right_bottom_ref),
        )
    ):
        total = sum(ref[...].astype(F32) for ref in refs).astype(BF16)
        out_ref[i * STEP : (i + 1) * STEP] = lax.dot_general(
            order, total, (((0,), (0,)), ((), ())), preferred_element_type=F32
        ).astype(BF16)


def mix_kernel(ids_ref, gates_ref, summed_ref, returned_ref, out_ref):
    rows, model_width = summed_ref.shape
    deep = MOST * COLS
    experts = returned_ref.shape[0] // deep
    part = model_width // COLS
    chosen, weight, earlier = routes(ids_ref[...], gates_ref[...], experts)
    repeat_shape = (COLS * rows, rows)
    repeat = one_hot(lax.rem(iota(repeat_shape, 0), rows) == iota(repeat_shape, 1))
    wide = (experts, experts * deep)
    spread = one_hot(iota(wide, 0) == lax.div(iota(wide, 1), deep))
    pick_shape = (COLS * rows, experts * deep)
    column = iota(pick_shape, 1)
    same_part = lax.div(iota(pick_shape, 0), rows) == lax.rem(column, COLS)
    slot_here = lax.rem(lax.div(column, COLS), MOST)
    returned = returned_ref[...]
    coarse_pick = jnp.zeros(pick_shape, F32)
    fine_pick = jnp.zeros(pick_shape, F32)
    for s in range(MOST):
        placed = jnp.where((earlier == float(s)) & (chosen > 0.5), weight, 0.0)
        coarse = placed.astype(BF16)
        fine = (placed - coarse.astype(F32)).astype(BF16)
        here = same_part & (slot_here == s)
        by_row = jnp.dot(
            jnp.dot(repeat, coarse, preferred_element_type=F32).astype(BF16),
            spread,
            preferred_element_type=F32,
        )
        coarse_pick = jnp.where(here, by_row, coarse_pick)
        by_row = jnp.dot(
            jnp.dot(repeat, fine, preferred_element_type=F32).astype(BF16),
            spread,
            preferred_element_type=F32,
        )
        fine_pick = jnp.where(here, by_row, fine_pick)
    mixture = jnp.dot(coarse_pick.astype(BF16), returned, preferred_element_type=F32)
    mixture += jnp.dot(fine_pick.astype(BF16), returned, preferred_element_type=F32)
    for c in range(COLS):
        here = slice(c * part, (c + 1) * part)
        out_ref[:, here] = (
            summed_ref[:, here] + mixture[c * rows : (c + 1) * rows]
        ).astype(BF16)


def settle_kernel(
    ep_count,
    plan_ref,
    cache0_ref,
    cache1_ref,
    keys_in_ref,
    values_in_ref,
    keys_ref,
    values_ref,
    sems,
):
    del keys_in_ref, values_in_ref
    requests, slots, _ = keys_ref.shape
    rank = lax.axis_index("ep")
    copies = []
    for d, (distance, cache_ref) in enumerate(zip(distances(ep_count), (cache0_ref, cache1_ref))):
        origin = lax.rem(rank + ep_count - distance, ep_count)
        slot = find_slot(plan_ref, 0, origin, requests, ep_count)
        for i, ref in enumerate((keys_ref, values_ref)):
            copies.append(
                pltpu.make_async_copy(
                    cache_ref.at[pl.ds(i * slots, slots)], ref.at[slot], sems.at[d, i]
                )
            )
            copies[-1].start()
    for copy in copies:
        copy.wait()


def shape_of(shape, dtype):
    return jax.ShapeDtypeStruct(shape, dtype)


def call(kernel, outs, scalars, staged, resident, flops, moved, limit=16, scratch=()):
    n_scalars, n_staged, n_resident = map(len, (scalars, staged, resident))
    n_outs = len(outs) if isinstance(outs, tuple) else 1

    def body(*refs):
        refs = list(refs)

        def take(count):
            taken = refs[:count]
            del refs[:count]
            return taken

        scalar_refs, sources, resident_refs, out_refs = map(
            take, (n_scalars, n_staged, n_resident, n_outs)
        )
        own_refs = take(len(scratch))
        staged_refs = take(n_staged)
        copies = [
            pltpu.make_async_copy(source, target, refs[0].at[i])
            for i, (source, target) in enumerate(zip(sources, staged_refs))
        ]
        for copy in copies:
            copy.start()
        for copy in copies:
            copy.wait()
        kernel(*scalar_refs, *staged_refs, *resident_refs, *out_refs, *own_refs)

    stages = [pltpu.VMEM(arg.shape, arg.dtype) for arg in staged]
    if staged:
        stages.append(pltpu.SemaphoreType.DMA((n_staged,)))
    return pl.pallas_call(
        body,
        out_shape=outs,
        grid_spec=pltpu.PrefetchScalarGridSpec(
            num_scalar_prefetch=n_scalars,
            grid=(),
            in_specs=[HBM] * n_staged + [VMEM] * n_resident,
            out_specs=tuple([VMEM] * n_outs) if isinstance(outs, tuple) else VMEM,
            scratch_shapes=[*scratch, *stages],
        ),
        compiler_params=pltpu.CompilerParams(vmem_limit_bytes=limit * 2**20),
        cost_estimate=pl.CostEstimate(flops=flops, bytes_accessed=moved, transcendentals=0),
    )(*scalars, *staged, *resident)


def experts_of(pieces, weights):
    rows = sum(piece.shape[0] for piece in pieces)
    part = pieces[0].shape[1]
    n_blocks = rows // STEP
    model_width, hidden_width = weights[0].shape[1:]
    tokens = rows // COLS

    def kernel(*refs):
        expert_kernel(len(pieces), n_blocks, *refs)

    return call(
        kernel,
        tuple(shape_of((STEP, part), BF16) for _ in range(n_blocks)),
        (),
        (),
        (*pieces, *weights),
        6 * tokens * model_width * hidden_width,
        6 * model_width * hidden_width + 4 * rows * part,
        limit=20,
        scratch=[pltpu.VMEM((tokens, model_width), BF16)],
    )


def rotate(member, axis, distance):
    count = lax.axis_size(axis)
    return lax.ppermute(member, axis, [(s, (s + distance) % count) for s in range(count)])


def exchange(member):
    experts = lax.axis_size("ep")
    cut = member.reshape(experts, member.shape[0] // experts, member.shape[1])
    cut = lax.all_to_all(cut, "ep", split_axis=0, concat_axis=0, tiled=True)
    return cut.reshape(member.shape)


def after(member, *earlier):
    return lax.optimization_barrier((member, *earlier))[0]


def through_experts(own, weights, beside):
    from_left = rotate(own, "dp", 1)
    from_right = rotate(own, "dp", -1)
    own_top, own_bottom = experts_of([own], weights)
    from_left, from_right, own_top, own_bottom, *beside = lax.optimization_barrier(
        (from_left, from_right, own_top, own_bottom, *beside)
    )
    far_top = rotate(from_left[:STEP], "dp", 1)
    far_bottom = rotate(from_right[STEP:], "dp", -1)
    left_top, left_bottom, right_top, right_bottom = experts_of([from_left, from_right], weights)
    far_top, far_bottom, right_top, left_bottom = lax.optimization_barrier(
        (far_top, far_bottom, right_top, left_bottom)
    )
    direct_left = rotate(after(right_bottom, far_top, far_bottom), "dp", 1)
    direct_right = rotate(after(left_top, far_top, far_bottom), "dp", -1)
    far_terms = experts_of([far_top, far_bottom], weights)
    relayed_left = rotate(far_terms[0], "dp", 1)
    relayed_right = rotate(far_terms[1], "dp", -1)
    block = shape_of(far_top.shape, BF16)
    size = 2 * block.size
    to_right, to_left = call(
        relay_kernel,
        (block, block),
        (),
        (),
        (right_top, left_bottom, relayed_left, relayed_right),
        size,
        5 * size,
    )
    sums_left = rotate(to_right, "dp", 1)
    sums_right = rotate(to_left, "dp", -1)
    sums = call(
        gather_kernel,
        shape_of(own.shape, BF16),
        (),
        (),
        (own_top, own_bottom, sums_left, direct_left, direct_right, sums_right),
        2 * size * STEP,
        8 * size,
    )
    return sums, beside


def local(
    queries,
    key_cache,
    value_cache,
    new_keys,
    new_values,
    cache_lengths,
    residual,
    move_plan,
    norm_gain,
    expert_ids,
    gate_weights,
    w_gate,
    w_up,
    w_down,
):
    requests, model_width = queries.shape
    slots, width = key_cache.shape[1:]
    ep_count = lax.axis_size("ep")
    plan = move_plan.T
    cache = shape_of(key_cache.shape, BF16)
    row = shape_of((1, model_width), F32)
    moving = shape_of((2 * slots, width), BF16)
    summed_shape = shape_of((requests, model_width), F32)
    steps = distances(ep_count)

    def attend(*refs):
        attend_kernel(ep_count, *refs)

    keys, values, carry, row0, row1, cache0, cache1 = call(
        attend,
        (cache, cache, shape_of((3 * requests, model_width), F32), row, row, moving, moving),
        (cache_lengths, plan),
        (
            queries,
            key_cache,
            value_cache,
            new_keys,
            new_values,
            residual,
            expert_ids,
            norm_gain.reshape(1, model_width),
        ),
        (),
        10**8,
        3 * 10**6,
        limit=58,
    )
    got_row0 = rotate(row0, "ep", steps[0])
    got_row1 = rotate(row1, "ep", steps[1])

    def place(*refs):
        place_kernel(ep_count, *refs)

    part = model_width // COLS
    summed, outgoing = call(
        place,
        (summed_shape, shape_of((ep_count * MOST * COLS, part), BF16)),
        (),
        (),
        (carry, got_row0, got_row1),
        10**8,
        2 * 10**6,
    )
    rows = exchange(outgoing)
    cache0, cache1, rows = lax.optimization_barrier((cache0, cache1, rows))
    got_cache0 = rotate(cache0, "ep", steps[0])
    got_cache1 = rotate(cache1, "ep", steps[1])

    def settle(*refs):
        settle_kernel(ep_count, *refs)

    sums, (got_cache0, got_cache1) = through_experts(
        rows, (w_gate, w_up, w_down), (got_cache0, got_cache1)
    )
    keys_out, values_out = pl.pallas_call(
        settle,
        out_shape=(cache, cache),
        grid_spec=pltpu.PrefetchScalarGridSpec(
            num_scalar_prefetch=1,
            grid=(),
            in_specs=[VMEM, VMEM, HBM, HBM],
            out_specs=(HBM, HBM),
            scratch_shapes=[pltpu.SemaphoreType.DMA((MIG, 2))],
        ),
        input_output_aliases={3: 0, 4: 1},
        compiler_params=pltpu.CompilerParams(vmem_limit_bytes=4 * 2**20),
        cost_estimate=pl.CostEstimate(flops=0, bytes_accessed=10**6, transcendentals=0),
    )(plan, got_cache0, got_cache1, keys, values)
    returned = exchange(after(sums, keys_out, values_out))
    layer_out = call(
        mix_kernel,
        shape_of((requests, model_width), BF16),
        (),
        (expert_ids, gate_weights),
        (summed, returned),
        10**8,
        2 * 10**6,
    )
    return (layer_out, keys_out, values_out)


def solution(mesh):
    rows = P(("dp", "ep"), None)
    caches = P(("dp", "ep"), None, None)
    placed = (
        rows,
        caches,
        caches,
        rows,
        rows,
        P(("dp", "ep")),
        rows,
        rows,
        P(),
        rows,
        rows,
        P("ep", None, "dp"),
        P("ep", None, "dp"),
        P("ep", "dp", None),
    )
    return jax.shard_map(
        local,
        mesh=mesh,
        in_specs=placed,
        out_specs=(rows, caches, caches),
        check_vma=False,
    )
```

time: 457 us -> 172 us (0.38)
  waiting for transfers between devices: 198 us -> 43.4 us
  local copies, waits for them, and re-layouts: 68.4 us -> 4.86 us
  matrix products: 46.2 us -> 0 us
  blocking collectives: 35.1 us -> 78.2 us
  starting transfers between devices: 60.6 us -> 26.2 us
  other arithmetic: 31.2 us -> 0 us
  Pallas kernels: 0 us -> 18.5 us
  between operations: 14.4 us -> 0.91 us
    all_to_all x8 -> x0, waiting for transfers between devices: 101 us -> none  [the longest x1 36.7 us: local(): lax.all_to_all(send_keys, 'ep', split_axis=0, concat_axis=0, tiled=True)]
    all_to_all x8 -> x0, starting transfers between devices: 60.3 us -> none  [the longest x1 13 us: local(): lax.all_to_all(send_lengths, 'ep', split_axis=0, concat_axis=0, tiled=True)]
    reduce_scatter x1 -> x0, waiting for transfers between devices: 49.9 us -> none  [local(): lax.psum_scatter(expert_terms(everyone, w_gate, w_up, w_down).astype(jnp....]
    all_gather x1 -> x0, waiting for transfers between devices: 48 us -> none  [local(): lax.all_gather(arrived_rows.reshape(buffer_rows, model_width), 'dp', axis...]
    unnamed x58 -> x14, local copies, waits for them, and re-layouts: 52.1 us -> 4.79 us
    dot_general x17 -> x0, matrix products: 46.2 us -> none  [the longest x12 25.8 us: pick_floats(): jnp.dot(selector, member, preferred_element_type=jnp.float32)]
    ppermute x0 -> x14, waiting for transfers between devices: none -> 43.4 us  [rotate(): lax.ppermute(member, axis, [(s, (s + distance) % count) for s in range(co...]
    all_to_all x1 -> x2, blocking collectives: 35.1 us -> 78.2 us  [exchange(): cut = lax.all_to_all(cut, 'ep', split_axis=0, concat_axis=0, tiled=True)]
  transfers between devices with their start and end apart: 10 -> 14, of which waited for: 10 -> 8; matrix products, arithmetic and copies ran while one was open for 19% -> 0% of each run, Pallas kernels for 0% -> 5%
where the time goes in v1:
time: 172 us
  blocking collectives  78.2 us (45%)
  waiting for transfers between devices  43.4 us (25%)
  starting transfers between devices  26.2 us (15%)
  Pallas kernels  18.5 us (11%)
  local copies, waits for them, and re-layouts  4.86 us (3%)
    all_to_all x2, blocking collectives, exchange(): cut = lax.all_to_all(cut, 'ep', split_axis=0, concat_axis=0, tiled=True)  78.2 us
    ppermute x14, waiting for transfers between devices, rotate(): lax.ppermute(member, axis, [(s, (s + distance) % count) for s in range(co...  43.4 us
    ppermute x14, starting transfers between devices, rotate(): lax.ppermute(member, axis, [(s, (s + distance) % count) for s in range(co...  26.2 us
    pallas_call x8, Pallas kernels, call(): pl.pallas_call(body, out_shape=outs, grid_spec=pltpu.PrefetchScalarGridSp...  17.2 us
    unnamed x14, local copies, waits for them, and re-layouts  4.79 us
  transfers between devices with their start and end apart: 14, of which 8 were waited for; matrix products, arithmetic and copies ran while one was open for 0% of the time, Pallas kernels for 5%

profile of v1, /device:TPU:1, one launch (start us, length us, event | category | flops | bytes accessed | tf_op | source)
XLA Modules:
  0.0 171.9 jit_solution(1382270149129894002)
XLA Ops:
  0.6 0.0 copy-start
  0.6 3.9 %shard_map.157 = (bf16[8,64,256]{2,1,0:T(8,128)(2,1)}, bf16[8,64,256]{2,1,0:T(8,128)(2,1)}, f32[24,4096]{1,0:T(8,128)}, f32[1,4096]{1,0:T(1,128)}, f32[1,4096]{1...) custom-call(s32[8]{0:T(128)} %refs_0_.2, s32[2,8]{1,0:T(2,128)} %bitcast.12, bf16[8,4096]{1,0:T(8,128)(2,1)} %refs_2_.4, ...), custom_call_target="tpu_custom_call" | custom-call | flops 100000000 | bytes 3000000 | tf_op jit(solution)/shard_map/pallas_call | solution.py:363
  4.5 2.7 %collective-permute-start = (f32[1,4096]{1,0:T(1,128)}, f32[1,4096]{1,0:T(1,128)S(1)}, u32[]{:S(2)}, u32[]{:S(2)}) collective-permute-start(f32[1,4096]{1,0:T(1,128)} %get-tuple-element.41), channel_id=1, source_target_pairs={{0,1},{1,2},{2,3},{3,4},{4,5},{5,6},{6,7},{7,8},{8,9},{9,10},{10,1... | collective-permute-start | bytes 49160 | tf_op jit(solution)/shard_map/ppermute | solution.py:403
  7.2 6.9 %collective-permute-start.1 = (f32[1,4096]{1,0:T(1,128)}, f32[1,4096]{1,0:T(1,128)S(1)}, u32[]{:S(2)}, u32[]{:S(2)}) collective-permute-start(f32[1,4096]{1,0:T(1,128)} %get-tuple-element.42), channel_id=1, source_target_pairs={{0,32},{1,33},{2,34},{3,35},{4,36},{5,37},{6,38},{7,39},{8,40},{9,... | collective-permute-start | bytes 49160 | tf_op jit(solution)/shard_map/ppermute | solution.py:403
  14.1 0.0 collective-permute-done.refs_1_
  14.1 1.3 collective-permute-done.1.refs_2_
  15.4 0.0 copy-start.3
  15.4 1.0 copy-done.3
  16.4 0.7 shard_map.158
  17.2 37.9 %all_to_all.10 = bf16[64,16,512]{2,1,0:T(8,128)(2,1)S(1)} all-to-all(bf16[64,16,512]{2,1,0:T(8,128)(2,1)S(1)} %bitcast.11), channel_id=1, replica_groups=mesh['dp'=4,'ep'=64] {'ep'}, dimensions={0} | all-to-all | bytes 2097152 | tf_op jit(solution)/shard_map/all_to_all | solution.py:409
  55.1 1.3 collective-permute-start.2
  56.4 1.4 collective-permute-start.3
  57.9 2.9 %collective-permute-start.4 = (bf16[128,256]{1,0:T(8,128)(2,1)}, bf16[128,256]{1,0:T(8,128)(2,1)S(1)}, u32[]{:S(2)}, u32[]{:S(2)}) collective-permute-start(bf16[128,256]{1,0:T(8,128)(2,1)} %get-tuple-element.50), channel_id=1, source_target_pairs={{0,1},{1,2},{2,3},{3,4},{4,5},{5,6},{6,7},{7,8},{8,9},{9,10},{10,1... | collective-permute-start | bytes 196616 | tf_op jit(solution)/shard_map/ppermute | solution.py:403
  60.8 0.8 collective-permute-start.5
  61.6 0.0 copy-done
  61.6 0.0 copy-start.1
  61.6 1.9 %copy-done.1 = bf16[1,4096,384]{2,1,0:T(8,128)(2,1)S(1)} copy-done((bf16[1,4096,384]{2,1,0:T(8,128)(2,1)S(1)}, bf16[1,4096,384]{2,1,0:T(8,128)(2,1)}, u32[]{:S(2)}) %copy-start.1) | copy-done | bytes 3145752
  63.5 0.0 copy-start.2
  63.5 1.9 %copy-done.2 = bf16[1,384,4096]{2,1,0:T(8,128)(2,1)S(1)} copy-done((bf16[1,384,4096]{2,1,0:T(8,128)(2,1)S(1)}, bf16[1,384,4096]{2,1,0:T(8,128)(2,1)}, u32[]{:S(2)}) %copy-start.2) | copy-done | bytes 3145752
  65.4 2.5 %shard_map.159 = (bf16[512,512]{1,0:T(8,128)(2,1)S(1)}, bf16[512,512]{1,0:T(8,128)(2,1)S(1)}) custom-call(bf16[1024,512]{1,0:T(8,128)(2,1)S(1)} %bitcast.8, bf16[1,4096,384]{2,1,0:T(8,128)(2,1)S(1)} %copy-done, bf16[1,4096,384]{2,1,0:T(8,128)(2,1)S(1)} %copy-done.1, bf16[1,384,4096]{2,1,0:T(8,128)(2,1)S(1)} %copy-done.2), custom_call_target="tpu_custom_call" | custom-call | flops 1207959552 | bytes 11534336 | tf_op jit(solution)/shard_map/pallas_call | solution.py:363
  67.9 0.0 collective-permute-done.4.refs_1_
  67.9 0.6 collective-permute-done.5.refs_2_
  68.5 11.3 %collective-permute-done.2.refs_0_ = bf16[1024,512]{1,0:T(8,128)(2,1)S(1)} collective-permute-done((bf16[1024,512]{1,0:T(8,128)(2,1)S(1)}, bf16[1024,512]{1,0:T(8,128)(2,1)S(1)}, u32[]{:S(2)}, u32[]{:S(2)}) %collective-permute-start.2) | collective-permute-done | bytes 1048608 | tf_op jit(solution)/shard_map/ppermute | solution.py:403
  79.7 0.0 collective-permute-done.3.refs_1_
  79.8 1.0 collective-permute-start.6
  80.9 2.0 %collective-permute-start.7 = (bf16[512,512]{1,0:T(8,128)(2,1)S(1)}, bf16[512,512]{1,0:T(8,128)(2,1)S(1)}, u32[]{:S(2)}, u32[]{:S(2)}) collective-permute-start(bf16[512,512]{1,0:T(8,128)(2,1)S(1)} %slice.7), channel_id=1, source_target_pairs={{0,192},{64,0},{128,64},{192,128},{1,193},{65,1},{129,65},{193,129... | collective-permute-start | bytes 1572872 | tf_op jit(solution)/shard_map/ppermute | solution.py:403
  82.8 4.6 %shard_map.160 = (bf16[512,512]{1,0:T(8,128)(2,1)S(1)}, bf16[512,512]{1,0:T(8,128)(2,1)S(1)}, bf16[512,512]{1,0:T(8,128)(2,1)S(1)}, bf16[512,512]{1,0:T(8,128)(2,1)S(1)}) custom-call(bf16[1024,512]{1,0:T(8,128)(2,1)S(1)} %collective-permute-done.2.refs_0_, bf16[1024,512]{1,0:T(8,128)(2,1)S(1)} %collective-permute-done.3.refs_1_, ...), custom_call_target="tpu_custom_call" | custom-call | flops 2415919104 | bytes 13631488 | tf_op jit(solution)/shard_map/pallas_call | solution.py:363
  87.5 4.8 %collective-permute-done.6.refs_0_ = bf16[512,512]{1,0:T(8,128)(2,1)S(1)} collective-permute-done((bf16[512,512]{1,0:T(8,128)(2,1)S(1)}, bf16[512,512]{1,0:T(8,128)(2,1)S(1)}, u32[]{:S(2)}, u32[]{:S(2)}) %collective-permute-start.6) | collective-permute-done | bytes 524320 | tf_op jit(solution)/shard_map/ppermute | solution.py:403
  92.3 0.0 collective-permute-done.7.refs_1_
  92.3 0.0 copy-start.6
  92.3 2.5 %shard_map.161 = (bf16[512,512]{1,0:T(8,128)(2,1)S(1)}, bf16[512,512]{1,0:T(8,128)(2,1)S(1)}) custom-call(bf16[512,512]{1,0:T(8,128)(2,1)S(1)} %collective-permute-done.6.refs_0_, bf16[512,512]{1,0:T(8,128)(2,1)S(1)} %collective-permute-done.7.refs_1_, bf16[1,4096,384]{2,1,0:T(8,128)(2,1)S(1)} %copy-done, bf16[1,4096,384]{2,1,0:T(8,128)(2,1)S(1)} %copy-done.1, ...), custom_call_target="tpu_custom_call" | custom-call | flops 1207959552 | bytes 11534336 | tf_op jit(solution)/shard_map/pallas_call | solution.py:363
  94.7 0.5 collective-permute-start.8
  95.3 2.3 %collective-permute-start.9 = (bf16[512,512]{1,0:T(8,128)(2,1)S(1)}, bf16[512,512]{1,0:T(8,128)(2,1)S(1)}, u32[]{:S(2)}, u32[]{:S(2)}) collective-permute-start(bf16[512,512]{1,0:T(8,128)(2,1)S(1)} %get-tuple-element.63), channel_id=1, source_target_pairs={{0,192},{64,0},{128,64},{192,128},{1,193},{65,1},{129,65},{193,129... | collective-permute-start | bytes 1572872 | tf_op jit(solution)/shard_map/ppermute | solution.py:403
  97.6 1.4 collective-permute-start.12
  99.0 0.1 collective-permute-start.11
  99.0 7.2 %collective-permute-done.8.refs_2_ = bf16[512,512]{1,0:T(8,128)(2,1)S(1)} collective-permute-done((bf16[512,512]{1,0:T(8,128)(2,1)S(1)}, bf16[512,512]{1,0:T(8,128)(2,1)S(1)}, u32[]{:S(2)}, u32[]{:S(2)}) %collective-permute-start.8) | collective-permute-done | bytes 524320 | tf_op jit(solution)/shard_map/ppermute | solution.py:403
  106.3 0.0 collective-permute-done.9.refs_3_
  106.3 0.2 shard_map.162
  106.5 0.4 collective-permute-start.10
  106.9 2.3 %collective-permute-start.13 = (bf16[512,512]{1,0:T(8,128)(2,1)S(1)}, bf16[512,512]{1,0:T(8,128)(2,1)S(1)}, u32[]{:S(2)}, u32[]{:S(2)}) collective-permute-start(bf16[512,512]{1,0:T(8,128)(2,1)S(1)} %get-tuple-element.69), channel_id=1, source_target_pairs={{0,192},{64,0},{128,64},{192,128},{1,193},{65,1},{129,65},{193,129... | collective-permute-start | bytes 1572872 | tf_op jit(solution)/shard_map/ppermute | solution.py:403
  109.3 0.0 copy-done.6
  109.3 1.3 shard_map.164
  110.5 0.0 copy-start.4
  110.5 0.0 copy-start.5
  110.6 6.0 %collective-permute-done.12.refs_4_ = bf16[512,512]{1,0:T(8,128)(2,1)S(1)} collective-permute-done((bf16[512,512]{1,0:T(8,128)(2,1)S(1)}, bf16[512,512]{1,0:T(8,128)(2,1)S(1)}, u32[]{:S(2)}, u32[]{:S(2)}) %collective-permute-start.12) | collective-permute-done | bytes 524320 | tf_op jit(solution)/shard_map/ppermute | solution.py:403
  116.6 0.9 collective-permute-done.11.refs_3_
  117.5 11.2 %collective-permute-done.10.refs_2_ = bf16[512,512]{1,0:T(8,128)(2,1)S(1)} collective-permute-done((bf16[512,512]{1,0:T(8,128)(2,1)S(1)}, bf16[512,512]{1,0:T(8,128)(2,1)S(1)}, u32[]{:S(2)}, u32[]{:S(2)}) %collective-permute-start.10) | collective-permute-done | bytes 524320 | tf_op jit(solution)/shard_map/ppermute | solution.py:403
  128.7 0.0 collective-permute-done.13.refs_5_
  128.7 0.9 shard_map.163
  129.6 40.2 %all_to_all.11 = bf16[64,16,512]{2,1,0:T(8,128)(2,1)S(1)} all-to-all(bf16[64,16,512]{2,1,0:T(8,128)(2,1)S(1)} %bitcast.10), channel_id=1, replica_groups=mesh['dp'=4,'ep'=64] {'ep'}, dimensions={0} | all-to-all | bytes 2097152 | tf_op jit(solution)/shard_map/all_to_all | solution.py:409
  169.8 0.0 copy-done.4
  169.8 0.0 copy-done.5
  169.8 2.0 %shard_map.165 = bf16[8,4096]{1,0:T(8,128)(2,1)} custom-call(s32[8,8]{1,0:T(8,128)S(1)} %copy-done.4, f32[8,8]{1,0:T(8,128)S(1)} %copy-done.5, f32[8,4096]{1,0:T(8,128)S(1)} %get-tuple-element.43.refs_2_, bf16[1024,512]{1,0:T(8,128)(2,1)S(1)} %bitcast.9), custom_call_target="tpu_custom_call" | custom-call | flops 100000000 | bytes 2000000 | tf_op jit(solution)/shard_map/pallas_call | solution.py:363
  (2 shorter events, 0.1 us)
Async XLA Ops:
  0.6 61.0 %copy-start = (bf16[1,4096,384]{2,1,0:T(8,128)(2,1)S(1)}, bf16[1,4096,384]{2,1,0:T(8,128)(2,1)}, u32[]{:S(2)}) copy-start(bf16[1,4096,384]{2,1,0:T(8,128)(2,1)} %refs_2_.7) | copy-start | bytes 9437188
  4.5 9.6 %collective-permute-start = (f32[1,4096]{1,0:T(1,128)}, f32[1,4096]{1,0:T(1,128)S(1)}, u32[]{:S(2)}, u32[]{:S(2)}) collective-permute-start(f32[1,4096]{1,0:T(1,128)} %get-tuple-element.41), channel_id=1, source_target_pairs={{0,1},{1,2},{2,3},{3,4},{4,5},{5,6},{6,7},{7,8},{8,9},{9,10},{10,1... | collective-permute-start | bytes 49160 | tf_op jit(solution)/shard_map/ppermute | solution.py:403
  7.2 8.2 %collective-permute-start.1 = (f32[1,4096]{1,0:T(1,128)}, f32[1,4096]{1,0:T(1,128)S(1)}, u32[]{:S(2)}, u32[]{:S(2)}) collective-permute-start(f32[1,4096]{1,0:T(1,128)} %get-tuple-element.42), channel_id=1, source_target_pairs={{0,32},{1,33},{2,34},{3,35},{4,36},{5,37},{6,38},{7,39},{8,40},{9,... | collective-permute-start | bytes 49160 | tf_op jit(solution)/shard_map/ppermute | solution.py:403
  15.4 1.0 copy-start.3
  55.1 24.6 %collective-permute-start.2 = (bf16[1024,512]{1,0:T(8,128)(2,1)S(1)}, bf16[1024,512]{1,0:T(8,128)(2,1)S(1)}, u32[]{:S(2)}, u32[]{:S(2)}) collective-permute-start(bf16[1024,512]{1,0:T(8,128)(2,1)S(1)} %bitcast.6), channel_id=1, source_target_pairs={{0,64},{64,128},{128,192},{192,0},{1,65},{65,129},{129,193},{193,1... | collective-permute-start | bytes 3145736 | tf_op jit(solution)/shard_map/ppermute | solution.py:403
  56.4 23.3 %collective-permute-start.3 = (bf16[1024,512]{1,0:T(8,128)(2,1)S(1)}, bf16[1024,512]{1,0:T(8,128)(2,1)S(1)}, u32[]{:S(2)}, u32[]{:S(2)}) collective-permute-start(bf16[1024,512]{1,0:T(8,128)(2,1)S(1)} %bitcast.7), channel_id=1, source_target_pairs={{0,192},{64,0},{128,64},{192,128},{1,193},{65,1},{129,65},{193,129... | collective-permute-start | bytes 3145736 | tf_op jit(solution)/shard_map/ppermute | solution.py:403
  57.9 10.0 %collective-permute-start.4 = (bf16[128,256]{1,0:T(8,128)(2,1)}, bf16[128,256]{1,0:T(8,128)(2,1)S(1)}, u32[]{:S(2)}, u32[]{:S(2)}) collective-permute-start(bf16[128,256]{1,0:T(8,128)(2,1)} %get-tuple-element.50), channel_id=1, source_target_pairs={{0,1},{1,2},{2,3},{3,4},{4,5},{5,6},{6,7},{7,8},{8,9},{9,10},{10,1... | collective-permute-start | bytes 196616 | tf_op jit(solution)/shard_map/ppermute | solution.py:403
  60.8 7.7 %collective-permute-start.5 = (bf16[128,256]{1,0:T(8,128)(2,1)}, bf16[128,256]{1,0:T(8,128)(2,1)S(1)}, u32[]{:S(2)}, u32[]{:S(2)}) collective-permute-start(bf16[128,256]{1,0:T(8,128)(2,1)} %get-tuple-element.51), channel_id=1, source_target_pairs={{0,32},{1,33},{2,34},{3,35},{4,36},{5,37},{6,38},{7,39},{8,40},{9,... | collective-permute-start | bytes 196616 | tf_op jit(solution)/shard_map/ppermute | solution.py:403
  61.6 1.9 %copy-start.1 = (bf16[1,4096,384]{2,1,0:T(8,128)(2,1)S(1)}, bf16[1,4096,384]{2,1,0:T(8,128)(2,1)}, u32[]{:S(2)}) copy-start(bf16[1,4096,384]{2,1,0:T(8,128)(2,1)} %refs_3_.7) | copy-start | bytes 9437188
  63.5 1.9 %copy-start.2 = (bf16[1,384,4096]{2,1,0:T(8,128)(2,1)S(1)}, bf16[1,384,4096]{2,1,0:T(8,128)(2,1)}, u32[]{:S(2)}) copy-start(bf16[1,384,4096]{2,1,0:T(8,128)(2,1)} %refs_4_.5) | copy-start | bytes 9437188
  79.8 12.5 %collective-permute-start.6 = (bf16[512,512]{1,0:T(8,128)(2,1)S(1)}, bf16[512,512]{1,0:T(8,128)(2,1)S(1)}, u32[]{:S(2)}, u32[]{:S(2)}) collective-permute-start(bf16[512,512]{1,0:T(8,128)(2,1)S(1)} %slice.6), channel_id=1, source_target_pairs={{0,64},{64,128},{128,192},{192,0},{1,65},{65,129},{129,193},{193,1... | collective-permute-start | bytes 1572872 | tf_op jit(solution)/shard_map/ppermute | solution.py:403
  80.9 11.4 %collective-permute-start.7 = (bf16[512,512]{1,0:T(8,128)(2,1)S(1)}, bf16[512,512]{1,0:T(8,128)(2,1)S(1)}, u32[]{:S(2)}, u32[]{:S(2)}) collective-permute-start(bf16[512,512]{1,0:T(8,128)(2,1)S(1)} %slice.7), channel_id=1, source_target_pairs={{0,192},{64,0},{128,64},{192,128},{1,193},{65,1},{129,65},{193,129... | collective-permute-start | bytes 1572872 | tf_op jit(solution)/shard_map/ppermute | solution.py:403
  92.3 17.0 %copy-start.6 = (s32[8,2]{0,1:T(2,128)S(1)}, s32[8,2]{0,1:T(2,128)}, u32[]{:S(2)}) copy-start(s32[8,2]{0,1:T(2,128)} %param.21) | copy-start | bytes 196
  94.7 11.5 %collective-permute-start.8 = (bf16[512,512]{1,0:T(8,128)(2,1)S(1)}, bf16[512,512]{1,0:T(8,128)(2,1)S(1)}, u32[]{:S(2)}, u32[]{:S(2)}) collective-permute-start(bf16[512,512]{1,0:T(8,128)(2,1)S(1)} %get-tuple-element.62), channel_id=1, source_target_pairs={{0,64},{64,128},{128,192},{192,0},{1,65},{65,129},{129,193},{193,1... | collective-permute-start | bytes 1572872 | tf_op jit(solution)/shard_map/ppermute | solution.py:403
  95.3 11.0 %collective-permute-start.9 = (bf16[512,512]{1,0:T(8,128)(2,1)S(1)}, bf16[512,512]{1,0:T(8,128)(2,1)S(1)}, u32[]{:S(2)}, u32[]{:S(2)}) collective-permute-start(bf16[512,512]{1,0:T(8,128)(2,1)S(1)} %get-tuple-element.63), channel_id=1, source_target_pairs={{0,192},{64,0},{128,64},{192,128},{1,193},{65,1},{129,65},{193,129... | collective-permute-start | bytes 1572872 | tf_op jit(solution)/shard_map/ppermute | solution.py:403
  97.6 19.0 %collective-permute-start.12 = (bf16[512,512]{1,0:T(8,128)(2,1)S(1)}, bf16[512,512]{1,0:T(8,128)(2,1)S(1)}, u32[]{:S(2)}, u32[]{:S(2)}) collective-permute-start(bf16[512,512]{1,0:T(8,128)(2,1)S(1)} %get-tuple-element.68), channel_id=1, source_target_pairs={{0,192},{64,0},{128,64},{192,128},{1,193},{65,1},{129,65},{193,129... | collective-permute-start | bytes 1572872 | tf_op jit(solution)/shard_map/ppermute | solution.py:403
  99.0 18.5 %collective-permute-start.11 = (bf16[512,512]{1,0:T(8,128)(2,1)S(1)}, bf16[512,512]{1,0:T(8,128)(2,1)S(1)}, u32[]{:S(2)}, u32[]{:S(2)}) collective-permute-start(bf16[512,512]{1,0:T(8,128)(2,1)S(1)} %get-tuple-element.66), channel_id=1, source_target_pairs={{0,64},{64,128},{128,192},{192,0},{1,65},{65,129},{129,193},{193,1... | collective-permute-start | bytes 1572872 | tf_op jit(solution)/shard_map/ppermute | solution.py:403
  106.5 22.2 %collective-permute-start.10 = (bf16[512,512]{1,0:T(8,128)(2,1)S(1)}, bf16[512,512]{1,0:T(8,128)(2,1)S(1)}, u32[]{:S(2)}, u32[]{:S(2)}) collective-permute-start(bf16[512,512]{1,0:T(8,128)(2,1)S(1)} %get-tuple-element.64), channel_id=1, source_target_pairs={{0,64},{64,128},{128,192},{192,0},{1,65},{65,129},{129,193},{193,1... | collective-permute-start | bytes 1572872 | tf_op jit(solution)/shard_map/ppermute | solution.py:403
  106.9 21.8 %collective-permute-start.13 = (bf16[512,512]{1,0:T(8,128)(2,1)S(1)}, bf16[512,512]{1,0:T(8,128)(2,1)S(1)}, u32[]{:S(2)}, u32[]{:S(2)}) collective-permute-start(bf16[512,512]{1,0:T(8,128)(2,1)S(1)} %get-tuple-element.69), channel_id=1, source_target_pairs={{0,192},{64,0},{128,64},{192,128},{1,193},{65,1},{129,65},{193,129... | collective-permute-start | bytes 1572872 | tf_op jit(solution)/shard_map/ppermute | solution.py:403
  110.5 59.3 %copy-start.4 = (s32[8,8]{1,0:T(8,128)S(1)}, s32[8,8]{1,0:T(8,128)}, u32[]{:S(2)}) copy-start(s32[8,8]{1,0:T(8,128)} %refs_0_.3) | copy-start | bytes 772
  110.5 59.3 %copy-start.5 = (f32[8,8]{1,0:T(8,128)S(1)}, f32[8,8]{1,0:T(8,128)}, u32[]{:S(2)}) copy-start(f32[8,8]{1,0:T(8,128)} %refs_1_.3) | copy-start | bytes 772

commit v2 on v1

--- a/solution.py
+++ b/solution.py
@@ -13,6 +13,7 @@
 MOST = 2
 COLS = 8
 STEP = 512
+SIDE = 1536
 F32 = jnp.float32
 BF16 = jnp.bfloat16
 VMEM = pl.BlockSpec(memory_space=pltpu.VMEM)
@@ -199,6 +200,7 @@
     piece_refs = refs[:n_pieces]
     gate_ref, up_ref, down_ref = refs[n_pieces : n_pieces + 3]
     out_refs = refs[n_pieces + 3 : n_pieces + 3 + n_blocks]
+    hidden_refs = refs[n_pieces + 3 + n_blocks : -1]
     rows_ref = refs[-1]
     model_width, hidden_width = gate_ref.shape[1:]
     count = STEP // COLS
@@ -219,7 +221,10 @@
     gate_proj = jnp.dot(rows, gate_ref[0], preferred_element_type=F32)
     up_proj = jnp.dot(rows, up_ref[0], preferred_element_type=F32)
     hidden = (gate_proj / (1.0 + jnp.exp(-gate_proj)) * up_proj).astype(BF16)
-    for c in range(COLS):
+    per_group = hidden.shape[0] // len(hidden_refs)
+    for i, ref in enumerate(hidden_refs):
+        ref[...] = hidden[i * per_group : (i + 1) * per_group]
+    for c in range((model_width - SIDE) // part):
         term = jnp.dot(
             hidden, down_ref[0, :, c * part : (c + 1) * part], preferred_element_type=F32
         ).astype(BF16)
@@ -230,6 +235,23 @@
 def relay_kernel(right_ref, left_ref, from_left_ref, from_right_ref, to_right_ref, to_left_ref):
     to_right_ref[...] = (right_ref[...].astype(F32) + from_left_ref[...].astype(F32)).astype(BF16)
     to_left_ref[...] = (left_ref[...].astype(F32) + from_right_ref[...].astype(F32)).astype(BF16)
+
+
+def down_kernel(*refs):
+    hidden_refs, (own_ref, left_ref, right_ref, top_ref, bottom_ref) = refs[:4], refs[4:9]
+    out_refs = refs[9:]
+    far = jnp.concatenate([top_ref[...], bottom_ref[...]], axis=0)
+    matrices = (own_ref[...], left_ref[...], right_ref[...], far)
+    count, part = STEP // COLS, out_refs[0].shape[1]
+    total = jnp.zeros((hidden_refs[0].shape[0], far.shape[1]), F32)
+    for ref, matrix in zip(hidden_refs, matrices):
+        total += jnp.dot(ref[...], matrix, preferred_element_type=F32)
+    total = total.astype(BF16)
+    for i, out_ref in enumerate(out_refs):
+        for c in range(far.shape[1] // part):
+            out_ref[c * count : (c + 1) * count] = total[
+                i * count : (i + 1) * count, c * part : (c + 1) * part
+            ]
 
 
 def gather_kernel(
@@ -239,16 +261,19 @@
     left_bottom_ref,
     right_top_ref,
     right_bottom_ref,
+    side_top_ref,
+    side_bottom_ref,
     out_ref,
 ):
     order = regroup(STEP)
-    for i, refs in enumerate(
+    for i, (side_ref, *refs) in enumerate(
         (
-            (own_top_ref, left_top_ref, right_top_ref),
-            (own_bottom_ref, left_bottom_ref, right_bottom_ref),
+            (side_top_ref, own_top_ref, left_top_ref, right_top_ref),
+            (side_bottom_ref, own_bottom_ref, left_bottom_ref, right_bottom_ref),
         )
     ):
         total = sum(ref[...].astype(F32) for ref in refs).astype(BF16)
+        total = jnp.concatenate([total, side_ref[...]], axis=0)
         out_ref[i * STEP : (i + 1) * STEP] = lax.dot_general(
             order, total, (((0,), (0,)), ((), ())), preferred_element_type=F32
         ).astype(BF16)
@@ -381,13 +406,15 @@
     n_blocks = rows // STEP
     model_width, hidden_width = weights[0].shape[1:]
     tokens = rows // COLS
+    terms = (model_width - SIDE) // part * (STEP // COLS)
 
     def kernel(*refs):
         expert_kernel(len(pieces), n_blocks, *refs)
 
     return call(
         kernel,
-        tuple(shape_of((STEP, part), BF16) for _ in range(n_blocks)),
+        tuple(shape_of((terms, part), BF16) for _ in range(n_blocks))
+        + tuple(shape_of((2 * STEP // COLS, hidden_width), BF16) for _ in range(n_blocks // 2)),
         (),
         (),
         (*pieces, *weights),
@@ -414,25 +441,41 @@
     return lax.optimization_barrier((member, *earlier))[0]
 
 
-def through_experts(own, weights, beside):
+def gather_down(w_down):
+    own = w_down[0, :, w_down.shape[2] - SIDE :]
+    half = own.shape[0] // 2
     from_left = rotate(own, "dp", 1)
     from_right = rotate(own, "dp", -1)
-    own_top, own_bottom = experts_of([own], weights)
+    far_top = rotate(from_left[:half], "dp", 1)
+    far_bottom = rotate(from_right[half:], "dp", -1)
+    return own, from_left, from_right, far_top, far_bottom
+
+
+def through_experts(own, weights, side_weights, beside):
+    own, *side_weights = lax.optimization_barrier((own, *side_weights))
+    from_left = rotate(own, "dp", 1)
+    from_right = rotate(own, "dp", -1)
+    own_top, own_bottom, own_hidden = experts_of([own], weights)
     from_left, from_right, own_top, own_bottom, *beside = lax.optimization_barrier(
         (from_left, from_right, own_top, own_bottom, *beside)
     )
     far_top = rotate(from_left[:STEP], "dp", 1)
     far_bottom = rotate(from_right[STEP:], "dp", -1)
-    left_top, left_bottom, right_top, right_bottom = experts_of([from_left, from_right], weights)
+    left_top, left_bottom, right_top, right_bottom, left_hidden, right_hidden = experts_of(
+        [from_left, from_right], weights
+    )
     far_top, far_bottom, right_top, left_bottom = lax.optimization_barrier(
         (far_top, far_bottom, right_top, left_bottom)
     )
     direct_left = rotate(after(right_bottom, far_top, far_bottom), "dp", 1)
     direct_right = rotate(after(left_top, far_top, far_bottom), "dp", -1)
-    far_terms = experts_of([far_top, far_bottom], weights)
+    *far_terms, far_hidden = experts_of([far_top, far_bottom], weights)
     relayed_left = rotate(far_terms[0], "dp", 1)
     relayed_right = rotate(far_terms[1], "dp", -1)
-    block = shape_of(far_top.shape, BF16)
+    hidden_left = rotate(after(right_hidden, far_top, far_bottom), "dp", 1)
+    hidden_right = rotate(after(left_hidden, far_top, far_bottom), "dp", -1)
+    hidden_far = rotate(far_hidden, "dp", 2)
+    block = shape_of(far_terms[0].shape, BF16)
     size = 2 * block.size
     to_right, to_left = call(
         relay_kernel,
@@ -445,12 +488,32 @@
     )
     sums_left = rotate(to_right, "dp", 1)
     sums_right = rotate(to_left, "dp", -1)
+    part = block.shape[1]
+    side_block = shape_of((SIDE // part * (STEP // COLS), part), BF16)
+    side_top, side_bottom = call(
+        down_kernel,
+        (side_block, side_block),
+        (),
+        (),
+        (own_hidden, hidden_left, hidden_right, hidden_far, *side_weights),
+        10**9,
+        6 * 10**6,
+    )
     sums = call(
         gather_kernel,
-        shape_of(own.shape, BF16),
-        (),
-        (),
-        (own_top, own_bottom, sums_left, direct_left, direct_right, sums_right),
+        shape_of((2 * STEP, part), BF16),
+        (),
+        (),
+        (
+            own_top,
+            own_bottom,
+            sums_left,
+            direct_left,
+            direct_right,
+            sums_right,
+            side_top,
+            side_bottom,
+        ),
         2 * size * STEP,
         8 * size,
     )
@@ -483,6 +546,8 @@
     summed_shape = shape_of((requests, model_width), F32)
     steps = distances(ep_count)
 
+    side_weights = gather_down(w_down)
+
     def attend(*refs):
         attend_kernel(ep_count, *refs)
 
@@ -530,7 +595,7 @@
         settle_kernel(ep_count, *refs)
 
     sums, (got_cache0, got_cache1) = through_experts(
-        rows, (w_gate, w_up, w_down), (got_cache0, got_cache1)
+        rows, (w_gate, w_up, w_down), side_weights, (got_cache0, got_cache1)
     )
     keys_out, values_out = pl.pallas_call(
         settle,

time: 172 us -> 193 us (1.12)
  blocking collectives: 78.2 us -> 45.3 us
  starting transfers between devices: 26.2 us -> 52.2 us
  waiting for transfers between devices: 43.4 us -> 63.1 us
  local copies, waits for them, and re-layouts: 4.86 us -> 9.16 us
  Pallas kernels: 18.5 us -> 21.1 us
    all_to_all x2 -> x1, blocking collectives: 78.2 us -> 45.3 us  [exchange(): cut = lax.all_to_all(cut, 'ep', split_axis=0, concat_axis=0, tiled=True)]
    ppermute x14 -> x21, waiting for transfers between devices: 43.4 us -> 63.1 us  [rotate(): lax.ppermute(member, axis, [(s, (s + distance) % count) for s in range(co...]
    ppermute x14 -> x21, starting transfers between devices: 26.2 us -> 41.8 us  [rotate(): lax.ppermute(member, axis, [(s, (s + distance) % count) for s in range(co...]
    all_to_all x0 -> x1, starting transfers between devices: none -> 10.5 us  [exchange(): cut = lax.all_to_all(cut, 'ep', split_axis=0, concat_axis=0, tiled=True)]
    pallas_call x8 -> x9, Pallas kernels: 17.2 us -> 19.8 us  [call(): pl.pallas_call(body, out_shape=outs, grid_spec=pltpu.PrefetchScalarGridSp...]
    unnamed x14 -> x34, local copies, waits for them, and re-layouts: 4.79 us -> 7.15 us
  transfers between devices with their start and end apart: 14 -> 22, of which waited for: 8 -> 11; matrix products, arithmetic and copies ran while one was open for 0% -> 1% of each run, Pallas kernels for 5% -> 6%
where the time goes in v2:
time: 193 us; the launch traced here: 192 us
  waiting for transfers between devices  63.1 us (33%)
  starting transfers between devices  52.2 us (27%)
  blocking collectives  45.3 us (23%)
  Pallas kernels  21.1 us (11%)
  local copies, waits for them, and re-layouts  9.16 us (5%)
    ppermute x21, waiting for transfers between devices, rotate(): lax.ppermute(member, axis, [(s, (s + distance) % count) for s in range(co...  63.1 us
    all_to_all x1, blocking collectives, exchange(): cut = lax.all_to_all(cut, 'ep', split_axis=0, concat_axis=0, tiled=True)  45.3 us
    ppermute x21, starting transfers between devices, rotate(): lax.ppermute(member, axis, [(s, (s + distance) % count) for s in range(co...  41.8 us
    pallas_call x9, Pallas kernels, call(): pl.pallas_call(body, out_shape=outs, grid_spec=pltpu.PrefetchScalarGridSp...  19.8 us
    all_to_all x1, starting transfers between devices, exchange(): cut = lax.all_to_all(cut, 'ep', split_axis=0, concat_axis=0, tiled=True)  10.5 us
    unnamed x34, local copies, waits for them, and re-layouts  7.15 us
  transfers between devices with their start and end apart: 22, of which 11 were waited for; matrix products, arithmetic and copies ran while one was open for 1% of the time, Pallas kernels for 6%

profile of v2, /device:TPU:1, one launch (start us, length us, event | category | flops | bytes accessed | tf_op | source)
XLA Modules:
  0.0 192.0 jit_solution(2449204495993306388)
XLA Ops:
  0.6 3.9 %shard_map.157 = (bf16[8,64,256]{2,1,0:T(8,128)(2,1)}, bf16[8,64,256]{2,1,0:T(8,128)(2,1)}, f32[24,4096]{1,0:T(8,128)}, f32[1,4096]{1,0:T(1,128)}, f32[1,4096]{1...) custom-call(s32[8]{0:T(128)} %refs_0_.2, s32[2,8]{1,0:T(2,128)} %bitcast.11, bf16[8,4096]{1,0:T(8,128)(2,1)} %refs_2_.4, ...), custom_call_target="tpu_custom_call" | custom-call | flops 100000000 | bytes 3000000 | tf_op jit(solution)/shard_map/pallas_call | solution.py:388
  4.5 2.7 %collective-permute-start = (f32[1,4096]{1,0:T(1,128)}, f32[1,4096]{1,0:T(1,128)S(1)}, u32[]{:S(2)}, u32[]{:S(2)}) collective-permute-start(f32[1,4096]{1,0:T(1,128)} %get-tuple-element.55), channel_id=1, source_target_pairs={{0,1},{1,2},{2,3},{3,4},{4,5},{5,6},{6,7},{7,8},{8,9},{9,10},{10,1... | collective-permute-start | bytes 49160 | tf_op jit(solution)/shard_map/ppermute | solution.py:430
  7.2 6.9 %collective-permute-start.1 = (f32[1,4096]{1,0:T(1,128)}, f32[1,4096]{1,0:T(1,128)S(1)}, u32[]{:S(2)}, u32[]{:S(2)}) collective-permute-start(f32[1,4096]{1,0:T(1,128)} %get-tuple-element.56), channel_id=1, source_target_pairs={{0,32},{1,33},{2,34},{3,35},{4,36},{5,37},{6,38},{7,39},{8,40},{9,... | collective-permute-start | bytes 49160 | tf_op jit(solution)/shard_map/ppermute | solution.py:430
  14.1 0.0 collective-permute-done.refs_1_
  14.1 1.3 collective-permute-done.1.refs_2_
  15.4 1.0 copy-done.11
  16.4 0.7 shard_map.158
  17.2 1.0 copy-done.10
  18.2 10.5 %all-to-all-start = ((bf16[64,16,512]{2,1,0:T(8,128)(2,1)}), bf16[64,16,512]{2,1,0:T(8,128)(2,1)}, u32[]{:S(2)}, u32[]{:S(2)}) async-start(bf16[64,16,512]{2,1,0:T(8,128)(2,1)} %bitcast.10), calls=%async_computation | async-start | bytes 2097152 | tf_op jit(solution)/shard_map/all_to_all | solution.py:436
  28.7 0.1 slice_bitcast_fusion.refs_4_
  28.8 2.8 %collective-permute-start.3 = (bf16[384,1536]{1,0:T(8,128)(2,1)S(1)}, bf16[384,1536]{1,0:T(8,128)(2,1)S(1)}, u32[]{:S(2)}, u32[]{:S(2)}) collective-permute-start(bf16[384,1536]{1,0:T(8,128)(2,1)S(1)} %slice_bitcast_fusion.refs_4_), channel_id=1, source_target_pairs={{0,192},{64,0},{128,64},{192,128},{1,193},{65,1},{129,65},{193,129... | collective-permute-start | bytes 3538952 | tf_op jit(solution)/shard_map/ppermute | solution.py:430
  31.6 0.0 collective-permute-start.2
  31.6 1.0 copy-done.4
  32.6 23.8 %collective-permute-done.3.refs_6_ = bf16[384,1536]{1,0:T(8,128)(2,1)S(1)} collective-permute-done((bf16[384,1536]{1,0:T(8,128)(2,1)S(1)}, bf16[384,1536]{1,0:T(8,128)(2,1)S(1)}, u32[]{:S(2)}, u32[]{:S(2)}) %collective-permute-start.3) | collective-permute-done | bytes 1179680 | tf_op jit(solution)/shard_map/ppermute | solution.py:430
  56.4 0.9 slice.21
  57.3 3.5 %collective-permute-start.5 = (bf16[192,1536]{1,0:T(8,128)(2,1)}, bf16[192,1536]{1,0:T(8,128)(2,1)}, u32[]{:S(2)}, u32[]{:S(2)}) collective-permute-start(bf16[192,1536]{1,0:T(8,128)(2,1)} %slice.21), channel_id=1, source_target_pairs={{0,192},{64,0},{128,64},{192,128},{1,193},{65,1},{129,65},{193,129... | collective-permute-start | bytes 1769480 | tf_op jit(solution)/shard_map/ppermute | solution.py:430
  60.8 0.0 collective-permute-done.2.refs_5_
  60.8 0.9 slice.20
  61.8 0.3 copy-done.8
  62.1 0.0 collective-permute-start.4
  62.1 0.0 all-to-all-done
  62.1 10.4 %collective-permute-done.5.refs_8_ = bf16[192,1536]{1,0:T(8,128)(2,1)} collective-permute-done((bf16[192,1536]{1,0:T(8,128)(2,1)}, bf16[192,1536]{1,0:T(8,128)(2,1)}, u32[]{:S(2)}, u32[]{:S(2)}) %collective-permute-start.5) | collective-permute-done | bytes 589856 | tf_op jit(solution)/shard_map/ppermute | solution.py:430
  72.5 4.4 %collective-permute-done.4.refs_7_ = bf16[192,1536]{1,0:T(8,128)(2,1)} collective-permute-done((bf16[192,1536]{1,0:T(8,128)(2,1)}, bf16[192,1536]{1,0:T(8,128)(2,1)}, u32[]{:S(2)}, u32[]{:S(2)}) %collective-permute-start.4) | collective-permute-done | bytes 589856 | tf_op jit(solution)/shard_map/ppermute | solution.py:430
  76.8 0.0 collective-permute-start.7
  76.8 1.5 collective-permute-start.6
  78.3 4.5 %collective-permute-start.8 = (bf16[128,256]{1,0:T(8,128)(2,1)S(1)}, bf16[128,256]{1,0:T(8,128)(2,1)S(1)}, u32[]{:S(2)}, u32[]{:S(2)}) collective-permute-start(bf16[128,256]{1,0:T(8,128)(2,1)S(1)} %copy-done.16), channel_id=1, source_target_pairs={{0,1},{1,2},{2,3},{3,4},{4,5},{5,6},{6,7},{7,8},{8,9},{9,10},{10,1... | collective-permute-start | bytes 196616 | tf_op jit(solution)/shard_map/ppermute | solution.py:430
  82.8 5.1 %collective-permute-start.9 = (bf16[128,256]{1,0:T(8,128)(2,1)S(1)}, bf16[128,256]{1,0:T(8,128)(2,1)S(1)}, u32[]{:S(2)}, u32[]{:S(2)}) collective-permute-start(bf16[128,256]{1,0:T(8,128)(2,1)S(1)} %copy-done.15), channel_id=1, source_target_pairs={{0,32},{1,33},{2,34},{3,35},{4,36},{5,37},{6,38},{7,39},{8,40},{9,... | collective-permute-start | bytes 196616 | tf_op jit(solution)/shard_map/ppermute | solution.py:430
  87.9 1.9 copy-done.1
  89.8 1.9 copy-done.3
  91.7 3.6 %shard_map.159 = (bf16[320,512]{1,0:T(8,128)(2,1)S(1)}, bf16[320,512]{1,0:T(8,128)(2,1)S(1)}, bf16[128,384]{1,0:T(8,128)(2,1)S(1)}) custom-call(bf16[1024,512]{1,0:T(8,128)(2,1)} %bitcast.3.refs_0_, bf16[1,4096,384]{2,1,0:T(8,128)(2,1)S(1)} %copy-done.1, bf16[1,4096,384]{2,1,0:T(8,128)(2,1)S(1)} %copy-done.3, bf16[1,384,4096]{2,1,0:T(8,128)(2,1)S(1)} %copy-done), custom_call_target="tpu_custom_call" | custom-call | flops 1207959552 | bytes 11534336 | tf_op jit(solution)/shard_map/pallas_call | solution.py:388
  95.3 0.0 collective-permute-done.8.refs_1_
  95.4 0.0 collective-permute-done.9.refs_2_
  95.4 3.9 %collective-permute-done.7.refs_1_ = bf16[1024,512]{1,0:T(8,128)(2,1)S(1)} collective-permute-done((bf16[1024,512]{1,0:T(8,128)(2,1)}, bf16[1024,512]{1,0:T(8,128)(2,1)S(1)}, u32[]{:S(2)}, u32[]{:S(2)}) %collective-permute-start.7) | collective-permute-done | bytes 1048608 | tf_op jit(solution)/shard_map/ppermute | solution.py:430
  99.2 1.2 collective-permute-done.6.refs_0_
  100.5 0.5 collective-permute-start.11
  101.1 1.2 collective-permute-start.10
  102.3 4.2 %shard_map.160 = (bf16[320,512]{1,0:T(8,128)(2,1)S(1)}, bf16[320,512]{1,0:T(8,128)(2,1)S(1)}, bf16[320,512]{1,0:T(8,128)(2,1)S(1)}, bf16[320,512]{1,0:T(8,128)(2...) custom-call(bf16[1024,512]{1,0:T(8,128)(2,1)S(1)} %collective-permute-done.6.refs_0_, ...), custom_call_target="tpu_custom_call" | custom-call | flops 2415919104 | bytes 13631488 | tf_op jit(solution)/shard_map/pallas_call | solution.py:388
  106.5 4.3 %collective-permute-done.11.refs_1_ = bf16[512,512]{1,0:T(8,128)(2,1)S(1)} collective-permute-done((bf16[512,512]{1,0:T(8,128)(2,1)S(1)}, bf16[512,512]{1,0:T(8,128)(2,1)S(1)}, u32[]{:S(2)}, u32[]{:S(2)}) %collective-permute-start.11) | collective-permute-done | bytes 524320 | tf_op jit(solution)/shard_map/ppermute | solution.py:430
  110.8 1.5 collective-permute-done.10.refs_0_
  112.3 2.3 %shard_map.161 = (bf16[320,512]{1,0:T(8,128)(2,1)S(1)}, bf16[320,512]{1,0:T(8,128)(2,1)S(1)}, bf16[128,384]{1,0:T(8,128)(2,1)S(1)}) custom-call(bf16[512,512]{1,0:T(8,128)(2,1)S(1)} %collective-permute-done.10.refs_0_, bf16[512,512]{1,0:T(8,128)(2,1)S(1)} %collective-permute-done.11.refs_1_, bf16[1,4096,384]{2,1,0:T(8,128)(2,1)S(1)} %copy-done.2, ...), custom_call_target="tpu_custom_call" | custom-call | flops 1207959552 | bytes 11534336 | tf_op jit(solution)/shard_map/pallas_call | solution.py:388
  114.6 0.1 collective-permute-start.12
  114.7 2.7 %collective-permute-start.13 = (bf16[320,512]{1,0:T(8,128)(2,1)S(1)}, bf16[320,512]{1,0:T(8,128)(2,1)S(1)}, u32[]{:S(2)}, u32[]{:S(2)}) collective-permute-start(bf16[320,512]{1,0:T(8,128)(2,1)S(1)} %get-tuple-element.78), channel_id=1, source_target_pairs={{0,192},{64,0},{128,64},{192,128},{1,193},{65,1},{129,65},{193,129... | collective-permute-start | bytes 983048 | tf_op jit(solution)/shard_map/ppermute | solution.py:430
  117.3 0.0 collective-permute-start.18
  117.3 0.0 collective-permute-start.15
  117.3 2.7 %collective-permute-start.16 = (bf16[320,512]{1,0:T(8,128)(2,1)S(1)}, bf16[320,512]{1,0:T(8,128)(2,1)S(1)}, u32[]{:S(2)}, u32[]{:S(2)}) collective-permute-start(bf16[320,512]{1,0:T(8,128)(2,1)S(1)} %get-tuple-element.83), channel_id=1, source_target_pairs={{0,192},{64,0},{128,64},{192,128},{1,193},{65,1},{129,65},{193,129... | collective-permute-start | bytes 983048 | tf_op jit(solution)/shard_map/ppermute | solution.py:430
  120.0 1.7 collective-permute-done.12.refs_2_
  121.8 0.0 collective-permute-done.13.refs_3_
  121.8 0.2 shard_map.162
  121.9 0.1 collective-permute-start.14
  122.0 3.0 %collective-permute-start.17 = (bf16[320,512]{1,0:T(8,128)(2,1)S(1)}, bf16[320,512]{1,0:T(8,128)(2,1)S(1)}, u32[]{:S(2)}, u32[]{:S(2)}) collective-permute-start(bf16[320,512]{1,0:T(8,128)(2,1)S(1)} %get-tuple-element.84), channel_id=1, source_target_pairs={{0,192},{64,0},{128,64},{192,128},{1,193},{65,1},{129,65},{193,129... | collective-permute-start | bytes 983048 | tf_op jit(solution)/shard_map/ppermute | solution.py:430
  125.0 0.0 collective-permute-done.18.refs_1_
  125.0 1.2 collective-permute-start.19
  126.2 9.7 %collective-permute-done.19.refs_2_ = bf16[128,384]{1,0:T(8,128)(2,1)S(1)} collective-permute-done((bf16[128,384]{1,0:T(8,128)(2,1)S(1)}, bf16[128,384]{1,0:T(8,128)(2,1)S(1)}, u32[]{:S(2)}, u32[]{:S(2)}) %collective-permute-start.19) | collective-permute-done | bytes 98336 | tf_op jit(solution)/shard_map/ppermute | solution.py:430
  135.9 3.4 %collective-permute-start.20 = (bf16[128,384]{1,0:T(8,128)(2,1)S(1)}, bf16[128,384]{1,0:T(8,128)(2,1)S(1)}, u32[]{:S(2)}, u32[]{:S(2)}) collective-permute-start(bf16[128,384]{1,0:T(8,128)(2,1)S(1)} %get-tuple-element.90), channel_id=1, source_target_pairs={{0,128},{64,192},{128,0},{192,64},{1,129},{65,193},{129,1},{193,65... | collective-permute-start | bytes 294920 | tf_op jit(solution)/shard_map/ppermute | solution.py:430
  139.2 1.3 shard_map.165
  140.5 0.9 collective-permute-done.20.refs_3_
  141.4 2.2 %shard_map.163 = (bf16[192,512]{1,0:T(8,128)(2,1)S(1)}, bf16[192,512]{1,0:T(8,128)(2,1)S(1)}) custom-call(bf16[128,384]{1,0:T(8,128)(2,1)S(1)} %get-tuple-element.85.refs_0_, bf16[128,384]{1,0:T(8,128)(2,1)S(1)} %collective-permute-done.18.refs_1_, bf16[128,384]{1,0:T(8,128)(2,1)S(1)} %collective-permute-done.19.refs_2_, ...), custom_call_target="tpu_custom_call" | custom-call | flops 1000000000 | bytes 6000000 | tf_op jit(solution)/shard_map/pallas_call | solution.py:388
  143.6 0.0 copy-start.12
  143.6 0.0 copy-start.13
  143.7 0.0 collective-permute-done.16.refs_4_
  143.7 0.0 collective-permute-done.14.refs_2_
  143.7 0.8 shard_map.164
  144.6 45.3 %all_to_all.10 = bf16[64,16,512]{2,1,0:T(8,128)(2,1)S(1)} all-to-all(bf16[64,16,512]{2,1,0:T(8,128)(2,1)S(1)} %bitcast.8), channel_id=1, replica_groups=mesh['dp'=4,'ep'=64] {'ep'}, dimensions={0} | all-to-all | bytes 2097152 | tf_op jit(solution)/shard_map/all_to_all | solution.py:436
  189.8 2.0 %shard_map.166 = bf16[8,4096]{1,0:T(8,128)(2,1)} custom-call(s32[8,8]{1,0:T(8,128)S(1)} %copy-done.12, f32[8,8]{1,0:T(8,128)S(1)} %copy-done.13, f32[8,4096]{1,0:T(8,128)S(1)} %get-tuple-element.57.refs_2_, bf16[1024,512]{1,0:T(8,128)(2,1)S(1)} %bitcast.9), custom_call_target="tpu_custom_call" | custom-call | flops 100000000 | bytes 2000000 | tf_op jit(solution)/shard_map/pallas_call | solution.py:388
  (30 shorter events, 0.1 us)
Async XLA Ops:
  0.6 28.0 %copy-start = (bf16[1,384,4096]{2,1,0:T(8,128)(2,1)S(1)}, bf16[1,384,4096]{2,1,0:T(8,128)(2,1)}, u32[]{:S(2)}) copy-start(bf16[1,384,4096]{2,1,0:T(8,128)(2,1)} %refs_4_.5) | copy-start | bytes 9437188
  4.5 9.6 %collective-permute-start = (f32[1,4096]{1,0:T(1,128)}, f32[1,4096]{1,0:T(1,128)S(1)}, u32[]{:S(2)}, u32[]{:S(2)}) collective-permute-start(f32[1,4096]{1,0:T(1,128)} %get-tuple-element.55), channel_id=1, source_target_pairs={{0,1},{1,2},{2,3},{3,4},{4,5},{5,6},{6,7},{7,8},{8,9},{9,10},{10,1... | collective-permute-start | bytes 49160 | tf_op jit(solution)/shard_map/ppermute | solution.py:430
  7.2 8.2 %collective-permute-start.1 = (f32[1,4096]{1,0:T(1,128)}, f32[1,4096]{1,0:T(1,128)S(1)}, u32[]{:S(2)}, u32[]{:S(2)}) collective-permute-start(f32[1,4096]{1,0:T(1,128)} %get-tuple-element.56), channel_id=1, source_target_pairs={{0,32},{1,33},{2,34},{3,35},{4,36},{5,37},{6,38},{7,39},{8,40},{9,... | collective-permute-start | bytes 49160 | tf_op jit(solution)/shard_map/ppermute | solution.py:430
  15.4 1.0 copy-start.11
  17.2 1.0 copy-start.10
  18.2 60.1 %copy-start.16 = (bf16[128,256]{1,0:T(8,128)(2,1)S(1)}, bf16[128,256]{1,0:T(8,128)(2,1)}, u32[]{:S(2)}) copy-start(bf16[128,256]{1,0:T(8,128)(2,1)} %get-tuple-element.65) | copy-start | bytes 196612
  18.2 64.6 %copy-start.15 = (bf16[128,256]{1,0:T(8,128)(2,1)S(1)}, bf16[128,256]{1,0:T(8,128)(2,1)}, u32[]{:S(2)}) copy-start(bf16[128,256]{1,0:T(8,128)(2,1)} %get-tuple-element.66) | copy-start | bytes 196612
  18.2 43.9 %all-to-all-start = ((bf16[64,16,512]{2,1,0:T(8,128)(2,1)}), bf16[64,16,512]{2,1,0:T(8,128)(2,1)}, u32[]{:S(2)}, u32[]{:S(2)}) async-start(bf16[64,16,512]{2,1,0:T(8,128)(2,1)} %bitcast.10), calls=%async_computation | async-start | bytes 2097152 | tf_op jit(solution)/shard_map/all_to_all | solution.py:436
  28.8 27.6 %collective-permute-start.3 = (bf16[384,1536]{1,0:T(8,128)(2,1)S(1)}, bf16[384,1536]{1,0:T(8,128)(2,1)S(1)}, u32[]{:S(2)}, u32[]{:S(2)}) collective-permute-start(bf16[384,1536]{1,0:T(8,128)(2,1)S(1)} %slice_bitcast_fusion.refs_4_), channel_id=1, source_target_pairs={{0,192},{64,0},{128,64},{192,128},{1,193},{65,1},{129,65},{193,129... | collective-permute-start | bytes 3538952 | tf_op jit(solution)/shard_map/ppermute | solution.py:430
  31.6 29.2 %collective-permute-start.2 = (bf16[384,1536]{1,0:T(8,128)(2,1)S(1)}, bf16[384,1536]{1,0:T(8,128)(2,1)S(1)}, u32[]{:S(2)}, u32[]{:S(2)}) collective-permute-start(bf16[384,1536]{1,0:T(8,128)(2,1)S(1)} %slice_bitcast_fusion.refs_4_), channel_id=1, source_target_pairs={{0,64},{64,128},{128,192},{192,0},{1,65},{65,129},{129,193},{193,1... | collective-permute-start | bytes 3538952 | tf_op jit(solution)/shard_map/ppermute | solution.py:430
  31.6 1.0 copy-start.4
  56.4 4.4 %copy-start.6 = (bf16[384,1536]{1,0:T(8,128)(2,1)}, bf16[384,1536]{1,0:T(8,128)(2,1)S(1)}, u32[]{:S(2)}) copy-start(bf16[384,1536]{1,0:T(8,128)(2,1)S(1)} %collective-permute-done.3.refs_6_) | copy-start | bytes 3538948
  57.3 15.2 %collective-permute-start.5 = (bf16[192,1536]{1,0:T(8,128)(2,1)}, bf16[192,1536]{1,0:T(8,128)(2,1)}, u32[]{:S(2)}, u32[]{:S(2)}) collective-permute-start(bf16[192,1536]{1,0:T(8,128)(2,1)} %slice.21), channel_id=1, source_target_pairs={{0,192},{64,0},{128,64},{192,128},{1,193},{65,1},{129,65},{193,129... | collective-permute-start | bytes 1769480 | tf_op jit(solution)/shard_map/ppermute | solution.py:430
  60.8 1.2 copy-start.8
  62.1 14.8 %collective-permute-start.4 = (bf16[192,1536]{1,0:T(8,128)(2,1)}, bf16[192,1536]{1,0:T(8,128)(2,1)}, u32[]{:S(2)}, u32[]{:S(2)}) collective-permute-start(bf16[192,1536]{1,0:T(8,128)(2,1)} %slice.20), channel_id=1, source_target_pairs={{0,64},{64,128},{128,192},{192,0},{1,65},{65,129},{129,193},{193,1... | collective-permute-start | bytes 1769480 | tf_op jit(solution)/shard_map/ppermute | solution.py:430
  76.8 22.4 %collective-permute-start.7 = (bf16[1024,512]{1,0:T(8,128)(2,1)}, bf16[1024,512]{1,0:T(8,128)(2,1)S(1)}, u32[]{:S(2)}, u32[]{:S(2)}) collective-permute-start(bf16[1024,512]{1,0:T(8,128)(2,1)} %bitcast.3.refs_0_), channel_id=1, source_target_pairs={{0,192},{64,0},{128,64},{192,128},{1,193},{65,1},{129,65},{193,129... | collective-permute-start | bytes 3145736 | tf_op jit(solution)/shard_map/ppermute | solution.py:430
  76.8 23.6 %collective-permute-start.6 = (bf16[1024,512]{1,0:T(8,128)(2,1)}, bf16[1024,512]{1,0:T(8,128)(2,1)S(1)}, u32[]{:S(2)}, u32[]{:S(2)}) collective-permute-start(bf16[1024,512]{1,0:T(8,128)(2,1)} %bitcast.3.refs_0_), channel_id=1, source_target_pairs={{0,64},{64,128},{128,192},{192,0},{1,65},{65,129},{129,193},{193,1... | collective-permute-start | bytes 3145736 | tf_op jit(solution)/shard_map/ppermute | solution.py:430
  78.3 17.0 %collective-permute-start.8 = (bf16[128,256]{1,0:T(8,128)(2,1)S(1)}, bf16[128,256]{1,0:T(8,128)(2,1)S(1)}, u32[]{:S(2)}, u32[]{:S(2)}) collective-permute-start(bf16[128,256]{1,0:T(8,128)(2,1)S(1)} %copy-done.16), channel_id=1, source_target_pairs={{0,1},{1,2},{2,3},{3,4},{4,5},{5,6},{6,7},{7,8},{8,9},{9,10},{10,1... | collective-permute-start | bytes 196616 | tf_op jit(solution)/shard_map/ppermute | solution.py:430
  82.8 12.6 %collective-permute-start.9 = (bf16[128,256]{1,0:T(8,128)(2,1)S(1)}, bf16[128,256]{1,0:T(8,128)(2,1)S(1)}, u32[]{:S(2)}, u32[]{:S(2)}) collective-permute-start(bf16[128,256]{1,0:T(8,128)(2,1)S(1)} %copy-done.15), channel_id=1, source_target_pairs={{0,32},{1,33},{2,34},{3,35},{4,36},{5,37},{6,38},{7,39},{8,40},{9,... | collective-permute-start | bytes 196616 | tf_op jit(solution)/shard_map/ppermute | solution.py:430
  87.9 1.9 copy-start.1
  89.8 1.9 copy-start.3
  91.7 10.6 %copy-start.2 = (bf16[1,4096,384]{2,1,0:T(8,128)(2,1)S(1)}, bf16[1,4096,384]{2,1,0:T(8,128)(2,1)}, u32[]{:S(2)}) copy-start(bf16[1,4096,384]{2,1,0:T(8,128)(2,1)} %refs_2_.7) | copy-start | bytes 9437188
  100.5 10.3 %collective-permute-start.11 = (bf16[512,512]{1,0:T(8,128)(2,1)S(1)}, bf16[512,512]{1,0:T(8,128)(2,1)S(1)}, u32[]{:S(2)}, u32[]{:S(2)}) collective-permute-start(bf16[512,512]{1,0:T(8,128)(2,1)S(1)} %slice.19), channel_id=1, source_target_pairs={{0,192},{64,0},{128,64},{192,128},{1,193},{65,1},{129,65},{193,129... | collective-permute-start | bytes 1572872 | tf_op jit(solution)/shard_map/ppermute | solution.py:430
  101.1 11.2 %collective-permute-start.10 = (bf16[512,512]{1,0:T(8,128)(2,1)S(1)}, bf16[512,512]{1,0:T(8,128)(2,1)S(1)}, u32[]{:S(2)}, u32[]{:S(2)}) collective-permute-start(bf16[512,512]{1,0:T(8,128)(2,1)S(1)} %slice.18), channel_id=1, source_target_pairs={{0,64},{64,128},{128,192},{192,0},{1,65},{65,129},{129,193},{193,1... | collective-permute-start | bytes 1572872 | tf_op jit(solution)/shard_map/ppermute | solution.py:430
  112.3 27.0 %copy-start.14 = (s32[8,2]{0,1:T(2,128)S(1)}, s32[8,2]{0,1:T(2,128)}, u32[]{:S(2)}) copy-start(s32[8,2]{0,1:T(2,128)} %param.21) | copy-start | bytes 196
  112.3 29.1 %copy-start.5 = (bf16[384,1536]{1,0:T(8,128)(2,1)S(1)}, bf16[384,1536]{1,0:T(8,128)(2,1)}, u32[]{:S(2)}) copy-start(bf16[384,1536]{1,0:T(8,128)(2,1)} %copy-done.4) | copy-start | bytes 3538948
  112.3 29.1 %copy-start.7 = (bf16[384,1536]{1,0:T(8,128)(2,1)S(1)}, bf16[384,1536]{1,0:T(8,128)(2,1)}, u32[]{:S(2)}) copy-start(bf16[384,1536]{1,0:T(8,128)(2,1)} %copy-done.6) | copy-start | bytes 3538948
  112.3 29.1 %copy-start.9 = (bf16[384,1536]{1,0:T(8,128)(2,1)S(1)}, bf16[384,1536]{1,0:T(8,128)(2,1)}, u32[]{:S(2)}) copy-start(bf16[384,1536]{1,0:T(8,128)(2,1)} %copy-done.8) | copy-start | bytes 3538948
  114.6 7.2 %collective-permute-start.12 = (bf16[320,512]{1,0:T(8,128)(2,1)S(1)}, bf16[320,512]{1,0:T(8,128)(2,1)S(1)}, u32[]{:S(2)}, u32[]{:S(2)}) collective-permute-start(bf16[320,512]{1,0:T(8,128)(2,1)S(1)} %get-tuple-element.77), channel_id=1, source_target_pairs={{0,64},{64,128},{128,192},{192,0},{1,65},{65,129},{129,193},{193,1... | collective-permute-start | bytes 983048 | tf_op jit(solution)/shard_map/ppermute | solution.py:430
  114.7 7.1 %collective-permute-start.13 = (bf16[320,512]{1,0:T(8,128)(2,1)S(1)}, bf16[320,512]{1,0:T(8,128)(2,1)S(1)}, u32[]{:S(2)}, u32[]{:S(2)}) collective-permute-start(bf16[320,512]{1,0:T(8,128)(2,1)S(1)} %get-tuple-element.78), channel_id=1, source_target_pairs={{0,192},{64,0},{128,64},{192,128},{1,193},{65,1},{129,65},{193,129... | collective-permute-start | bytes 983048 | tf_op jit(solution)/shard_map/ppermute | solution.py:430
  117.3 7.7 %collective-permute-start.18 = (bf16[128,384]{1,0:T(8,128)(2,1)S(1)}, bf16[128,384]{1,0:T(8,128)(2,1)S(1)}, u32[]{:S(2)}, u32[]{:S(2)}) collective-permute-start(bf16[128,384]{1,0:T(8,128)(2,1)S(1)} %get-tuple-element.87), channel_id=1, source_target_pairs={{0,64},{64,128},{128,192},{192,0},{1,65},{65,129},{129,193},{193,1... | collective-permute-start | bytes 294920 | tf_op jit(solution)/shard_map/ppermute | solution.py:430
  117.3 26.3 %collective-permute-start.15 = (bf16[320,512]{1,0:T(8,128)(2,1)S(1)}, bf16[320,512]{1,0:T(8,128)(2,1)S(1)}, u32[]{:S(2)}, u32[]{:S(2)}) collective-permute-start(bf16[320,512]{1,0:T(8,128)(2,1)S(1)} %get-tuple-element.81), channel_id=1, source_target_pairs={{0,64},{64,128},{128,192},{192,0},{1,65},{65,129},{129,193},{193,1... | collective-permute-start | bytes 983048 | tf_op jit(solution)/shard_map/ppermute | solution.py:430
  117.3 26.3 %collective-permute-start.16 = (bf16[320,512]{1,0:T(8,128)(2,1)S(1)}, bf16[320,512]{1,0:T(8,128)(2,1)S(1)}, u32[]{:S(2)}, u32[]{:S(2)}) collective-permute-start(bf16[320,512]{1,0:T(8,128)(2,1)S(1)} %get-tuple-element.83), channel_id=1, source_target_pairs={{0,192},{64,0},{128,64},{192,128},{1,193},{65,1},{129,65},{193,129... | collective-permute-start | bytes 983048 | tf_op jit(solution)/shard_map/ppermute | solution.py:430
  121.9 21.7 %collective-permute-start.14 = (bf16[320,512]{1,0:T(8,128)(2,1)S(1)}, bf16[320,512]{1,0:T(8,128)(2,1)S(1)}, u32[]{:S(2)}, u32[]{:S(2)}) collective-permute-start(bf16[320,512]{1,0:T(8,128)(2,1)S(1)} %get-tuple-element.79), channel_id=1, source_target_pairs={{0,64},{64,128},{128,192},{192,0},{1,65},{65,129},{129,193},{193,1... | collective-permute-start | bytes 983048 | tf_op jit(solution)/shard_map/ppermute | solution.py:430
  122.0 21.7 %collective-permute-start.17 = (bf16[320,512]{1,0:T(8,128)(2,1)S(1)}, bf16[320,512]{1,0:T(8,128)(2,1)S(1)}, u32[]{:S(2)}, u32[]{:S(2)}) collective-permute-start(bf16[320,512]{1,0:T(8,128)(2,1)S(1)} %get-tuple-element.84), channel_id=1, source_target_pairs={{0,192},{64,0},{128,64},{192,128},{1,193},{65,1},{129,65},{193,129... | collective-permute-start | bytes 983048 | tf_op jit(solution)/shard_map/ppermute | solution.py:430
  125.0 10.9 %collective-permute-start.19 = (bf16[128,384]{1,0:T(8,128)(2,1)S(1)}, bf16[128,384]{1,0:T(8,128)(2,1)S(1)}, u32[]{:S(2)}, u32[]{:S(2)}) collective-permute-start(bf16[128,384]{1,0:T(8,128)(2,1)S(1)} %get-tuple-element.89), channel_id=1, source_target_pairs={{0,192},{64,0},{128,64},{192,128},{1,193},{65,1},{129,65},{193,129... | collective-permute-start | bytes 294920 | tf_op jit(solution)/shard_map/ppermute | solution.py:430
  135.9 5.5 %collective-permute-start.20 = (bf16[128,384]{1,0:T(8,128)(2,1)S(1)}, bf16[128,384]{1,0:T(8,128)(2,1)S(1)}, u32[]{:S(2)}, u32[]{:S(2)}) collective-permute-start(bf16[128,384]{1,0:T(8,128)(2,1)S(1)} %get-tuple-element.90), channel_id=1, source_target_pairs={{0,128},{64,192},{128,0},{192,64},{1,129},{65,193},{129,1},{193,65... | collective-permute-start | bytes 294920 | tf_op jit(solution)/shard_map/ppermute | solution.py:430
  143.6 46.2 %copy-start.12 = (s32[8,8]{1,0:T(8,128)S(1)}, s32[8,8]{1,0:T(8,128)}, u32[]{:S(2)}) copy-start(s32[8,8]{1,0:T(8,128)} %refs_0_.3) | copy-start | bytes 772
  143.6 46.2 %copy-start.13 = (f32[8,8]{1,0:T(8,128)S(1)}, f32[8,8]{1,0:T(8,128)}, u32[]{:S(2)}) copy-start(f32[8,8]{1,0:T(8,128)} %refs_1_.3) | copy-start | bytes 772

commit v3 on v1

--- a/solution.py
+++ b/solution.py
@@ -39,41 +39,62 @@
     return found
 
 
+def insert_new(lengths_ref, cached_ref, fresh_ref, out_ref):
+    requests, slots, width = cached_ref.shape
+    fresh = fresh_ref[...].astype(F32)
+    position = iota((slots, width), 0)
+    for r in range(requests):
+        out_ref[r] = jnp.where(
+            position == lengths_ref[r], fresh[r : r + 1], cached_ref[r].astype(F32)
+        ).astype(BF16)
+
+
+def store_kernel(
+    ep_count,
+    lengths_ref,
+    plan_ref,
+    keys_ref,
+    values_ref,
+    new_keys_ref,
+    new_values_ref,
+    keys_out_ref,
+    values_out_ref,
+    cache0_ref,
+    cache1_ref,
+):
+    requests, slots, _ = keys_ref.shape
+    insert_new(lengths_ref, keys_ref, new_keys_ref, keys_out_ref)
+    insert_new(lengths_ref, values_ref, new_values_ref, values_out_ref)
+    rank = lax.axis_index("ep")
+    for distance, cache_ref in zip(distances(ep_count), (cache0_ref, cache1_ref)):
+        slot = find_slot(plan_ref, 1, lax.rem(rank + distance, ep_count), requests, ep_count)
+        cache_ref[0:slots] = keys_out_ref[slot]
+        cache_ref[slots : 2 * slots] = values_out_ref[slot]
+
+
 def attend_kernel(
     ep_count,
+    copies,
     lengths_ref,
     plan_ref,
     queries_ref,
     keys_ref,
+    new_keys_ref,
     values_ref,
-    new_keys_ref,
     new_values_ref,
     residual_ref,
     ids_ref,
     gain_ref,
-    keys_out_ref,
-    values_out_ref,
     carry_ref,
     row0_ref,
     row1_ref,
-    cache0_ref,
-    cache1_ref,
+    keys_out_ref,
+    values_out_ref,
 ):
     requests, slots, width = keys_ref.shape
     heads = queries_ref.shape[1] // HD
     kv_heads = width // HD
     groups = heads // kv_heads
-    fresh_keys = new_keys_ref[...].astype(F32)
-    fresh_values = new_values_ref[...].astype(F32)
-    position = iota((slots, width), 0)
-    for r in range(requests):
-        newest = position == lengths_ref[r]
-        keys_out_ref[r] = jnp.where(
-            newest, fresh_keys[r : r + 1], keys_ref[r].astype(F32)
-        ).astype(BF16)
-        values_out_ref[r] = jnp.where(
-            newest, fresh_values[r : r + 1], values_ref[r].astype(F32)
-        ).astype(BF16)
     total = requests * slots
     column = iota((groups * requests, total), 1)
     holder = lax.div(column, slots)
@@ -82,10 +103,12 @@
         limit = jnp.where(holder == r, lengths_ref[r], limit)
     own_row = lax.rem(iota((groups * requests, total), 0), requests)
     visible = (holder == own_row) & (lax.rem(column, slots) <= limit)
+    for copy in copies[:3]:
+        copy.wait()
+    insert_new(lengths_ref, keys_ref, new_keys_ref, keys_out_ref)
     queries = queries_ref[...].astype(F32)
-    residual = residual_ref[...].astype(F32)
     all_keys = keys_out_ref[...].reshape(total, width)
-    all_values = values_out_ref[...].reshape(total, width)
+    spread = []
     for k in range(kv_heads):
         stacked = jnp.concatenate(
             [
@@ -102,7 +125,13 @@
         ) * (1.0 / math.sqrt(HD))
         scores = jnp.where(visible, scores, -jnp.inf)
         weights = jnp.exp(scores - jnp.max(scores, axis=1, keepdims=True))
-        probabilities = (weights / jnp.sum(weights, axis=1, keepdims=True)).astype(BF16)
+        spread.append((weights / jnp.sum(weights, axis=1, keepdims=True)).astype(BF16))
+    for copy in copies[3:]:
+        copy.wait()
+    insert_new(lengths_ref, values_ref, new_values_ref, values_out_ref)
+    all_values = values_out_ref[...].reshape(total, width)
+    residual = residual_ref[...].astype(F32)
+    for k, probabilities in enumerate(spread):
         attended = jnp.dot(
             probabilities, all_values[:, k * HD : (k + 1) * HD], preferred_element_type=F32
         )
@@ -114,13 +143,9 @@
     rank = lax.axis_index("ep")
     summed = carry_ref[0:requests]
     row_number = iota(summed.shape, 0)
-    for d, (distance, row_ref, cache_ref) in enumerate(
-        zip(distances(ep_count), (row0_ref, row1_ref), (cache0_ref, cache1_ref))
-    ):
+    for d, (distance, row_ref) in enumerate(zip(distances(ep_count), (row0_ref, row1_ref))):
         slot = find_slot(plan_ref, 1, lax.rem(rank + distance, ep_count), requests, ep_count)
         row_ref[...] = jnp.sum(jnp.where(row_number == slot, summed, 0.0), axis=0, keepdims=True)
-        cache_ref[0:slots] = keys_out_ref[slot]
-        cache_ref[slots : 2 * slots] = values_out_ref[slot]
         origin = lax.rem(rank + ep_count - distance, ep_count)
         arrival = find_slot(plan_ref, 0, origin, requests, ep_count)
         carry_ref[2 * requests : 3 * requests, (2 + d) * HD : (3 + d) * HD] = jnp.where(
@@ -254,11 +279,9 @@
         ).astype(BF16)
 
 
-def mix_kernel(ids_ref, gates_ref, summed_ref, returned_ref, out_ref):
-    rows, model_width = summed_ref.shape
-    deep = MOST * COLS
-    experts = returned_ref.shape[0] // deep
-    part = model_width // COLS
+def weigh_kernel(ids_ref, gates_ref, coarse_ref, fine_ref):
+    rows, deep = ids_ref.shape[0], MOST * COLS
+    experts = coarse_ref.shape[1] // deep
     chosen, weight, earlier = routes(ids_ref[...], gates_ref[...], experts)
     repeat_shape = (COLS * rows, rows)
     repeat = one_hot(lax.rem(iota(repeat_shape, 0), rows) == iota(repeat_shape, 1))
@@ -268,28 +291,28 @@
     column = iota(pick_shape, 1)
     same_part = lax.div(iota(pick_shape, 0), rows) == lax.rem(column, COLS)
     slot_here = lax.rem(lax.div(column, COLS), MOST)
-    returned = returned_ref[...]
-    coarse_pick = jnp.zeros(pick_shape, F32)
-    fine_pick = jnp.zeros(pick_shape, F32)
+    picks = [jnp.zeros(pick_shape, F32), jnp.zeros(pick_shape, F32)]
     for s in range(MOST):
         placed = jnp.where((earlier == float(s)) & (chosen > 0.5), weight, 0.0)
         coarse = placed.astype(BF16)
         fine = (placed - coarse.astype(F32)).astype(BF16)
-        here = same_part & (slot_here == s)
-        by_row = jnp.dot(
-            jnp.dot(repeat, coarse, preferred_element_type=F32).astype(BF16),
-            spread,
-            preferred_element_type=F32,
-        )
-        coarse_pick = jnp.where(here, by_row, coarse_pick)
-        by_row = jnp.dot(
-            jnp.dot(repeat, fine, preferred_element_type=F32).astype(BF16),
-            spread,
-            preferred_element_type=F32,
-        )
-        fine_pick = jnp.where(here, by_row, fine_pick)
-    mixture = jnp.dot(coarse_pick.astype(BF16), returned, preferred_element_type=F32)
-    mixture += jnp.dot(fine_pick.astype(BF16), returned, preferred_element_type=F32)
+        for i, member in enumerate((coarse, fine)):
+            by_row = jnp.dot(
+                jnp.dot(repeat, member, preferred_element_type=F32).astype(BF16),
+                spread,
+                preferred_element_type=F32,
+            )
+            picks[i] = jnp.where(same_part & (slot_here == s), by_row, picks[i])
+    coarse_ref[...] = picks[0].astype(BF16)
+    fine_ref[...] = picks[1].astype(BF16)
+
+
+def mix_kernel(coarse_ref, fine_ref, summed_ref, returned_ref, out_ref):
+    rows, model_width = summed_ref.shape
+    part = model_width // COLS
+    returned = returned_ref[...]
+    mixture = jnp.dot(coarse_ref[...], returned, preferred_element_type=F32)
+    mixture += jnp.dot(fine_ref[...], returned, preferred_element_type=F32)
     for c in range(COLS):
         here = slice(c * part, (c + 1) * part)
         out_ref[:, here] = (
@@ -330,7 +353,7 @@
     return jax.ShapeDtypeStruct(shape, dtype)
 
 
-def call(kernel, outs, scalars, staged, resident, flops, moved, limit=16, scratch=()):
+def call(kernel, outs, scalars, staged, resident, flops, moved, limit=16, scratch=(), lazy=False):
     n_scalars, n_staged, n_resident = map(len, (scalars, staged, resident))
     n_outs = len(outs) if isinstance(outs, tuple) else 1
 
@@ -353,9 +376,11 @@
         ]
         for copy in copies:
             copy.start()
-        for copy in copies:
-            copy.wait()
-        kernel(*scalar_refs, *staged_refs, *resident_refs, *out_refs, *own_refs)
+        if not lazy:
+            for copy in copies:
+                copy.wait()
+        first = (copies,) if lazy else ()
+        kernel(*first, *scalar_refs, *staged_refs, *resident_refs, *out_refs, *own_refs)
 
     stages = [pltpu.VMEM(arg.shape, arg.dtype) for arg in staged]
     if staged:
@@ -415,20 +440,25 @@
 
 
 def through_experts(own, weights, beside):
-    from_left = rotate(own, "dp", 1)
-    from_right = rotate(own, "dp", -1)
+    top, bottom = own[:STEP], own[STEP:]
+    left_rows_top = rotate(top, "dp", 1)
+    right_rows_bottom = rotate(bottom, "dp", -1)
+    left_rows_bottom = rotate(bottom, "dp", 1)
+    right_rows_top = rotate(top, "dp", -1)
     own_top, own_bottom = experts_of([own], weights)
-    from_left, from_right, own_top, own_bottom, *beside = lax.optimization_barrier(
-        (from_left, from_right, own_top, own_bottom, *beside)
-    )
-    far_top = rotate(from_left[:STEP], "dp", 1)
-    far_bottom = rotate(from_right[STEP:], "dp", -1)
-    left_top, left_bottom, right_top, right_bottom = experts_of([from_left, from_right], weights)
+    left_rows_top, right_rows_bottom, own_top, own_bottom, beside = lax.optimization_barrier(
+        (left_rows_top, right_rows_bottom, own_top, own_bottom, beside)
+    )
+    far_top = rotate(left_rows_top, "dp", 1)
+    far_bottom = rotate(right_rows_bottom, "dp", -1)
+    left_top, left_bottom, right_top, right_bottom = experts_of(
+        [left_rows_top, left_rows_bottom, right_rows_top, right_rows_bottom], weights
+    )
+    direct_left = rotate(right_bottom, "dp", 1)
+    direct_right = rotate(left_top, "dp", -1)
     far_top, far_bottom, right_top, left_bottom = lax.optimization_barrier(
         (far_top, far_bottom, right_top, left_bottom)
     )
-    direct_left = rotate(after(right_bottom, far_top, far_bottom), "dp", 1)
-    direct_right = rotate(after(left_top, far_top, far_bottom), "dp", -1)
     far_terms = experts_of([far_top, far_bottom], weights)
     relayed_left = rotate(far_terms[0], "dp", 1)
     relayed_right = rotate(far_terms[1], "dp", -1)
@@ -486,15 +516,15 @@
     def attend(*refs):
         attend_kernel(ep_count, *refs)
 
-    keys, values, carry, row0, row1, cache0, cache1 = call(
+    carry, row0, row1 = call(
         attend,
-        (cache, cache, shape_of((3 * requests, model_width), F32), row, row, moving, moving),
+        (shape_of((3 * requests, model_width), F32), row, row),
         (cache_lengths, plan),
         (
             queries,
             key_cache,
+            new_keys,
             value_cache,
-            new_keys,
             new_values,
             residual,
             expert_ids,
@@ -504,6 +534,8 @@
         10**8,
         3 * 10**6,
         limit=58,
+        lazy=True,
+        scratch=[pltpu.VMEM(cache.shape, BF16), pltpu.VMEM(cache.shape, BF16)],
     )
     got_row0 = rotate(row0, "ep", steps[0])
     got_row1 = rotate(row1, "ep", steps[1])
@@ -522,16 +554,26 @@
         2 * 10**6,
     )
     rows = exchange(outgoing)
-    cache0, cache1, rows = lax.optimization_barrier((cache0, cache1, rows))
+
+    def store(*refs):
+        store_kernel(ep_count, *refs)
+
+    keys, values, cache0, cache1 = call(
+        store,
+        (cache, cache, moving, moving),
+        (cache_lengths, plan),
+        (after(key_cache, rows), value_cache, new_keys, new_values),
+        (),
+        0,
+        3 * 10**6,
+    )
     got_cache0 = rotate(cache0, "ep", steps[0])
     got_cache1 = rotate(cache1, "ep", steps[1])
 
     def settle(*refs):
         settle_kernel(ep_count, *refs)
 
-    sums, (got_cache0, got_cache1) = through_experts(
-        rows, (w_gate, w_up, w_down), (got_cache0, got_cache1)
-    )
+    sums, got_cache0 = through_experts(rows, (w_gate, w_up, w_down), got_cache0)
     keys_out, values_out = pl.pallas_call(
         settle,
         out_shape=(cache, cache),
@@ -546,13 +588,23 @@
         compiler_params=pltpu.CompilerParams(vmem_limit_bytes=4 * 2**20),
         cost_estimate=pl.CostEstimate(flops=0, bytes_accessed=10**6, transcendentals=0),
     )(plan, got_cache0, got_cache1, keys, values)
-    returned = exchange(after(sums, keys_out, values_out))
+    picks = shape_of((COLS * requests, ep_count * MOST * COLS), BF16)
+    coarse, fine = call(
+        weigh_kernel,
+        (picks, picks),
+        (),
+        (),
+        (after(expert_ids, rows), gate_weights),
+        10**7,
+        10**6,
+    )
+    returned = exchange(after(sums, keys_out, values_out, coarse, fine))
     layer_out = call(
         mix_kernel,
         shape_of((requests, model_width), BF16),
         (),
-        (expert_ids, gate_weights),
-        (summed, returned),
+        (),
+        (coarse, fine, summed, returned),
         10**8,
         2 * 10**6,
     )

time: 172 us -> 171 us (level)
  waiting for transfers between devices: 43.4 us -> 37.2 us
  starting transfers between devices: 26.2 us -> 31.8 us
  blocking collectives: 78.2 us -> 76.1 us
    ppermute x14 -> x16, waiting for transfers between devices: 43.4 us -> 37.2 us  [rotate(): lax.ppermute(member, axis, [(s, (s + distance) % count) for s in range(co...]
    ppermute x14 -> x16, starting transfers between devices: 26.2 us -> 31.8 us  [rotate(): lax.ppermute(member, axis, [(s, (s + distance) % count) for s in range(co...]
    all_to_all x2, blocking collectives: 78.2 us -> 76.1 us  [exchange(): cut = lax.all_to_all(cut, 'ep', split_axis=0, concat_axis=0, tiled=True)]
    pallas_call x8 -> x10, Pallas kernels: 17.2 us -> 18.5 us  [call(): pl.pallas_call(body, out_shape=outs, grid_spec=pltpu.PrefetchScalarGridSp...]
    unnamed x14 -> x24, local copies, waits for them, and re-layouts: 4.79 us -> 4.81 us
  transfers between devices with their start and end apart: 14 -> 16, of which waited for: 8 -> 7; matrix products, arithmetic and copies ran while one was open for 0% -> 0% of each run, Pallas kernels for 5% -> 6%
where the time goes in v3:
time: 171 us
  blocking collectives  76.1 us (45%)
  waiting for transfers between devices  37.2 us (22%)
  starting transfers between devices  31.8 us (19%)
  Pallas kernels  19.8 us (12%)
  local copies, waits for them, and re-layouts  4.88 us (3%)
    all_to_all x2, blocking collectives, exchange(): cut = lax.all_to_all(cut, 'ep', split_axis=0, concat_axis=0, tiled=True)  76.1 us
    ppermute x16, waiting for transfers between devices, rotate(): lax.ppermute(member, axis, [(s, (s + distance) % count) for s in range(co...  37.2 us
    ppermute x16, starting transfers between devices, rotate(): lax.ppermute(member, axis, [(s, (s + distance) % count) for s in range(co...  31.8 us
    pallas_call x10, Pallas kernels, call(): pl.pallas_call(body, out_shape=outs, grid_spec=pltpu.PrefetchScalarGridSp...  18.5 us
    unnamed x24, local copies, waits for them, and re-layouts  4.81 us
  transfers between devices with their start and end apart: 16, of which 7 were waited for; matrix products, arithmetic and copies ran while one was open for 0% of the time, Pallas kernels for 6%

profile of v3, /device:TPU:1, one launch (start us, length us, event | category | flops | bytes accessed | tf_op | source)
XLA Modules:
  0.0 170.6 jit_solution(15722555486236903557)
XLA Ops:
  0.6 0.0 copy-start.3
  0.6 0.0 copy-start.4
  0.7 0.0 copy-start
  0.7 3.6 %shard_map.157 = (f32[24,4096]{1,0:T(8,128)}, f32[1,4096]{1,0:T(1,128)}, f32[1,4096]{1,0:T(1,128)}) custom-call(s32[8]{0:T(128)} %refs_0_.4, s32[2,8]{1,0:T(2,128)} %bitcast.12, bf16[8,4096]{1,0:T(8,128)(2,1)} %refs_2_.3, bf16[8,64,256]{2,1,0:T(8,128)(2,1)} %refs_2_.5, bf16[8,256]{1,0:T(8,128)(2,1)} %refs_4_.5, bf16[8,64,256]{2,1,0:T(8,128)(2,1)} %refs_3_.6, ...), custom_call_target="tpu_custom_call" | custom-call | flops 100000000 | bytes 3000000 | tf_op jit(solution)/shard_map/pallas_call | solution.py:388
  4.3 2.7 %collective-permute-start = (f32[1,4096]{1,0:T(1,128)}, f32[1,4096]{1,0:T(1,128)S(1)}, u32[]{:S(2)}, u32[]{:S(2)}) collective-permute-start(f32[1,4096]{1,0:T(1,128)} %get-tuple-element.39), channel_id=1, source_target_pairs={{0,1},{1,2},{2,3},{3,4},{4,5},{5,6},{6,7},{7,8},{8,9},{9,10},{10,1... | collective-permute-start | bytes 49160 | tf_op jit(solution)/shard_map/ppermute | solution.py:428
  6.9 6.9 %collective-permute-start.1 = (f32[1,4096]{1,0:T(1,128)}, f32[1,4096]{1,0:T(1,128)S(1)}, u32[]{:S(2)}, u32[]{:S(2)}) collective-permute-start(f32[1,4096]{1,0:T(1,128)} %get-tuple-element.40), channel_id=1, source_target_pairs={{0,32},{1,33},{2,34},{3,35},{4,36},{5,37},{6,38},{7,39},{8,40},{9,... | collective-permute-start | bytes 49160 | tf_op jit(solution)/shard_map/ppermute | solution.py:428
  13.9 0.0 collective-permute-done.refs_1_
  13.9 1.3 collective-permute-done.1.refs_2_
  15.2 0.0 copy-start.5
  15.2 1.0 copy-done.5
  16.2 0.0 copy-start.6
  16.2 0.0 copy-start.8
  16.2 0.7 shard_map.158
  16.9 37.9 %all_to_all.10 = bf16[64,16,512]{2,1,0:T(8,128)(2,1)S(1)} all-to-all(bf16[64,16,512]{2,1,0:T(8,128)(2,1)S(1)} %bitcast.11), channel_id=1, replica_groups=mesh['dp'=4,'ep'=64] {'ep'}, dimensions={0} | all-to-all | bytes 2097152 | tf_op jit(solution)/shard_map/all_to_all | solution.py:434
  54.9 0.1 fusion
  55.0 1.4 collective-permute-start.2
  56.3 1.5 collective-permute-start.3
  57.9 0.0 collective-permute-start.7
  57.9 2.7 %collective-permute-start.8 = (bf16[512,512]{1,0:T(8,128)(2,1)S(1)}, bf16[512,512]{1,0:T(8,128)(2,1)S(1)}, u32[]{:S(2)}, u32[]{:S(2)}) collective-permute-start(bf16[512,512]{1,0:T(8,128)(2,1)S(1)} %bitcast.16), channel_id=1, source_target_pairs={{0,192},{64,0},{128,64},{192,128},{1,193},{65,1},{129,65},{193,129... | collective-permute-start | bytes 1572872 | tf_op jit(solution)/shard_map/ppermute | solution.py:428
  60.5 0.0 copy-done.3
  60.5 0.0 copy-done.4
  60.5 0.0 copy-done.6
  60.5 0.0 copy-done.7
  60.5 0.0 copy-done.8
  60.6 0.0 copy-done.10
  60.6 1.5 shard_map.161
  62.1 3.5 %collective-permute-start.4 = (bf16[128,256]{1,0:T(8,128)(2,1)S(1)}, bf16[128,256]{1,0:T(8,128)(2,1)S(1)}, u32[]{:S(2)}, u32[]{:S(2)}) collective-permute-start(bf16[128,256]{1,0:T(8,128)(2,1)S(1)} %get-tuple-element.49), channel_id=1, source_target_pairs={{0,1},{1,2},{2,3},{3,4},{4,5},{5,6},{6,7},{7,8},{8,9},{9,10},{10,1... | collective-permute-start | bytes 196616 | tf_op jit(solution)/shard_map/ppermute | solution.py:428
  65.6 0.0 copy-done
  65.6 1.9 %copy-done.1 = bf16[1,4096,384]{2,1,0:T(8,128)(2,1)S(1)} copy-done((bf16[1,4096,384]{2,1,0:T(8,128)(2,1)S(1)}, bf16[1,4096,384]{2,1,0:T(8,128)(2,1)}, u32[]{:S(2)}) %copy-start.1) | copy-done | bytes 3145752
  67.5 1.9 %copy-done.2 = bf16[1,384,4096]{2,1,0:T(8,128)(2,1)S(1)} copy-done((bf16[1,384,4096]{2,1,0:T(8,128)(2,1)S(1)}, bf16[1,384,4096]{2,1,0:T(8,128)(2,1)}, u32[]{:S(2)}) %copy-start.2) | copy-done | bytes 3145752
  69.3 2.5 %shard_map.160 = (bf16[512,512]{1,0:T(8,128)(2,1)S(1)}, bf16[512,512]{1,0:T(8,128)(2,1)S(1)}) custom-call(bf16[1024,512]{1,0:T(8,128)(2,1)S(1)} %bitcast.8, bf16[1,4096,384]{2,1,0:T(8,128)(2,1)S(1)} %copy-done, bf16[1,4096,384]{2,1,0:T(8,128)(2,1)S(1)} %copy-done.1, bf16[1,384,4096]{2,1,0:T(8,128)(2,1)S(1)} %copy-done.2), custom_call_target="tpu_custom_call" | custom-call | flops 1207959552 | bytes 11534336 | tf_op jit(solution)/shard_map/pallas_call | solution.py:388
  71.8 0.0 collective-permute-done.4.refs_1_
  71.8 0.0 collective-permute-done.2.refs_0_
  71.8 0.0 collective-permute-done.3.refs_3_
  71.9 0.1 collective-permute-start.5
  71.9 2.7 %collective-permute-start.6 = (bf16[512,512]{1,0:T(8,128)(2,1)S(1)}, bf16[512,512]{1,0:T(8,128)(2,1)S(1)}, u32[]{:S(2)}, u32[]{:S(2)}) collective-permute-start(bf16[512,512]{1,0:T(8,128)(2,1)S(1)} %collective-permute-done.3.refs_3_), channel_id=1, source_target_pairs={{0,192},{64,0},{128,64},{192,128},{1,193},{65,1},{129,65},{193,129... | collective-permute-start | bytes 1572872 | tf_op jit(solution)/shard_map/ppermute | solution.py:428
  74.6 5.1 %collective-permute-done.7.refs_1_ = bf16[512,512]{1,0:T(8,128)(2,1)S(1)} collective-permute-done((bf16[512,512]{1,0:T(8,128)(2,1)S(1)}, bf16[512,512]{1,0:T(8,128)(2,1)S(1)}, u32[]{:S(2)}, u32[]{:S(2)}) %collective-permute-start.7) | collective-permute-done | bytes 524320 | tf_op jit(solution)/shard_map/ppermute | solution.py:428
  79.7 0.0 collective-permute-done.8.refs_2_
  79.7 4.6 %shard_map.162 = (bf16[512,512]{1,0:T(8,128)(2,1)S(1)}, bf16[512,512]{1,0:T(8,128)(2,1)S(1)}, bf16[512,512]{1,0:T(8,128)(2,1)S(1)}, bf16[512,512]{1,0:T(8,128)(2,1)S(1)}) custom-call(bf16[512,512]{1,0:T(8,128)(2,1)S(1)} %collective-permute-done.2.refs_0_, bf16[512,512]{1,0:T(8,128)(2,1)S(1)} %collective-permute-done.7.refs_1_, ...), custom_call_target="tpu_custom_call" | custom-call | flops 2415919104 | bytes 13631488 | tf_op jit(solution)/shard_map/pallas_call | solution.py:388
  84.3 6.6 %collective-permute-done.5.refs_0_ = bf16[512,512]{1,0:T(8,128)(2,1)S(1)} collective-permute-done((bf16[512,512]{1,0:T(8,128)(2,1)S(1)}, bf16[512,512]{1,0:T(8,128)(2,1)S(1)}, u32[]{:S(2)}, u32[]{:S(2)}) %collective-permute-start.5) | collective-permute-done | bytes 524320 | tf_op jit(solution)/shard_map/ppermute | solution.py:428
  90.9 0.0 collective-permute-done.6.refs_1_
  90.9 2.5 %shard_map.163 = (bf16[512,512]{1,0:T(8,128)(2,1)S(1)}, bf16[512,512]{1,0:T(8,128)(2,1)S(1)}) custom-call(bf16[512,512]{1,0:T(8,128)(2,1)S(1)} %collective-permute-done.5.refs_0_, bf16[512,512]{1,0:T(8,128)(2,1)S(1)} %collective-permute-done.6.refs_1_, bf16[1,4096,384]{2,1,0:T(8,128)(2,1)S(1)} %copy-done, bf16[1,4096,384]{2,1,0:T(8,128)(2,1)S(1)} %copy-done.1, ...), custom_call_target="tpu_custom_call" | custom-call | flops 1207959552 | bytes 11534336 | tf_op jit(solution)/shard_map/pallas_call | solution.py:388
  93.4 2.6 %collective-permute-start.10 = (bf16[512,512]{1,0:T(8,128)(2,1)S(1)}, bf16[512,512]{1,0:T(8,128)(2,1)S(1)}, u32[]{:S(2)}, u32[]{:S(2)}) collective-permute-start(bf16[512,512]{1,0:T(8,128)(2,1)S(1)} %get-tuple-element.61), channel_id=1, source_target_pairs={{0,192},{64,0},{128,64},{192,128},{1,193},{65,1},{129,65},{193,129... | collective-permute-start | bytes 1572872 | tf_op jit(solution)/shard_map/ppermute | solution.py:428
  96.0 0.0 collective-permute-start.9
  96.0 0.0 collective-permute-start.12
  96.0 2.7 %collective-permute-start.13 = (bf16[512,512]{1,0:T(8,128)(2,1)S(1)}, bf16[512,512]{1,0:T(8,128)(2,1)S(1)}, u32[]{:S(2)}, u32[]{:S(2)}) collective-permute-start(bf16[512,512]{1,0:T(8,128)(2,1)S(1)} %get-tuple-element.64), channel_id=1, source_target_pairs={{0,192},{64,0},{128,64},{192,128},{1,193},{65,1},{129,65},{193,129... | collective-permute-start | bytes 1572872 | tf_op jit(solution)/shard_map/ppermute | solution.py:428
  98.7 6.1 %collective-permute-done.10.refs_3_ = bf16[512,512]{1,0:T(8,128)(2,1)S(1)} collective-permute-done((bf16[512,512]{1,0:T(8,128)(2,1)S(1)}, bf16[512,512]{1,0:T(8,128)(2,1)S(1)}, u32[]{:S(2)}, u32[]{:S(2)}) %collective-permute-start.10) | collective-permute-done | bytes 524320 | tf_op jit(solution)/shard_map/ppermute | solution.py:428
  104.8 3.1 %collective-permute-done.9.refs_2_ = bf16[512,512]{1,0:T(8,128)(2,1)S(1)} collective-permute-done((bf16[512,512]{1,0:T(8,128)(2,1)S(1)}, bf16[512,512]{1,0:T(8,128)(2,1)S(1)}, u32[]{:S(2)}, u32[]{:S(2)}) %collective-permute-start.9) | collective-permute-done | bytes 524320 | tf_op jit(solution)/shard_map/ppermute | solution.py:428
  108.0 0.2 shard_map.164
  108.2 0.1 collective-permute-start.11
  108.3 2.7 %collective-permute-start.14 = (bf16[512,512]{1,0:T(8,128)(2,1)S(1)}, bf16[512,512]{1,0:T(8,128)(2,1)S(1)}, u32[]{:S(2)}, u32[]{:S(2)}) collective-permute-start(bf16[512,512]{1,0:T(8,128)(2,1)S(1)} %get-tuple-element.65), channel_id=1, source_target_pairs={{0,192},{64,0},{128,64},{192,128},{1,193},{65,1},{129,65},{193,129... | collective-permute-start | bytes 1572872 | tf_op jit(solution)/shard_map/ppermute | solution.py:428
  111.0 2.3 %collective-permute-start.15 = (bf16[128,256]{1,0:T(8,128)(2,1)S(1)}, bf16[128,256]{1,0:T(8,128)(2,1)S(1)}, u32[]{:S(2)}, u32[]{:S(2)}) collective-permute-start(bf16[128,256]{1,0:T(8,128)(2,1)S(1)} %get-tuple-element.67), channel_id=1, source_target_pairs={{0,32},{1,33},{2,34},{3,35},{4,36},{5,37},{6,38},{7,39},{8,40},{9,... | collective-permute-start | bytes 196616 | tf_op jit(solution)/shard_map/ppermute | solution.py:428
  113.3 0.0 copy-done.9
  113.3 0.0 copy-done.11
  113.3 0.9 shard_map.159
  114.2 3.8 %collective-permute-done.15.refs_2_ = bf16[128,256]{1,0:T(8,128)(2,1)S(1)} collective-permute-done((bf16[128,256]{1,0:T(8,128)(2,1)S(1)}, bf16[128,256]{1,0:T(8,128)(2,1)S(1)}, u32[]{:S(2)}, u32[]{:S(2)}) %collective-permute-start.15) | collective-permute-done | bytes 65568 | tf_op jit(solution)/shard_map/ppermute | solution.py:428
  118.0 1.3 shard_map.166
  119.3 0.0 collective-permute-done.12.refs_3_
  119.3 0.0 collective-permute-done.13.refs_4_
  119.3 11.2 %collective-permute-done.11.refs_2_ = bf16[512,512]{1,0:T(8,128)(2,1)S(1)} collective-permute-done((bf16[512,512]{1,0:T(8,128)(2,1)S(1)}, bf16[512,512]{1,0:T(8,128)(2,1)S(1)}, u32[]{:S(2)}, u32[]{:S(2)}) %collective-permute-start.11) | collective-permute-done | bytes 524320 | tf_op jit(solution)/shard_map/ppermute | solution.py:428
  130.4 0.0 collective-permute-done.14.refs_5_
  130.4 0.9 shard_map.165
  131.4 38.1 %all_to_all.11 = bf16[64,16,512]{2,1,0:T(8,128)(2,1)S(1)} all-to-all(bf16[64,16,512]{2,1,0:T(8,128)(2,1)S(1)} %bitcast.10), channel_id=1, replica_groups=mesh['dp'=4,'ep'=64] {'ep'}, dimensions={0} | all-to-all | bytes 2097152 | tf_op jit(solution)/shard_map/all_to_all | solution.py:434
  169.5 1.1 shard_map.167
  (6 shorter events, 0.0 us)
Async XLA Ops:
  0.6 59.9 %copy-start.3 = (bf16[8,64,256]{2,1,0:T(8,128)(2,1)S(1)}, bf16[8,64,256]{2,1,0:T(8,128)(2,1)}, u32[]{:S(2)}) copy-start(bf16[8,64,256]{2,1,0:T(8,128)(2,1)} %refs_2_.5) | copy-start | bytes 786436
  0.6 59.9 %copy-start.4 = (bf16[8,64,256]{2,1,0:T(8,128)(2,1)S(1)}, bf16[8,64,256]{2,1,0:T(8,128)(2,1)}, u32[]{:S(2)}) copy-start(bf16[8,64,256]{2,1,0:T(8,128)(2,1)} %refs_3_.6) | copy-start | bytes 786436
  0.7 64.9 %copy-start = (bf16[1,4096,384]{2,1,0:T(8,128)(2,1)S(1)}, bf16[1,4096,384]{2,1,0:T(8,128)(2,1)}, u32[]{:S(2)}) copy-start(bf16[1,4096,384]{2,1,0:T(8,128)(2,1)} %refs_2_.6) | copy-start | bytes 9437188
  4.3 9.6 %collective-permute-start = (f32[1,4096]{1,0:T(1,128)}, f32[1,4096]{1,0:T(1,128)S(1)}, u32[]{:S(2)}, u32[]{:S(2)}) collective-permute-start(f32[1,4096]{1,0:T(1,128)} %get-tuple-element.39), channel_id=1, source_target_pairs={{0,1},{1,2},{2,3},{3,4},{4,5},{5,6},{6,7},{7,8},{8,9},{9,10},{10,1... | collective-permute-start | bytes 49160 | tf_op jit(solution)/shard_map/ppermute | solution.py:428
  6.9 8.2 %collective-permute-start.1 = (f32[1,4096]{1,0:T(1,128)}, f32[1,4096]{1,0:T(1,128)S(1)}, u32[]{:S(2)}, u32[]{:S(2)}) collective-permute-start(f32[1,4096]{1,0:T(1,128)} %get-tuple-element.40), channel_id=1, source_target_pairs={{0,32},{1,33},{2,34},{3,35},{4,36},{5,37},{6,38},{7,39},{8,40},{9,... | collective-permute-start | bytes 49160 | tf_op jit(solution)/shard_map/ppermute | solution.py:428
  15.2 1.0 copy-start.5
  16.2 44.4 %copy-start.6 = (bf16[8,256]{1,0:T(8,128)(2,1)S(1)}, bf16[8,256]{1,0:T(8,128)(2,1)}, u32[]{:S(2)}) copy-start(bf16[8,256]{1,0:T(8,128)(2,1)} %refs_4_.5) | copy-start | bytes 12292
  16.2 44.4 %copy-start.7 = (bf16[8,256]{1,0:T(8,128)(2,1)S(1)}, bf16[8,256]{1,0:T(8,128)(2,1)}, u32[]{:S(2)}) copy-start(bf16[8,256]{1,0:T(8,128)(2,1)} %refs_5_.4) | copy-start | bytes 12292
  16.2 44.4 %copy-start.8 = (s32[8,2]{0,1:T(2,128)S(1)}, s32[8,2]{0,1:T(2,128)}, u32[]{:S(2)}) copy-start(s32[8,2]{0,1:T(2,128)} %param.21) | copy-start | bytes 196
  16.2 44.4 %copy-start.10 = (s32[8]{0:T(128)S(1)}, s32[8]{0:T(128)}, u32[]{:S(2)}) copy-start(s32[8]{0:T(128)} %refs_0_.4) | copy-start | bytes 100
  55.0 16.9 %collective-permute-start.2 = (bf16[512,512]{1,0:T(8,128)(2,1)S(1)}, bf16[512,512]{1,0:T(8,128)(2,1)S(1)}, u32[]{:S(2)}, u32[]{:S(2)}) collective-permute-start(bf16[512,512]{1,0:T(8,128)(2,1)S(1)} %bitcast.15), channel_id=1, source_target_pairs={{0,64},{64,128},{128,192},{192,0},{1,65},{65,129},{129,193},{193,1... | collective-permute-start | bytes 1572872 | tf_op jit(solution)/shard_map/ppermute | solution.py:428
  56.3 15.5 %collective-permute-start.3 = (bf16[512,512]{1,0:T(8,128)(2,1)S(1)}, bf16[512,512]{1,0:T(8,128)(2,1)S(1)}, u32[]{:S(2)}, u32[]{:S(2)}) collective-permute-start(bf16[512,512]{1,0:T(8,128)(2,1)S(1)} %bitcast.17), channel_id=1, source_target_pairs={{0,192},{64,0},{128,64},{192,128},{1,193},{65,1},{129,65},{193,129... | collective-permute-start | bytes 1572872 | tf_op jit(solution)/shard_map/ppermute | solution.py:428
  57.9 21.8 %collective-permute-start.7 = (bf16[512,512]{1,0:T(8,128)(2,1)S(1)}, bf16[512,512]{1,0:T(8,128)(2,1)S(1)}, u32[]{:S(2)}, u32[]{:S(2)}) collective-permute-start(bf16[512,512]{1,0:T(8,128)(2,1)S(1)} %bitcast.18), channel_id=1, source_target_pairs={{0,64},{64,128},{128,192},{192,0},{1,65},{65,129},{129,193},{193,1... | collective-permute-start | bytes 1572872 | tf_op jit(solution)/shard_map/ppermute | solution.py:428
  57.9 21.8 %collective-permute-start.8 = (bf16[512,512]{1,0:T(8,128)(2,1)S(1)}, bf16[512,512]{1,0:T(8,128)(2,1)S(1)}, u32[]{:S(2)}, u32[]{:S(2)}) collective-permute-start(bf16[512,512]{1,0:T(8,128)(2,1)S(1)} %bitcast.16), channel_id=1, source_target_pairs={{0,192},{64,0},{128,64},{192,128},{1,193},{65,1},{129,65},{193,129... | collective-permute-start | bytes 1572872 | tf_op jit(solution)/shard_map/ppermute | solution.py:428
  62.1 9.7 %collective-permute-start.4 = (bf16[128,256]{1,0:T(8,128)(2,1)S(1)}, bf16[128,256]{1,0:T(8,128)(2,1)S(1)}, u32[]{:S(2)}, u32[]{:S(2)}) collective-permute-start(bf16[128,256]{1,0:T(8,128)(2,1)S(1)} %get-tuple-element.49), channel_id=1, source_target_pairs={{0,1},{1,2},{2,3},{3,4},{4,5},{5,6},{6,7},{7,8},{8,9},{9,10},{10,1... | collective-permute-start | bytes 196616 | tf_op jit(solution)/shard_map/ppermute | solution.py:428
  65.6 1.9 %copy-start.1 = (bf16[1,4096,384]{2,1,0:T(8,128)(2,1)S(1)}, bf16[1,4096,384]{2,1,0:T(8,128)(2,1)}, u32[]{:S(2)}) copy-start(bf16[1,4096,384]{2,1,0:T(8,128)(2,1)} %refs_3_.7) | copy-start | bytes 9437188
  67.5 1.9 %copy-start.2 = (bf16[1,384,4096]{2,1,0:T(8,128)(2,1)S(1)}, bf16[1,384,4096]{2,1,0:T(8,128)(2,1)}, u32[]{:S(2)}) copy-start(bf16[1,384,4096]{2,1,0:T(8,128)(2,1)} %refs_4_.7) | copy-start | bytes 9437188
  71.9 19.0 %collective-permute-start.5 = (bf16[512,512]{1,0:T(8,128)(2,1)S(1)}, bf16[512,512]{1,0:T(8,128)(2,1)S(1)}, u32[]{:S(2)}, u32[]{:S(2)}) collective-permute-start(bf16[512,512]{1,0:T(8,128)(2,1)S(1)} %collective-permute-done.2.refs_0_), channel_id=1, source_target_pairs={{0,64},{64,128},{128,192},{192,0},{1,65},{65,129},{129,193},{193,1... | collective-permute-start | bytes 1572872 | tf_op jit(solution)/shard_map/ppermute | solution.py:428
  71.9 19.0 %collective-permute-start.6 = (bf16[512,512]{1,0:T(8,128)(2,1)S(1)}, bf16[512,512]{1,0:T(8,128)(2,1)S(1)}, u32[]{:S(2)}, u32[]{:S(2)}) collective-permute-start(bf16[512,512]{1,0:T(8,128)(2,1)S(1)} %collective-permute-done.3.refs_3_), channel_id=1, source_target_pairs={{0,192},{64,0},{128,64},{192,128},{1,193},{65,1},{129,65},{193,129... | collective-permute-start | bytes 1572872 | tf_op jit(solution)/shard_map/ppermute | solution.py:428
  90.9 22.4 %copy-start.9 = (s32[8,8]{1,0:T(8,128)S(1)}, s32[8,8]{1,0:T(8,128)}, u32[]{:S(2)}) copy-start(s32[8,8]{1,0:T(8,128)} %refs_0_.3) | copy-start | bytes 772
  90.9 22.4 %copy-start.11 = (f32[8,8]{1,0:T(8,128)S(1)}, f32[8,8]{1,0:T(8,128)}, u32[]{:S(2)}) copy-start(f32[8,8]{1,0:T(8,128)} %refs_1_.2) | copy-start | bytes 772
  93.4 11.5 %collective-permute-start.10 = (bf16[512,512]{1,0:T(8,128)(2,1)S(1)}, bf16[512,512]{1,0:T(8,128)(2,1)S(1)}, u32[]{:S(2)}, u32[]{:S(2)}) collective-permute-start(bf16[512,512]{1,0:T(8,128)(2,1)S(1)} %get-tuple-element.61), channel_id=1, source_target_pairs={{0,192},{64,0},{128,64},{192,128},{1,193},{65,1},{129,65},{193,129... | collective-permute-start | bytes 1572872 | tf_op jit(solution)/shard_map/ppermute | solution.py:428
  96.0 11.9 %collective-permute-start.9 = (bf16[512,512]{1,0:T(8,128)(2,1)S(1)}, bf16[512,512]{1,0:T(8,128)(2,1)S(1)}, u32[]{:S(2)}, u32[]{:S(2)}) collective-permute-start(bf16[512,512]{1,0:T(8,128)(2,1)S(1)} %get-tuple-element.60), channel_id=1, source_target_pairs={{0,64},{64,128},{128,192},{192,0},{1,65},{65,129},{129,193},{193,1... | collective-permute-start | bytes 1572872 | tf_op jit(solution)/shard_map/ppermute | solution.py:428
  96.0 23.2 %collective-permute-start.12 = (bf16[512,512]{1,0:T(8,128)(2,1)S(1)}, bf16[512,512]{1,0:T(8,128)(2,1)S(1)}, u32[]{:S(2)}, u32[]{:S(2)}) collective-permute-start(bf16[512,512]{1,0:T(8,128)(2,1)S(1)} %get-tuple-element.63), channel_id=1, source_target_pairs={{0,64},{64,128},{128,192},{192,0},{1,65},{65,129},{129,193},{193,1... | collective-permute-start | bytes 1572872 | tf_op jit(solution)/shard_map/ppermute | solution.py:428
  96.0 23.2 %collective-permute-start.13 = (bf16[512,512]{1,0:T(8,128)(2,1)S(1)}, bf16[512,512]{1,0:T(8,128)(2,1)S(1)}, u32[]{:S(2)}, u32[]{:S(2)}) collective-permute-start(bf16[512,512]{1,0:T(8,128)(2,1)S(1)} %get-tuple-element.64), channel_id=1, source_target_pairs={{0,192},{64,0},{128,64},{192,128},{1,193},{65,1},{129,65},{193,129... | collective-permute-start | bytes 1572872 | tf_op jit(solution)/shard_map/ppermute | solution.py:428
  108.2 22.2 %collective-permute-start.11 = (bf16[512,512]{1,0:T(8,128)(2,1)S(1)}, bf16[512,512]{1,0:T(8,128)(2,1)S(1)}, u32[]{:S(2)}, u32[]{:S(2)}) collective-permute-start(bf16[512,512]{1,0:T(8,128)(2,1)S(1)} %get-tuple-element.62), channel_id=1, source_target_pairs={{0,64},{64,128},{128,192},{192,0},{1,65},{65,129},{129,193},{193,1... | collective-permute-start | bytes 1572872 | tf_op jit(solution)/shard_map/ppermute | solution.py:428
  108.3 22.1 %collective-permute-start.14 = (bf16[512,512]{1,0:T(8,128)(2,1)S(1)}, bf16[512,512]{1,0:T(8,128)(2,1)S(1)}, u32[]{:S(2)}, u32[]{:S(2)}) collective-permute-start(bf16[512,512]{1,0:T(8,128)(2,1)S(1)} %get-tuple-element.65), channel_id=1, source_target_pairs={{0,192},{64,0},{128,64},{192,128},{1,193},{65,1},{129,65},{193,129... | collective-permute-start | bytes 1572872 | tf_op jit(solution)/shard_map/ppermute | solution.py:428
  111.0 7.0 %collective-permute-start.15 = (bf16[128,256]{1,0:T(8,128)(2,1)S(1)}, bf16[128,256]{1,0:T(8,128)(2,1)S(1)}, u32[]{:S(2)}, u32[]{:S(2)}) collective-permute-start(bf16[128,256]{1,0:T(8,128)(2,1)S(1)} %get-tuple-element.67), channel_id=1, source_target_pairs={{0,32},{1,33},{2,34},{3,35},{4,36},{5,37},{6,38},{7,39},{8,40},{9,... | collective-permute-start | bytes 196616 | tf_op jit(solution)/shard_map/ppermute | solution.py:428

commit v4 on v3

--- a/solution.py
+++ b/solution.py
@@ -462,6 +462,9 @@
     far_terms = experts_of([far_top, far_bottom], weights)
     relayed_left = rotate(far_terms[0], "dp", 1)
     relayed_right = rotate(far_terms[1], "dp", -1)
+    relayed_left, relayed_right, direct_left, direct_right = lax.optimization_barrier(
+        (relayed_left, relayed_right, direct_left, direct_right)
+    )
     block = shape_of(far_top.shape, BF16)
     size = 2 * block.size
     to_right, to_left = call(

time: 171 us -> 166 us (0.971)
  waiting for transfers between devices: 37.2 us -> 33 us
    ppermute x16, waiting for transfers between devices: 37.2 us -> 33 us  [rotate(): lax.ppermute(member, axis, [(s, (s + distance) % count) for s in range(co...]
  transfers between devices with their start and end apart: 16 -> 16, of which waited for: 7 -> 8; matrix products, arithmetic and copies ran while one was open for 0% -> 0% of each run, Pallas kernels for 6% -> 8%
where the time goes in v4:
time: 166 us
  blocking collectives  75.6 us (46%)
  waiting for transfers between devices  33 us (20%)
  starting transfers between devices  31.7 us (19%)
  Pallas kernels  19.7 us (12%)
  local copies, waits for them, and re-layouts  4.88 us (3%)
    all_to_all x2, blocking collectives, exchange(): cut = lax.all_to_all(cut, 'ep', split_axis=0, concat_axis=0, tiled=True)  75.6 us
    ppermute x16, waiting for transfers between devices, rotate(): lax.ppermute(member, axis, [(s, (s + distance) % count) for s in range(co...  33 us
    ppermute x16, starting transfers between devices, rotate(): lax.ppermute(member, axis, [(s, (s + distance) % count) for s in range(co...  31.7 us
    pallas_call x10, Pallas kernels, call(): pl.pallas_call(body, out_shape=outs, grid_spec=pltpu.PrefetchScalarGridSp...  18.5 us
    unnamed x24, local copies, waits for them, and re-layouts  4.81 us
  transfers between devices with their start and end apart: 16, of which 8 were waited for; matrix products, arithmetic and copies ran while one was open for 0% of the time, Pallas kernels for 8%

profile of v4, /device:TPU:1, one launch (start us, length us, event | category | flops | bytes accessed | tf_op | source)
XLA Modules:
  0.0 165.7 jit_solution(16201838400794251605)
XLA Ops:
  0.6 0.0 copy-start.3
  0.6 0.0 copy-start.4
  0.7 0.0 copy-start
  0.7 3.6 %shard_map.157 = (f32[24,4096]{1,0:T(8,128)}, f32[1,4096]{1,0:T(1,128)}, f32[1,4096]{1,0:T(1,128)}) custom-call(s32[8]{0:T(128)} %refs_0_.4, s32[2,8]{1,0:T(2,128)} %bitcast.12, bf16[8,4096]{1,0:T(8,128)(2,1)} %refs_2_.3, bf16[8,64,256]{2,1,0:T(8,128)(2,1)} %refs_2_.5, bf16[8,256]{1,0:T(8,128)(2,1)} %refs_4_.5, bf16[8,64,256]{2,1,0:T(8,128)(2,1)} %refs_3_.6, ...), custom_call_target="tpu_custom_call" | custom-call | flops 100000000 | bytes 3000000 | tf_op jit(solution)/shard_map/pallas_call | solution.py:388
  4.3 2.7 %collective-permute-start = (f32[1,4096]{1,0:T(1,128)}, f32[1,4096]{1,0:T(1,128)S(1)}, u32[]{:S(2)}, u32[]{:S(2)}) collective-permute-start(f32[1,4096]{1,0:T(1,128)} %get-tuple-element.43), channel_id=1, source_target_pairs={{0,1},{1,2},{2,3},{3,4},{4,5},{5,6},{6,7},{7,8},{8,9},{9,10},{10,1... | collective-permute-start | bytes 49160 | tf_op jit(solution)/shard_map/ppermute | solution.py:428
  6.9 6.9 %collective-permute-start.1 = (f32[1,4096]{1,0:T(1,128)}, f32[1,4096]{1,0:T(1,128)S(1)}, u32[]{:S(2)}, u32[]{:S(2)}) collective-permute-start(f32[1,4096]{1,0:T(1,128)} %get-tuple-element.44), channel_id=1, source_target_pairs={{0,32},{1,33},{2,34},{3,35},{4,36},{5,37},{6,38},{7,39},{8,40},{9,... | collective-permute-start | bytes 49160 | tf_op jit(solution)/shard_map/ppermute | solution.py:428
  13.9 0.0 collective-permute-done.refs_1_
  13.9 1.3 collective-permute-done.1.refs_2_
  15.2 0.0 copy-start.5
  15.2 1.0 copy-done.5
  16.2 0.0 copy-start.6
  16.2 0.0 copy-start.7
  16.2 0.7 shard_map.158
  16.9 37.9 %all_to_all.10 = bf16[64,16,512]{2,1,0:T(8,128)(2,1)S(1)} all-to-all(bf16[64,16,512]{2,1,0:T(8,128)(2,1)S(1)} %bitcast.11), channel_id=1, replica_groups=mesh['dp'=4,'ep'=64] {'ep'}, dimensions={0} | all-to-all | bytes 2097152 | tf_op jit(solution)/shard_map/all_to_all | solution.py:434
  54.9 0.1 fusion
  55.0 1.4 collective-permute-start.2
  56.3 1.5 collective-permute-start.3
  57.9 0.0 collective-permute-start.7
  57.9 2.7 %collective-permute-start.8 = (bf16[512,512]{1,0:T(8,128)(2,1)S(1)}, bf16[512,512]{1,0:T(8,128)(2,1)S(1)}, u32[]{:S(2)}, u32[]{:S(2)}) collective-permute-start(bf16[512,512]{1,0:T(8,128)(2,1)S(1)} %bitcast.16), channel_id=1, source_target_pairs={{0,192},{64,0},{128,64},{192,128},{1,193},{65,1},{129,65},{193,129... | collective-permute-start | bytes 1572872 | tf_op jit(solution)/shard_map/ppermute | solution.py:428
  60.5 0.0 copy-done.3
  60.5 0.0 copy-done.4
  60.5 0.0 copy-done.6
  60.5 0.0 copy-done.7
  60.5 0.0 copy-done.8
  60.6 0.0 copy-done.10
  60.6 1.5 shard_map.161
  62.1 3.5 %collective-permute-start.4 = (bf16[128,256]{1,0:T(8,128)(2,1)S(1)}, bf16[128,256]{1,0:T(8,128)(2,1)S(1)}, u32[]{:S(2)}, u32[]{:S(2)}) collective-permute-start(bf16[128,256]{1,0:T(8,128)(2,1)S(1)} %get-tuple-element.53), channel_id=1, source_target_pairs={{0,1},{1,2},{2,3},{3,4},{4,5},{5,6},{6,7},{7,8},{8,9},{9,10},{10,1... | collective-permute-start | bytes 196616 | tf_op jit(solution)/shard_map/ppermute | solution.py:428
  65.6 0.0 copy-done
  65.6 1.9 %copy-done.1 = bf16[1,4096,384]{2,1,0:T(8,128)(2,1)S(1)} copy-done((bf16[1,4096,384]{2,1,0:T(8,128)(2,1)S(1)}, bf16[1,4096,384]{2,1,0:T(8,128)(2,1)}, u32[]{:S(2)}) %copy-start.1) | copy-done | bytes 3145752
  67.5 1.9 %copy-done.2 = bf16[1,384,4096]{2,1,0:T(8,128)(2,1)S(1)} copy-done((bf16[1,384,4096]{2,1,0:T(8,128)(2,1)S(1)}, bf16[1,384,4096]{2,1,0:T(8,128)(2,1)}, u32[]{:S(2)}) %copy-start.2) | copy-done | bytes 3145752
  69.3 2.5 %shard_map.160 = (bf16[512,512]{1,0:T(8,128)(2,1)S(1)}, bf16[512,512]{1,0:T(8,128)(2,1)S(1)}) custom-call(bf16[1024,512]{1,0:T(8,128)(2,1)S(1)} %bitcast.8, bf16[1,4096,384]{2,1,0:T(8,128)(2,1)S(1)} %copy-done, bf16[1,4096,384]{2,1,0:T(8,128)(2,1)S(1)} %copy-done.1, bf16[1,384,4096]{2,1,0:T(8,128)(2,1)S(1)} %copy-done.2), custom_call_target="tpu_custom_call" | custom-call | flops 1207959552 | bytes 11534336 | tf_op jit(solution)/shard_map/pallas_call | solution.py:388
  71.8 0.0 collective-permute-done.4.refs_1_
  71.8 0.0 collective-permute-done.2.refs_0_
  71.8 0.0 collective-permute-done.3.refs_3_
  71.9 0.1 collective-permute-start.5
  71.9 2.7 %collective-permute-start.6 = (bf16[512,512]{1,0:T(8,128)(2,1)S(1)}, bf16[512,512]{1,0:T(8,128)(2,1)S(1)}, u32[]{:S(2)}, u32[]{:S(2)}) collective-permute-start(bf16[512,512]{1,0:T(8,128)(2,1)S(1)} %collective-permute-done.3.refs_3_), channel_id=1, source_target_pairs={{0,192},{64,0},{128,64},{192,128},{1,193},{65,1},{129,65},{193,129... | collective-permute-start | bytes 1572872 | tf_op jit(solution)/shard_map/ppermute | solution.py:428
  74.6 5.1 %collective-permute-done.7.refs_1_ = bf16[512,512]{1,0:T(8,128)(2,1)S(1)} collective-permute-done((bf16[512,512]{1,0:T(8,128)(2,1)S(1)}, bf16[512,512]{1,0:T(8,128)(2,1)S(1)}, u32[]{:S(2)}, u32[]{:S(2)}) %collective-permute-start.7) | collective-permute-done | bytes 524320 | tf_op jit(solution)/shard_map/ppermute | solution.py:428
  79.7 0.0 collective-permute-done.8.refs_2_
  79.7 4.6 %shard_map.162 = (bf16[512,512]{1,0:T(8,128)(2,1)S(1)}, bf16[512,512]{1,0:T(8,128)(2,1)S(1)}, bf16[512,512]{1,0:T(8,128)(2,1)S(1)}, bf16[512,512]{1,0:T(8,128)(2,1)S(1)}) custom-call(bf16[512,512]{1,0:T(8,128)(2,1)S(1)} %collective-permute-done.2.refs_0_, bf16[512,512]{1,0:T(8,128)(2,1)S(1)} %collective-permute-done.7.refs_1_, ...), custom_call_target="tpu_custom_call" | custom-call | flops 2415919104 | bytes 13631488 | tf_op jit(solution)/shard_map/pallas_call | solution.py:388
  84.3 1.0 collective-permute-start.11
  85.3 1.7 %collective-permute-start.12 = (bf16[512,512]{1,0:T(8,128)(2,1)S(1)}, bf16[512,512]{1,0:T(8,128)(2,1)S(1)}, u32[]{:S(2)}, u32[]{:S(2)}) collective-permute-start(bf16[512,512]{1,0:T(8,128)(2,1)S(1)} %get-tuple-element.67), channel_id=1, source_target_pairs={{0,192},{64,0},{128,64},{192,128},{1,193},{65,1},{129,65},{193,129... | collective-permute-start | bytes 1572872 | tf_op jit(solution)/shard_map/ppermute | solution.py:428
  87.0 3.9 %collective-permute-done.5.refs_0_ = bf16[512,512]{1,0:T(8,128)(2,1)S(1)} collective-permute-done((bf16[512,512]{1,0:T(8,128)(2,1)S(1)}, bf16[512,512]{1,0:T(8,128)(2,1)S(1)}, u32[]{:S(2)}, u32[]{:S(2)}) %collective-permute-start.5) | collective-permute-done | bytes 524320 | tf_op jit(solution)/shard_map/ppermute | solution.py:428
  90.9 0.0 collective-permute-done.6.refs_1_
  90.9 2.5 %shard_map.163 = (bf16[512,512]{1,0:T(8,128)(2,1)S(1)}, bf16[512,512]{1,0:T(8,128)(2,1)S(1)}) custom-call(bf16[512,512]{1,0:T(8,128)(2,1)S(1)} %collective-permute-done.5.refs_0_, bf16[512,512]{1,0:T(8,128)(2,1)S(1)} %collective-permute-done.6.refs_1_, bf16[1,4096,384]{2,1,0:T(8,128)(2,1)S(1)} %copy-done, bf16[1,4096,384]{2,1,0:T(8,128)(2,1)S(1)} %copy-done.1, ...), custom_call_target="tpu_custom_call" | custom-call | flops 1207959552 | bytes 11534336 | tf_op jit(solution)/shard_map/pallas_call | solution.py:388
  93.4 2.6 %collective-permute-start.10 = (bf16[512,512]{1,0:T(8,128)(2,1)S(1)}, bf16[512,512]{1,0:T(8,128)(2,1)S(1)}, u32[]{:S(2)}, u32[]{:S(2)}) collective-permute-start(bf16[512,512]{1,0:T(8,128)(2,1)S(1)} %get-tuple-element.65), channel_id=1, source_target_pairs={{0,192},{64,0},{128,64},{192,128},{1,193},{65,1},{129,65},{193,129... | collective-permute-start | bytes 1572872 | tf_op jit(solution)/shard_map/ppermute | solution.py:428
  96.0 0.0 collective-permute-start.9
  96.0 6.1 %collective-permute-done.11.refs_3_ = bf16[512,512]{1,0:T(8,128)(2,1)S(1)} collective-permute-done((bf16[512,512]{1,0:T(8,128)(2,1)S(1)}, bf16[512,512]{1,0:T(8,128)(2,1)S(1)}, u32[]{:S(2)}, u32[]{:S(2)}) %collective-permute-start.11) | collective-permute-done | bytes 524320 | tf_op jit(solution)/shard_map/ppermute | solution.py:428
  102.1 0.0 collective-permute-done.12.refs_4_
  102.1 10.9 %collective-permute-done.10.refs_3_ = bf16[512,512]{1,0:T(8,128)(2,1)S(1)} collective-permute-done((bf16[512,512]{1,0:T(8,128)(2,1)S(1)}, bf16[512,512]{1,0:T(8,128)(2,1)S(1)}, u32[]{:S(2)}, u32[]{:S(2)}) %collective-permute-start.10) | collective-permute-done | bytes 524320 | tf_op jit(solution)/shard_map/ppermute | solution.py:428
  113.0 0.3 collective-permute-done.9.refs_2_
  113.4 0.2 shard_map.164
  113.6 1.1 collective-permute-start.13
  114.7 1.7 %collective-permute-start.14 = (bf16[512,512]{1,0:T(8,128)(2,1)S(1)}, bf16[512,512]{1,0:T(8,128)(2,1)S(1)}, u32[]{:S(2)}, u32[]{:S(2)}) collective-permute-start(bf16[512,512]{1,0:T(8,128)(2,1)S(1)} %get-tuple-element.73), channel_id=1, source_target_pairs={{0,192},{64,0},{128,64},{192,128},{1,193},{65,1},{129,65},{193,129... | collective-permute-start | bytes 1572872 | tf_op jit(solution)/shard_map/ppermute | solution.py:428
  116.4 2.2 %collective-permute-start.15 = (bf16[128,256]{1,0:T(8,128)(2,1)S(1)}, bf16[128,256]{1,0:T(8,128)(2,1)S(1)}, u32[]{:S(2)}, u32[]{:S(2)}) collective-permute-start(bf16[128,256]{1,0:T(8,128)(2,1)S(1)} %get-tuple-element.75), channel_id=1, source_target_pairs={{0,32},{1,33},{2,34},{3,35},{4,36},{5,37},{6,38},{7,39},{8,40},{9,... | collective-permute-start | bytes 196616 | tf_op jit(solution)/shard_map/ppermute | solution.py:428
  118.5 0.0 copy-done.9
  118.5 0.0 copy-done.11
  118.5 0.9 shard_map.159
  119.4 4.0 %collective-permute-done.15.refs_2_ = bf16[128,256]{1,0:T(8,128)(2,1)S(1)} collective-permute-done((bf16[128,256]{1,0:T(8,128)(2,1)S(1)}, bf16[128,256]{1,0:T(8,128)(2,1)S(1)}, u32[]{:S(2)}, u32[]{:S(2)}) %collective-permute-start.15) | collective-permute-done | bytes 65568 | tf_op jit(solution)/shard_map/ppermute | solution.py:428
  123.4 1.3 shard_map.166
  124.7 1.4 collective-permute-done.13.refs_2_
  126.1 0.0 collective-permute-done.14.refs_5_
  126.1 0.9 shard_map.165
  127.0 37.7 %all_to_all.11 = bf16[64,16,512]{2,1,0:T(8,128)(2,1)S(1)} all-to-all(bf16[64,16,512]{2,1,0:T(8,128)(2,1)S(1)} %bitcast.10), channel_id=1, replica_groups=mesh['dp'=4,'ep'=64] {'ep'}, dimensions={0} | all-to-all | bytes 2097152 | tf_op jit(solution)/shard_map/all_to_all | solution.py:434
  164.6 1.1 shard_map.167
  (6 shorter events, 0.0 us)
Async XLA Ops:
  0.6 59.9 %copy-start.3 = (bf16[8,64,256]{2,1,0:T(8,128)(2,1)S(1)}, bf16[8,64,256]{2,1,0:T(8,128)(2,1)}, u32[]{:S(2)}) copy-start(bf16[8,64,256]{2,1,0:T(8,128)(2,1)} %refs_2_.5) | copy-start | bytes 786436
  0.6 59.9 %copy-start.4 = (bf16[8,64,256]{2,1,0:T(8,128)(2,1)S(1)}, bf16[8,64,256]{2,1,0:T(8,128)(2,1)}, u32[]{:S(2)}) copy-start(bf16[8,64,256]{2,1,0:T(8,128)(2,1)} %refs_3_.6) | copy-start | bytes 786436
  0.7 64.9 %copy-start = (bf16[1,4096,384]{2,1,0:T(8,128)(2,1)S(1)}, bf16[1,4096,384]{2,1,0:T(8,128)(2,1)}, u32[]{:S(2)}) copy-start(bf16[1,4096,384]{2,1,0:T(8,128)(2,1)} %refs_2_.6) | copy-start | bytes 9437188
  4.3 9.6 %collective-permute-start = (f32[1,4096]{1,0:T(1,128)}, f32[1,4096]{1,0:T(1,128)S(1)}, u32[]{:S(2)}, u32[]{:S(2)}) collective-permute-start(f32[1,4096]{1,0:T(1,128)} %get-tuple-element.43), channel_id=1, source_target_pairs={{0,1},{1,2},{2,3},{3,4},{4,5},{5,6},{6,7},{7,8},{8,9},{9,10},{10,1... | collective-permute-start | bytes 49160 | tf_op jit(solution)/shard_map/ppermute | solution.py:428
  6.9 8.2 %collective-permute-start.1 = (f32[1,4096]{1,0:T(1,128)}, f32[1,4096]{1,0:T(1,128)S(1)}, u32[]{:S(2)}, u32[]{:S(2)}) collective-permute-start(f32[1,4096]{1,0:T(1,128)} %get-tuple-element.44), channel_id=1, source_target_pairs={{0,32},{1,33},{2,34},{3,35},{4,36},{5,37},{6,38},{7,39},{8,40},{9,... | collective-permute-start | bytes 49160 | tf_op jit(solution)/shard_map/ppermute | solution.py:428
  15.2 1.0 copy-start.5
  16.2 44.4 %copy-start.6 = (bf16[8,256]{1,0:T(8,128)(2,1)S(1)}, bf16[8,256]{1,0:T(8,128)(2,1)}, u32[]{:S(2)}) copy-start(bf16[8,256]{1,0:T(8,128)(2,1)} %refs_4_.5) | copy-start | bytes 12292
  16.2 44.4 %copy-start.7 = (bf16[8,256]{1,0:T(8,128)(2,1)S(1)}, bf16[8,256]{1,0:T(8,128)(2,1)}, u32[]{:S(2)}) copy-start(bf16[8,256]{1,0:T(8,128)(2,1)} %refs_5_.4) | copy-start | bytes 12292
  16.2 44.4 %copy-start.8 = (s32[8,2]{0,1:T(2,128)S(1)}, s32[8,2]{0,1:T(2,128)}, u32[]{:S(2)}) copy-start(s32[8,2]{0,1:T(2,128)} %param.21) | copy-start | bytes 196
  16.2 44.4 %copy-start.10 = (s32[8]{0:T(128)S(1)}, s32[8]{0:T(128)}, u32[]{:S(2)}) copy-start(s32[8]{0:T(128)} %refs_0_.4) | copy-start | bytes 100
  55.0 16.9 %collective-permute-start.2 = (bf16[512,512]{1,0:T(8,128)(2,1)S(1)}, bf16[512,512]{1,0:T(8,128)(2,1)S(1)}, u32[]{:S(2)}, u32[]{:S(2)}) collective-permute-start(bf16[512,512]{1,0:T(8,128)(2,1)S(1)} %bitcast.15), channel_id=1, source_target_pairs={{0,64},{64,128},{128,192},{192,0},{1,65},{65,129},{129,193},{193,1... | collective-permute-start | bytes 1572872 | tf_op jit(solution)/shard_map/ppermute | solution.py:428
  56.3 15.5 %collective-permute-start.3 = (bf16[512,512]{1,0:T(8,128)(2,1)S(1)}, bf16[512,512]{1,0:T(8,128)(2,1)S(1)}, u32[]{:S(2)}, u32[]{:S(2)}) collective-permute-start(bf16[512,512]{1,0:T(8,128)(2,1)S(1)} %bitcast.17), channel_id=1, source_target_pairs={{0,192},{64,0},{128,64},{192,128},{1,193},{65,1},{129,65},{193,129... | collective-permute-start | bytes 1572872 | tf_op jit(solution)/shard_map/ppermute | solution.py:428
  57.9 21.8 %collective-permute-start.7 = (bf16[512,512]{1,0:T(8,128)(2,1)S(1)}, bf16[512,512]{1,0:T(8,128)(2,1)S(1)}, u32[]{:S(2)}, u32[]{:S(2)}) collective-permute-start(bf16[512,512]{1,0:T(8,128)(2,1)S(1)} %bitcast.18), channel_id=1, source_target_pairs={{0,64},{64,128},{128,192},{192,0},{1,65},{65,129},{129,193},{193,1... | collective-permute-start | bytes 1572872 | tf_op jit(solution)/shard_map/ppermute | solution.py:428
  57.9 21.8 %collective-permute-start.8 = (bf16[512,512]{1,0:T(8,128)(2,1)S(1)}, bf16[512,512]{1,0:T(8,128)(2,1)S(1)}, u32[]{:S(2)}, u32[]{:S(2)}) collective-permute-start(bf16[512,512]{1,0:T(8,128)(2,1)S(1)} %bitcast.16), channel_id=1, source_target_pairs={{0,192},{64,0},{128,64},{192,128},{1,193},{65,1},{129,65},{193,129... | collective-permute-start | bytes 1572872 | tf_op jit(solution)/shard_map/ppermute | solution.py:428
  62.1 9.7 %collective-permute-start.4 = (bf16[128,256]{1,0:T(8,128)(2,1)S(1)}, bf16[128,256]{1,0:T(8,128)(2,1)S(1)}, u32[]{:S(2)}, u32[]{:S(2)}) collective-permute-start(bf16[128,256]{1,0:T(8,128)(2,1)S(1)} %get-tuple-element.53), channel_id=1, source_target_pairs={{0,1},{1,2},{2,3},{3,4},{4,5},{5,6},{6,7},{7,8},{8,9},{9,10},{10,1... | collective-permute-start | bytes 196616 | tf_op jit(solution)/shard_map/ppermute | solution.py:428
  65.6 1.9 %copy-start.1 = (bf16[1,4096,384]{2,1,0:T(8,128)(2,1)S(1)}, bf16[1,4096,384]{2,1,0:T(8,128)(2,1)}, u32[]{:S(2)}) copy-start(bf16[1,4096,384]{2,1,0:T(8,128)(2,1)} %refs_3_.7) | copy-start | bytes 9437188
  67.5 1.9 %copy-start.2 = (bf16[1,384,4096]{2,1,0:T(8,128)(2,1)S(1)}, bf16[1,384,4096]{2,1,0:T(8,128)(2,1)}, u32[]{:S(2)}) copy-start(bf16[1,384,4096]{2,1,0:T(8,128)(2,1)} %refs_4_.7) | copy-start | bytes 9437188
  71.9 19.0 %collective-permute-start.5 = (bf16[512,512]{1,0:T(8,128)(2,1)S(1)}, bf16[512,512]{1,0:T(8,128)(2,1)S(1)}, u32[]{:S(2)}, u32[]{:S(2)}) collective-permute-start(bf16[512,512]{1,0:T(8,128)(2,1)S(1)} %collective-permute-done.2.refs_0_), channel_id=1, source_target_pairs={{0,64},{64,128},{128,192},{192,0},{1,65},{65,129},{129,193},{193,1... | collective-permute-start | bytes 1572872 | tf_op jit(solution)/shard_map/ppermute | solution.py:428
  71.9 19.0 %collective-permute-start.6 = (bf16[512,512]{1,0:T(8,128)(2,1)S(1)}, bf16[512,512]{1,0:T(8,128)(2,1)S(1)}, u32[]{:S(2)}, u32[]{:S(2)}) collective-permute-start(bf16[512,512]{1,0:T(8,128)(2,1)S(1)} %collective-permute-done.3.refs_3_), channel_id=1, source_target_pairs={{0,192},{64,0},{128,64},{192,128},{1,193},{65,1},{129,65},{193,129... | collective-permute-start | bytes 1572872 | tf_op jit(solution)/shard_map/ppermute | solution.py:428
  84.3 17.9 %collective-permute-start.11 = (bf16[512,512]{1,0:T(8,128)(2,1)S(1)}, bf16[512,512]{1,0:T(8,128)(2,1)S(1)}, u32[]{:S(2)}, u32[]{:S(2)}) collective-permute-start(bf16[512,512]{1,0:T(8,128)(2,1)S(1)} %get-tuple-element.66), channel_id=1, source_target_pairs={{0,64},{64,128},{128,192},{192,0},{1,65},{65,129},{129,193},{193,1... | collective-permute-start | bytes 1572872 | tf_op jit(solution)/shard_map/ppermute | solution.py:428
  85.3 16.8 %collective-permute-start.12 = (bf16[512,512]{1,0:T(8,128)(2,1)S(1)}, bf16[512,512]{1,0:T(8,128)(2,1)S(1)}, u32[]{:S(2)}, u32[]{:S(2)}) collective-permute-start(bf16[512,512]{1,0:T(8,128)(2,1)S(1)} %get-tuple-element.67), channel_id=1, source_target_pairs={{0,192},{64,0},{128,64},{192,128},{1,193},{65,1},{129,65},{193,129... | collective-permute-start | bytes 1572872 | tf_op jit(solution)/shard_map/ppermute | solution.py:428
  90.9 27.6 %copy-start.9 = (s32[8,8]{1,0:T(8,128)S(1)}, s32[8,8]{1,0:T(8,128)}, u32[]{:S(2)}) copy-start(s32[8,8]{1,0:T(8,128)} %refs_0_.3) | copy-start | bytes 772
  90.9 27.6 %copy-start.11 = (f32[8,8]{1,0:T(8,128)S(1)}, f32[8,8]{1,0:T(8,128)}, u32[]{:S(2)}) copy-start(f32[8,8]{1,0:T(8,128)} %refs_1_.2) | copy-start | bytes 772
  93.4 19.7 %collective-permute-start.10 = (bf16[512,512]{1,0:T(8,128)(2,1)S(1)}, bf16[512,512]{1,0:T(8,128)(2,1)S(1)}, u32[]{:S(2)}, u32[]{:S(2)}) collective-permute-start(bf16[512,512]{1,0:T(8,128)(2,1)S(1)} %get-tuple-element.65), channel_id=1, source_target_pairs={{0,192},{64,0},{128,64},{192,128},{1,193},{65,1},{129,65},{193,129... | collective-permute-start | bytes 1572872 | tf_op jit(solution)/shard_map/ppermute | solution.py:428
  96.0 17.4 %collective-permute-start.9 = (bf16[512,512]{1,0:T(8,128)(2,1)S(1)}, bf16[512,512]{1,0:T(8,128)(2,1)S(1)}, u32[]{:S(2)}, u32[]{:S(2)}) collective-permute-start(bf16[512,512]{1,0:T(8,128)(2,1)S(1)} %get-tuple-element.64), channel_id=1, source_target_pairs={{0,64},{64,128},{128,192},{192,0},{1,65},{65,129},{129,193},{193,1... | collective-permute-start | bytes 1572872 | tf_op jit(solution)/shard_map/ppermute | solution.py:428
  113.6 12.5 %collective-permute-start.13 = (bf16[512,512]{1,0:T(8,128)(2,1)S(1)}, bf16[512,512]{1,0:T(8,128)(2,1)S(1)}, u32[]{:S(2)}, u32[]{:S(2)}) collective-permute-start(bf16[512,512]{1,0:T(8,128)(2,1)S(1)} %get-tuple-element.70), channel_id=1, source_target_pairs={{0,64},{64,128},{128,192},{192,0},{1,65},{65,129},{129,193},{193,1... | collective-permute-start | bytes 1572872 | tf_op jit(solution)/shard_map/ppermute | solution.py:428
  114.7 11.4 %collective-permute-start.14 = (bf16[512,512]{1,0:T(8,128)(2,1)S(1)}, bf16[512,512]{1,0:T(8,128)(2,1)S(1)}, u32[]{:S(2)}, u32[]{:S(2)}) collective-permute-start(bf16[512,512]{1,0:T(8,128)(2,1)S(1)} %get-tuple-element.73), channel_id=1, source_target_pairs={{0,192},{64,0},{128,64},{192,128},{1,193},{65,1},{129,65},{193,129... | collective-permute-start | bytes 1572872 | tf_op jit(solution)/shard_map/ppermute | solution.py:428
  116.4 7.0 %collective-permute-start.15 = (bf16[128,256]{1,0:T(8,128)(2,1)S(1)}, bf16[128,256]{1,0:T(8,128)(2,1)S(1)}, u32[]{:S(2)}, u32[]{:S(2)}) collective-permute-start(bf16[128,256]{1,0:T(8,128)(2,1)S(1)} %get-tuple-element.75), channel_id=1, source_target_pairs={{0,32},{1,33},{2,34},{3,35},{4,36},{5,37},{6,38},{7,39},{8,40},{9,... | collective-permute-start | bytes 196616 | tf_op jit(solution)/shard_map/ppermute | solution.py:428

commit v5 on v3

--- a/solution.py
+++ b/solution.py
@@ -220,10 +220,10 @@
     )
 
 
-def expert_kernel(n_pieces, n_blocks, *refs):
+def expert_kernel(n_pieces, n_blocks, cuts, *refs):
     piece_refs = refs[:n_pieces]
     gate_ref, up_ref, down_ref = refs[n_pieces : n_pieces + 3]
-    out_refs = refs[n_pieces + 3 : n_pieces + 3 + n_blocks]
+    out_refs = refs[n_pieces + 3 : n_pieces + 3 + cuts * n_blocks]
     rows_ref = refs[-1]
     model_width, hidden_width = gate_ref.shape[1:]
     count = STEP // COLS
@@ -248,34 +248,44 @@
         term = jnp.dot(
             hidden, down_ref[0, :, c * part : (c + 1) * part], preferred_element_type=F32
         ).astype(BF16)
+        cut, at = divmod(c, COLS // cuts)
         for n in range(n_blocks):
-            out_refs[n][c * count : (c + 1) * count] = term[n * count : (n + 1) * count]
-
-
-def relay_kernel(right_ref, left_ref, from_left_ref, from_right_ref, to_right_ref, to_left_ref):
-    to_right_ref[...] = (right_ref[...].astype(F32) + from_left_ref[...].astype(F32)).astype(BF16)
-    to_left_ref[...] = (left_ref[...].astype(F32) + from_right_ref[...].astype(F32)).astype(BF16)
+            out_refs[cuts * n + cut][at * count : (at + 1) * count] = term[
+                n * count : (n + 1) * count
+            ]
+
+
+def relay_kernel(
+    cut, right_ref, left_ref, from_left_ref, from_right_ref, to_right_ref, to_left_ref
+):
+    rows = from_left_ref.shape[0]
+    here = slice(cut * rows, (cut + 1) * rows)
+    to_right_ref[...] = (right_ref[here].astype(F32) + from_left_ref[...].astype(F32)).astype(BF16)
+    to_left_ref[...] = (left_ref[here].astype(F32) + from_right_ref[...].astype(F32)).astype(BF16)
 
 
 def gather_kernel(
     own_top_ref,
     own_bottom_ref,
-    left_top_ref,
     left_bottom_ref,
     right_top_ref,
-    right_bottom_ref,
+    left_first_ref,
+    left_second_ref,
+    right_first_ref,
+    right_second_ref,
     out_ref,
 ):
     order = regroup(STEP)
-    for i, refs in enumerate(
+    for i, (refs, halves) in enumerate(
         (
-            (own_top_ref, left_top_ref, right_top_ref),
-            (own_bottom_ref, left_bottom_ref, right_bottom_ref),
+            ((own_top_ref, right_top_ref), (left_first_ref, left_second_ref)),
+            ((own_bottom_ref, left_bottom_ref), (right_first_ref, right_second_ref)),
         )
     ):
-        total = sum(ref[...].astype(F32) for ref in refs).astype(BF16)
+        total = sum(ref[...].astype(F32) for ref in refs)
+        total += jnp.concatenate([ref[...].astype(F32) for ref in halves], axis=0)
         out_ref[i * STEP : (i + 1) * STEP] = lax.dot_general(
-            order, total, (((0,), (0,)), ((), ())), preferred_element_type=F32
+            order, total.astype(BF16), (((0,), (0,)), ((), ())), preferred_element_type=F32
         ).astype(BF16)
 
 
@@ -400,7 +410,7 @@
     )(*scalars, *staged, *resident)
 
 
-def experts_of(pieces, weights):
+def experts_of(pieces, weights, cuts=1):
     rows = sum(piece.shape[0] for piece in pieces)
     part = pieces[0].shape[1]
     n_blocks = rows // STEP
@@ -408,11 +418,11 @@
     tokens = rows // COLS
 
     def kernel(*refs):
-        expert_kernel(len(pieces), n_blocks, *refs)
+        expert_kernel(len(pieces), n_blocks, cuts, *refs)
 
     return call(
         kernel,
-        tuple(shape_of((STEP, part), BF16) for _ in range(n_blocks)),
+        tuple(shape_of((STEP // cuts, part), BF16) for _ in range(cuts * n_blocks)),
         (),
         (),
         (*pieces, *weights),
@@ -446,11 +456,16 @@
     left_rows_bottom = rotate(bottom, "dp", 1)
     right_rows_top = rotate(top, "dp", -1)
     own_top, own_bottom = experts_of([own], weights)
-    left_rows_top, right_rows_bottom, own_top, own_bottom, beside = lax.optimization_barrier(
-        (left_rows_top, right_rows_bottom, own_top, own_bottom, beside)
-    )
+    one, other, distance = beside
+    left_rows_top, right_rows_bottom, own_top, own_bottom, one, other = lax.optimization_barrier(
+        (left_rows_top, right_rows_bottom, own_top, own_bottom, one, other)
+    )
+    other = rotate(other, "ep", distance)
     far_top = rotate(left_rows_top, "dp", 1)
     far_bottom = rotate(right_rows_bottom, "dp", -1)
+    left_rows_bottom, right_rows_top, other = lax.optimization_barrier(
+        (left_rows_bottom, right_rows_top, other)
+    )
     left_top, left_bottom, right_top, right_bottom = experts_of(
         [left_rows_top, left_rows_bottom, right_rows_top, right_rows_bottom], weights
     )
@@ -459,32 +474,46 @@
     far_top, far_bottom, right_top, left_bottom = lax.optimization_barrier(
         (far_top, far_bottom, right_top, left_bottom)
     )
-    far_terms = experts_of([far_top, far_bottom], weights)
-    relayed_left = rotate(far_terms[0], "dp", 1)
-    relayed_right = rotate(far_terms[1], "dp", -1)
-    block = shape_of(far_top.shape, BF16)
-    size = 2 * block.size
-    to_right, to_left = call(
-        relay_kernel,
-        (block, block),
-        (),
-        (),
-        (right_top, left_bottom, relayed_left, relayed_right),
-        size,
-        5 * size,
-    )
-    sums_left = rotate(to_right, "dp", 1)
-    sums_right = rotate(to_left, "dp", -1)
+    far_terms = experts_of([far_top, far_bottom], weights, cuts=2)
+    size = 2 * right_top.size
+    part = right_top.shape[1]
+    block = shape_of((STEP // 2, part), BF16)
+    sums_left, sums_right = [], []
+    to_right, to_left = direct_left, direct_right
+    for cut in range(2):
+        relayed_left = rotate(far_terms[cut], "dp", 1)
+        relayed_right = rotate(far_terms[2 + cut], "dp", -1)
+        if cut:
+            sums_left.append(rotate(to_right, "dp", 1))
+            sums_right.append(rotate(to_left, "dp", -1))
+        relayed_left, relayed_right, *_ = lax.optimization_barrier(
+            (relayed_left, relayed_right, to_right, to_left)
+        )
+
+        def relay(*refs, cut=cut):
+            relay_kernel(cut, *refs)
+
+        to_right, to_left = call(
+            relay,
+            (block, block),
+            (),
+            (),
+            (right_top, left_bottom, relayed_left, relayed_right),
+            size,
+            5 * size,
+        )
+    sums_left.append(rotate(to_right, "dp", 1))
+    sums_right.append(rotate(to_left, "dp", -1))
     sums = call(
         gather_kernel,
-        shape_of(own.shape, BF16),
-        (),
-        (),
-        (own_top, own_bottom, sums_left, direct_left, direct_right, sums_right),
+        shape_of((2 * STEP, part), BF16),
+        (),
+        (),
+        (own_top, own_bottom, direct_left, direct_right, *sums_left, *sums_right),
         2 * size * STEP,
         8 * size,
     )
-    return sums, beside
+    return sums, one, other
 
 
 def local(
@@ -568,12 +597,13 @@
         3 * 10**6,
     )
     got_cache0 = rotate(cache0, "ep", steps[0])
-    got_cache1 = rotate(cache1, "ep", steps[1])
 
     def settle(*refs):
         settle_kernel(ep_count, *refs)
 
-    sums, got_cache0 = through_experts(rows, (w_gate, w_up, w_down), got_cache0)
+    sums, got_cache0, got_cache1 = through_experts(
+        rows, (w_gate, w_up, w_down), (got_cache0, cache1, steps[1])
+    )
     keys_out, values_out = pl.pallas_call(
         settle,
         out_shape=(cache, cache),

time: 171 us -> 162 us (0.947)
  waiting for transfers between devices: 37.2 us -> 28.3 us
  starting transfers between devices: 31.8 us -> 34.9 us
  blocking collectives: 76.1 us -> 73.6 us
    ppermute x16 -> x20, waiting for transfers between devices: 37.2 us -> 28.3 us  [rotate(): lax.ppermute(member, axis, [(s, (s + distance) % count) for s in range(co...]
    ppermute x16 -> x20, starting transfers between devices: 31.8 us -> 34.9 us  [rotate(): lax.ppermute(member, axis, [(s, (s + distance) % count) for s in range(co...]
    all_to_all x2, blocking collectives: 76.1 us -> 73.6 us  [exchange(): cut = lax.all_to_all(cut, 'ep', split_axis=0, concat_axis=0, tiled=True)]
    pallas_call x10 -> x11, Pallas kernels: 18.5 us -> 18.5 us  [call(): pl.pallas_call(body, out_shape=outs, grid_spec=pltpu.PrefetchScalarGridSp...]
  transfers between devices with their start and end apart: 16 -> 20, of which waited for: 7 -> 8; matrix products, arithmetic and copies ran while one was open for 0% -> 0% of each run, Pallas kernels for 6% -> 8%
where the time goes in v5:
time: 162 us
  blocking collectives  73.6 us (45%)
  starting transfers between devices  34.9 us (22%)
  waiting for transfers between devices  28.3 us (17%)
  Pallas kernels  19.7 us (12%)
  local copies, waits for them, and re-layouts  4.88 us (3%)
    all_to_all x2, blocking collectives, exchange(): cut = lax.all_to_all(cut, 'ep', split_axis=0, concat_axis=0, tiled=True)  73.6 us
    ppermute x20, starting transfers between devices, rotate(): lax.ppermute(member, axis, [(s, (s + distance) % count) for s in range(co...  34.9 us
    ppermute x20, waiting for transfers between devices, rotate(): lax.ppermute(member, axis, [(s, (s + distance) % count) for s in range(co...  28.3 us
    pallas_call x11, Pallas kernels, call(): pl.pallas_call(body, out_shape=outs, grid_spec=pltpu.PrefetchScalarGridSp...  18.5 us
    unnamed x24, local copies, waits for them, and re-layouts  4.81 us
  transfers between devices with their start and end apart: 20, of which 8 were waited for; matrix products, arithmetic and copies ran while one was open for 0% of the time, Pallas kernels for 8%

profile of v5, /device:TPU:1, one launch (start us, length us, event | category | flops | bytes accessed | tf_op | source)
XLA Modules:
  0.0 162.2 jit_solution(12536281795029572651)
XLA Ops:
  0.6 0.0 copy-start.3
  0.7 3.6 %shard_map.157 = (f32[24,4096]{1,0:T(8,128)}, f32[1,4096]{1,0:T(1,128)}, f32[1,4096]{1,0:T(1,128)}) custom-call(s32[8]{0:T(128)} %refs_0_.4, s32[2,8]{1,0:T(2,128)} %bitcast.12, bf16[8,4096]{1,0:T(8,128)(2,1)} %refs_2_.3, bf16[8,64,256]{2,1,0:T(8,128)(2,1)} %refs_2_.5, bf16[8,256]{1,0:T(8,128)(2,1)} %refs_4_.5, bf16[8,64,256]{2,1,0:T(8,128)(2,1)} %refs_3_.6, ...), custom_call_target="tpu_custom_call" | custom-call | flops 100000000 | bytes 3000000 | tf_op jit(solution)/shard_map/pallas_call | solution.py:398
  4.3 2.7 %collective-permute-start = (f32[1,4096]{1,0:T(1,128)}, f32[1,4096]{1,0:T(1,128)S(1)}, u32[]{:S(2)}, u32[]{:S(2)}) collective-permute-start(f32[1,4096]{1,0:T(1,128)} %get-tuple-element.51), channel_id=1, source_target_pairs={{0,1},{1,2},{2,3},{3,4},{4,5},{5,6},{6,7},{7,8},{8,9},{9,10},{10,1... | collective-permute-start | bytes 49160 | tf_op jit(solution)/shard_map/ppermute | solution.py:438
  6.9 6.9 %collective-permute-start.1 = (f32[1,4096]{1,0:T(1,128)}, f32[1,4096]{1,0:T(1,128)S(1)}, u32[]{:S(2)}, u32[]{:S(2)}) collective-permute-start(f32[1,4096]{1,0:T(1,128)} %get-tuple-element.52), channel_id=1, source_target_pairs={{0,32},{1,33},{2,34},{3,35},{4,36},{5,37},{6,38},{7,39},{8,40},{9,... | collective-permute-start | bytes 49160 | tf_op jit(solution)/shard_map/ppermute | solution.py:438
  13.8 0.0 collective-permute-done.refs_1_
  13.9 1.3 collective-permute-done.1.refs_2_
  15.2 1.0 copy-done.5
  16.2 0.7 shard_map.158
  16.9 37.9 %all_to_all.10 = bf16[64,16,512]{2,1,0:T(8,128)(2,1)S(1)} all-to-all(bf16[64,16,512]{2,1,0:T(8,128)(2,1)S(1)} %bitcast.11), channel_id=1, replica_groups=mesh['dp'=4,'ep'=64] {'ep'}, dimensions={0} | all-to-all | bytes 2097152 | tf_op jit(solution)/shard_map/all_to_all | solution.py:444
  54.9 0.1 fusion
  54.9 1.4 collective-permute-start.2
  56.3 1.5 collective-permute-start.3
  57.8 0.0 collective-permute-start.5
  57.9 2.7 %collective-permute-start.6 = (bf16[512,512]{1,0:T(8,128)(2,1)S(1)}, bf16[512,512]{1,0:T(8,128)(2,1)S(1)}, u32[]{:S(2)}, u32[]{:S(2)}) collective-permute-start(bf16[512,512]{1,0:T(8,128)(2,1)S(1)} %bitcast.16), channel_id=1, source_target_pairs={{0,192},{64,0},{128,64},{192,128},{1,193},{65,1},{129,65},{193,129... | collective-permute-start | bytes 1572872 | tf_op jit(solution)/shard_map/ppermute | solution.py:438
  60.5 0.0 copy-done.3
  60.5 0.0 copy-done.6
  60.6 1.5 shard_map.161
  62.1 3.5 %collective-permute-start.4 = (bf16[128,256]{1,0:T(8,128)(2,1)S(1)}, bf16[128,256]{1,0:T(8,128)(2,1)S(1)}, u32[]{:S(2)}, u32[]{:S(2)}) collective-permute-start(bf16[128,256]{1,0:T(8,128)(2,1)S(1)} %get-tuple-element.61), channel_id=1, source_target_pairs={{0,1},{1,2},{2,3},{3,4},{4,5},{5,6},{6,7},{7,8},{8,9},{9,10},{10,1... | collective-permute-start | bytes 196616 | tf_op jit(solution)/shard_map/ppermute | solution.py:438
  65.6 1.9 %copy-done.1 = bf16[1,4096,384]{2,1,0:T(8,128)(2,1)S(1)} copy-done((bf16[1,4096,384]{2,1,0:T(8,128)(2,1)S(1)}, bf16[1,4096,384]{2,1,0:T(8,128)(2,1)}, u32[]{:S(2)}) %copy-start.1) | copy-done | bytes 3145752
  67.5 1.9 %copy-done.2 = bf16[1,384,4096]{2,1,0:T(8,128)(2,1)S(1)} copy-done((bf16[1,384,4096]{2,1,0:T(8,128)(2,1)S(1)}, bf16[1,384,4096]{2,1,0:T(8,128)(2,1)}, u32[]{:S(2)}) %copy-start.2) | copy-done | bytes 3145752
  69.3 2.5 %shard_map.160 = (bf16[512,512]{1,0:T(8,128)(2,1)S(1)}, bf16[512,512]{1,0:T(8,128)(2,1)S(1)}) custom-call(bf16[1024,512]{1,0:T(8,128)(2,1)S(1)} %bitcast.8, bf16[1,4096,384]{2,1,0:T(8,128)(2,1)S(1)} %copy-done, bf16[1,4096,384]{2,1,0:T(8,128)(2,1)S(1)} %copy-done.1, bf16[1,384,4096]{2,1,0:T(8,128)(2,1)S(1)} %copy-done.2), custom_call_target="tpu_custom_call" | custom-call | flops 1207959552 | bytes 11534336 | tf_op jit(solution)/shard_map/pallas_call | solution.py:398
  71.8 0.0 collective-permute-done.4.refs_1_
  71.8 0.0 collective-permute-done.2.refs_0_
  71.8 0.0 collective-permute-done.3.refs_3_
  71.8 0.9 collective-permute-start.7
  72.8 0.0 collective-permute-start.10
  72.8 2.7 %collective-permute-start.11 = (bf16[512,512]{1,0:T(8,128)(2,1)S(1)}, bf16[512,512]{1,0:T(8,128)(2,1)S(1)}, u32[]{:S(2)}, u32[]{:S(2)}) collective-permute-start(bf16[512,512]{1,0:T(8,128)(2,1)S(1)} %collective-permute-done.3.refs_3_), channel_id=1, source_target_pairs={{0,192},{64,0},{128,64},{192,128},{1,193},{65,1},{129,65},{193,129... | collective-permute-start | bytes 1572872 | tf_op jit(solution)/shard_map/ppermute | solution.py:438
  75.5 4.2 %collective-permute-done.5.refs_1_ = bf16[512,512]{1,0:T(8,128)(2,1)S(1)} collective-permute-done((bf16[512,512]{1,0:T(8,128)(2,1)S(1)}, bf16[512,512]{1,0:T(8,128)(2,1)S(1)}, u32[]{:S(2)}, u32[]{:S(2)}) %collective-permute-start.5) | collective-permute-done | bytes 524320 | tf_op jit(solution)/shard_map/ppermute | solution.py:438
  79.7 0.0 collective-permute-done.6.refs_2_
  79.7 0.0 collective-permute-done.7.refs_2_
  79.7 4.6 %shard_map.162 = (bf16[512,512]{1,0:T(8,128)(2,1)S(1)}, bf16[512,512]{1,0:T(8,128)(2,1)S(1)}, bf16[512,512]{1,0:T(8,128)(2,1)S(1)}, bf16[512,512]{1,0:T(8,128)(2,1)S(1)}) custom-call(bf16[512,512]{1,0:T(8,128)(2,1)S(1)} %collective-permute-done.2.refs_0_, bf16[512,512]{1,0:T(8,128)(2,1)S(1)} %collective-permute-done.5.refs_1_, ...), custom_call_target="tpu_custom_call" | custom-call | flops 2415919104 | bytes 13631488 | tf_op jit(solution)/shard_map/pallas_call | solution.py:398
  84.3 1.1 collective-permute-start.8
  85.3 1.7 %collective-permute-start.9 = (bf16[512,512]{1,0:T(8,128)(2,1)S(1)}, bf16[512,512]{1,0:T(8,128)(2,1)S(1)}, u32[]{:S(2)}, u32[]{:S(2)}) collective-permute-start(bf16[512,512]{1,0:T(8,128)(2,1)S(1)} %get-tuple-element.71), channel_id=1, source_target_pairs={{0,192},{64,0},{128,64},{192,128},{1,193},{65,1},{129,65},{193,129... | collective-permute-start | bytes 1572872 | tf_op jit(solution)/shard_map/ppermute | solution.py:438
  87.0 3.9 %collective-permute-done.10.refs_0_ = bf16[512,512]{1,0:T(8,128)(2,1)S(1)} collective-permute-done((bf16[512,512]{1,0:T(8,128)(2,1)S(1)}, bf16[512,512]{1,0:T(8,128)(2,1)S(1)}, u32[]{:S(2)}, u32[]{:S(2)}) %collective-permute-start.10) | collective-permute-done | bytes 524320 | tf_op jit(solution)/shard_map/ppermute | solution.py:438
  90.9 0.0 collective-permute-done.11.refs_1_
  90.9 2.5 %shard_map.163 = (bf16[256,512]{1,0:T(8,128)(2,1)S(1)}, bf16[256,512]{1,0:T(8,128)(2,1)S(1)}, bf16[256,512]{1,0:T(8,128)(2,1)S(1)}, bf16[256,512]{1,0:T(8,128)(2,1)S(1)}) custom-call(bf16[512,512]{1,0:T(8,128)(2,1)S(1)} %collective-permute-done.10.refs_0_, bf16[512,512]{1,0:T(8,128)(2,1)S(1)} %collective-permute-done.11.refs_1_, ...), custom_call_target="tpu_custom_call" | custom-call | flops 1207959552 | bytes 11534336 | tf_op jit(solution)/shard_map/pallas_call | solution.py:398
  93.4 0.0 copy-start.9
  93.4 0.0 copy-start.11
  93.4 1.1 collective-permute-start.12
  94.4 1.7 %collective-permute-start.13 = (bf16[256,512]{1,0:T(8,128)(2,1)S(1)}, bf16[256,512]{1,0:T(8,128)(2,1)S(1)}, u32[]{:S(2)}, u32[]{:S(2)}) collective-permute-start(bf16[256,512]{1,0:T(8,128)(2,1)S(1)} %get-tuple-element.79), channel_id=1, source_target_pairs={{0,192},{64,0},{128,64},{192,128},{1,193},{65,1},{129,65},{193,129... | collective-permute-start | bytes 786440 | tf_op jit(solution)/shard_map/ppermute | solution.py:438
  96.1 0.0 collective-permute-start.15
  96.1 6.0 %collective-permute-done.8.refs_2_ = bf16[512,512]{1,0:T(8,128)(2,1)S(1)} collective-permute-done((bf16[512,512]{1,0:T(8,128)(2,1)S(1)}, bf16[512,512]{1,0:T(8,128)(2,1)S(1)}, u32[]{:S(2)}, u32[]{:S(2)}) %collective-permute-start.8) | collective-permute-done | bytes 524320 | tf_op jit(solution)/shard_map/ppermute | solution.py:438
  102.1 1.4 collective-permute-start.16
  103.5 0.0 collective-permute-done.9.refs_3_
  103.5 4.2 %collective-permute-done.12.refs_2_ = bf16[256,512]{1,0:T(8,128)(2,1)S(1)} collective-permute-done((bf16[256,512]{1,0:T(8,128)(2,1)S(1)}, bf16[256,512]{1,0:T(8,128)(2,1)S(1)}, u32[]{:S(2)}, u32[]{:S(2)}) %collective-permute-start.12) | collective-permute-done | bytes 262176 | tf_op jit(solution)/shard_map/ppermute | solution.py:438
  107.7 0.0 collective-permute-done.13.refs_3_
  107.7 0.1 shard_map.164
  107.9 1.1 collective-permute-start.14
  108.9 1.9 %collective-permute-start.18 = (bf16[256,512]{1,0:T(8,128)(2,1)S(1)}, bf16[256,512]{1,0:T(8,128)(2,1)S(1)}, u32[]{:S(2)}, u32[]{:S(2)}) collective-permute-start(bf16[256,512]{1,0:T(8,128)(2,1)S(1)} %get-tuple-element.85), channel_id=1, source_target_pairs={{0,192},{64,0},{128,64},{192,128},{1,193},{65,1},{129,65},{193,129... | collective-permute-start | bytes 786440 | tf_op jit(solution)/shard_map/ppermute | solution.py:438
  110.8 2.5 %collective-permute-done.15.refs_2_ = bf16[256,512]{1,0:T(8,128)(2,1)S(1)} collective-permute-done((bf16[256,512]{1,0:T(8,128)(2,1)S(1)}, bf16[256,512]{1,0:T(8,128)(2,1)S(1)}, u32[]{:S(2)}, u32[]{:S(2)}) %collective-permute-start.15) | collective-permute-done | bytes 262176 | tf_op jit(solution)/shard_map/ppermute | solution.py:438
  113.4 0.0 collective-permute-done.16.refs_3_
  113.4 0.1 shard_map.165
  113.5 1.1 collective-permute-start.17
  114.5 1.7 %collective-permute-start.19 = (bf16[256,512]{1,0:T(8,128)(2,1)S(1)}, bf16[256,512]{1,0:T(8,128)(2,1)S(1)}, u32[]{:S(2)}, u32[]{:S(2)}) collective-permute-start(bf16[256,512]{1,0:T(8,128)(2,1)S(1)} %get-tuple-element.89), channel_id=1, source_target_pairs={{0,192},{64,0},{128,64},{192,128},{1,193},{65,1},{129,65},{193,129... | collective-permute-start | bytes 786440 | tf_op jit(solution)/shard_map/ppermute | solution.py:438
  116.2 0.0 copy-done.9
  116.2 0.9 shard_map.159
  117.1 1.3 shard_map.167
  118.4 0.6 collective-permute-done.14.refs_4_
  119.0 5.6 %collective-permute-done.17.refs_5_ = bf16[256,512]{1,0:T(8,128)(2,1)S(1)} collective-permute-done((bf16[256,512]{1,0:T(8,128)(2,1)S(1)}, bf16[256,512]{1,0:T(8,128)(2,1)S(1)}, u32[]{:S(2)}, u32[]{:S(2)}) %collective-permute-start.17) | collective-permute-done | bytes 262176 | tf_op jit(solution)/shard_map/ppermute | solution.py:438
  124.6 0.0 collective-permute-done.18.refs_6_
  124.6 0.0 collective-permute-done.19.refs_7_
  124.6 0.9 shard_map.166
  125.5 35.6 %all_to_all.11 = bf16[64,16,512]{2,1,0:T(8,128)(2,1)S(1)} all-to-all(bf16[64,16,512]{2,1,0:T(8,128)(2,1)S(1)} %bitcast.10), channel_id=1, replica_groups=mesh['dp'=4,'ep'=64] {'ep'}, dimensions={0} | all-to-all | bytes 2097152 | tf_op jit(solution)/shard_map/all_to_all | solution.py:444
  161.1 1.1 shard_map.168
  (15 shorter events, 0.0 us)
Async XLA Ops:
  0.6 59.9 %copy-start.3 = (bf16[8,64,256]{2,1,0:T(8,128)(2,1)S(1)}, bf16[8,64,256]{2,1,0:T(8,128)(2,1)}, u32[]{:S(2)}) copy-start(bf16[8,64,256]{2,1,0:T(8,128)(2,1)} %refs_2_.5) | copy-start | bytes 786436
  0.6 59.9 %copy-start.4 = (bf16[8,64,256]{2,1,0:T(8,128)(2,1)S(1)}, bf16[8,64,256]{2,1,0:T(8,128)(2,1)}, u32[]{:S(2)}) copy-start(bf16[8,64,256]{2,1,0:T(8,128)(2,1)} %refs_3_.6) | copy-start | bytes 786436
  0.7 64.9 %copy-start = (bf16[1,4096,384]{2,1,0:T(8,128)(2,1)S(1)}, bf16[1,4096,384]{2,1,0:T(8,128)(2,1)}, u32[]{:S(2)}) copy-start(bf16[1,4096,384]{2,1,0:T(8,128)(2,1)} %refs_2_.6) | copy-start | bytes 9437188
  4.3 9.6 %collective-permute-start = (f32[1,4096]{1,0:T(1,128)}, f32[1,4096]{1,0:T(1,128)S(1)}, u32[]{:S(2)}, u32[]{:S(2)}) collective-permute-start(f32[1,4096]{1,0:T(1,128)} %get-tuple-element.51), channel_id=1, source_target_pairs={{0,1},{1,2},{2,3},{3,4},{4,5},{5,6},{6,7},{7,8},{8,9},{9,10},{10,1... | collective-permute-start | bytes 49160 | tf_op jit(solution)/shard_map/ppermute | solution.py:438
  6.9 8.2 %collective-permute-start.1 = (f32[1,4096]{1,0:T(1,128)}, f32[1,4096]{1,0:T(1,128)S(1)}, u32[]{:S(2)}, u32[]{:S(2)}) collective-permute-start(f32[1,4096]{1,0:T(1,128)} %get-tuple-element.52), channel_id=1, source_target_pairs={{0,32},{1,33},{2,34},{3,35},{4,36},{5,37},{6,38},{7,39},{8,40},{9,... | collective-permute-start | bytes 49160 | tf_op jit(solution)/shard_map/ppermute | solution.py:438
  15.2 1.0 copy-start.5
  16.2 44.4 %copy-start.6 = (bf16[8,256]{1,0:T(8,128)(2,1)S(1)}, bf16[8,256]{1,0:T(8,128)(2,1)}, u32[]{:S(2)}) copy-start(bf16[8,256]{1,0:T(8,128)(2,1)} %refs_4_.5) | copy-start | bytes 12292
  16.2 44.4 %copy-start.7 = (bf16[8,256]{1,0:T(8,128)(2,1)S(1)}, bf16[8,256]{1,0:T(8,128)(2,1)}, u32[]{:S(2)}) copy-start(bf16[8,256]{1,0:T(8,128)(2,1)} %refs_5_.4) | copy-start | bytes 12292
  16.2 44.4 %copy-start.8 = (s32[8,2]{0,1:T(2,128)S(1)}, s32[8,2]{0,1:T(2,128)}, u32[]{:S(2)}) copy-start(s32[8,2]{0,1:T(2,128)} %param.21) | copy-start | bytes 196
  16.2 44.4 %copy-start.10 = (s32[8]{0:T(128)S(1)}, s32[8]{0:T(128)}, u32[]{:S(2)}) copy-start(s32[8]{0:T(128)} %refs_0_.4) | copy-start | bytes 100
  54.9 16.9 %collective-permute-start.2 = (bf16[512,512]{1,0:T(8,128)(2,1)S(1)}, bf16[512,512]{1,0:T(8,128)(2,1)S(1)}, u32[]{:S(2)}, u32[]{:S(2)}) collective-permute-start(bf16[512,512]{1,0:T(8,128)(2,1)S(1)} %bitcast.15), channel_id=1, source_target_pairs={{0,64},{64,128},{128,192},{192,0},{1,65},{65,129},{129,193},{193,1... | collective-permute-start | bytes 1572872 | tf_op jit(solution)/shard_map/ppermute | solution.py:438
  56.3 15.5 %collective-permute-start.3 = (bf16[512,512]{1,0:T(8,128)(2,1)S(1)}, bf16[512,512]{1,0:T(8,128)(2,1)S(1)}, u32[]{:S(2)}, u32[]{:S(2)}) collective-permute-start(bf16[512,512]{1,0:T(8,128)(2,1)S(1)} %bitcast.17), channel_id=1, source_target_pairs={{0,192},{64,0},{128,64},{192,128},{1,193},{65,1},{129,65},{193,129... | collective-permute-start | bytes 1572872 | tf_op jit(solution)/shard_map/ppermute | solution.py:438
  57.8 21.8 %collective-permute-start.5 = (bf16[512,512]{1,0:T(8,128)(2,1)S(1)}, bf16[512,512]{1,0:T(8,128)(2,1)S(1)}, u32[]{:S(2)}, u32[]{:S(2)}) collective-permute-start(bf16[512,512]{1,0:T(8,128)(2,1)S(1)} %bitcast.18), channel_id=1, source_target_pairs={{0,64},{64,128},{128,192},{192,0},{1,65},{65,129},{129,193},{193,1... | collective-permute-start | bytes 1572872 | tf_op jit(solution)/shard_map/ppermute | solution.py:438
  57.9 21.8 %collective-permute-start.6 = (bf16[512,512]{1,0:T(8,128)(2,1)S(1)}, bf16[512,512]{1,0:T(8,128)(2,1)S(1)}, u32[]{:S(2)}, u32[]{:S(2)}) collective-permute-start(bf16[512,512]{1,0:T(8,128)(2,1)S(1)} %bitcast.16), channel_id=1, source_target_pairs={{0,192},{64,0},{128,64},{192,128},{1,193},{65,1},{129,65},{193,129... | collective-permute-start | bytes 1572872 | tf_op jit(solution)/shard_map/ppermute | solution.py:438
  62.1 9.7 %collective-permute-start.4 = (bf16[128,256]{1,0:T(8,128)(2,1)S(1)}, bf16[128,256]{1,0:T(8,128)(2,1)S(1)}, u32[]{:S(2)}, u32[]{:S(2)}) collective-permute-start(bf16[128,256]{1,0:T(8,128)(2,1)S(1)} %get-tuple-element.61), channel_id=1, source_target_pairs={{0,1},{1,2},{2,3},{3,4},{4,5},{5,6},{6,7},{7,8},{8,9},{9,10},{10,1... | collective-permute-start | bytes 196616 | tf_op jit(solution)/shard_map/ppermute | solution.py:438
  65.6 1.9 %copy-start.1 = (bf16[1,4096,384]{2,1,0:T(8,128)(2,1)S(1)}, bf16[1,4096,384]{2,1,0:T(8,128)(2,1)}, u32[]{:S(2)}) copy-start(bf16[1,4096,384]{2,1,0:T(8,128)(2,1)} %refs_3_.7) | copy-start | bytes 9437188
  67.5 1.9 %copy-start.2 = (bf16[1,384,4096]{2,1,0:T(8,128)(2,1)S(1)}, bf16[1,384,4096]{2,1,0:T(8,128)(2,1)}, u32[]{:S(2)}) copy-start(bf16[1,384,4096]{2,1,0:T(8,128)(2,1)} %refs_4_.7) | copy-start | bytes 9437188
  71.8 7.8 %collective-permute-start.7 = (bf16[128,256]{1,0:T(8,128)(2,1)S(1)}, bf16[128,256]{1,0:T(8,128)(2,1)S(1)}, u32[]{:S(2)}, u32[]{:S(2)}) collective-permute-start(bf16[128,256]{1,0:T(8,128)(2,1)S(1)} %get-tuple-element.66), channel_id=1, source_target_pairs={{0,32},{1,33},{2,34},{3,35},{4,36},{5,37},{6,38},{7,39},{8,40},{9,... | collective-permute-start | bytes 196616 | tf_op jit(solution)/shard_map/ppermute | solution.py:438
  72.8 18.1 %collective-permute-start.10 = (bf16[512,512]{1,0:T(8,128)(2,1)S(1)}, bf16[512,512]{1,0:T(8,128)(2,1)S(1)}, u32[]{:S(2)}, u32[]{:S(2)}) collective-permute-start(bf16[512,512]{1,0:T(8,128)(2,1)S(1)} %collective-permute-done.2.refs_0_), channel_id=1, source_target_pairs={{0,64},{64,128},{128,192},{192,0},{1,65},{65,129},{129,193},{193,1... | collective-permute-start | bytes 1572872 | tf_op jit(solution)/shard_map/ppermute | solution.py:438
  72.8 18.1 %collective-permute-start.11 = (bf16[512,512]{1,0:T(8,128)(2,1)S(1)}, bf16[512,512]{1,0:T(8,128)(2,1)S(1)}, u32[]{:S(2)}, u32[]{:S(2)}) collective-permute-start(bf16[512,512]{1,0:T(8,128)(2,1)S(1)} %collective-permute-done.3.refs_3_), channel_id=1, source_target_pairs={{0,192},{64,0},{128,64},{192,128},{1,193},{65,1},{129,65},{193,129... | collective-permute-start | bytes 1572872 | tf_op jit(solution)/shard_map/ppermute | solution.py:438
  84.3 17.8 %collective-permute-start.8 = (bf16[512,512]{1,0:T(8,128)(2,1)S(1)}, bf16[512,512]{1,0:T(8,128)(2,1)S(1)}, u32[]{:S(2)}, u32[]{:S(2)}) collective-permute-start(bf16[512,512]{1,0:T(8,128)(2,1)S(1)} %get-tuple-element.70), channel_id=1, source_target_pairs={{0,64},{64,128},{128,192},{192,0},{1,65},{65,129},{129,193},{193,1... | collective-permute-start | bytes 1572872 | tf_op jit(solution)/shard_map/ppermute | solution.py:438
  85.3 18.2 %collective-permute-start.9 = (bf16[512,512]{1,0:T(8,128)(2,1)S(1)}, bf16[512,512]{1,0:T(8,128)(2,1)S(1)}, u32[]{:S(2)}, u32[]{:S(2)}) collective-permute-start(bf16[512,512]{1,0:T(8,128)(2,1)S(1)} %get-tuple-element.71), channel_id=1, source_target_pairs={{0,192},{64,0},{128,64},{192,128},{1,193},{65,1},{129,65},{193,129... | collective-permute-start | bytes 1572872 | tf_op jit(solution)/shard_map/ppermute | solution.py:438
  93.4 22.9 %copy-start.9 = (s32[8,8]{1,0:T(8,128)S(1)}, s32[8,8]{1,0:T(8,128)}, u32[]{:S(2)}) copy-start(s32[8,8]{1,0:T(8,128)} %refs_0_.3) | copy-start | bytes 772
  93.4 22.9 %copy-start.11 = (f32[8,8]{1,0:T(8,128)S(1)}, f32[8,8]{1,0:T(8,128)}, u32[]{:S(2)}) copy-start(f32[8,8]{1,0:T(8,128)} %refs_1_.2) | copy-start | bytes 772
  93.4 14.4 %collective-permute-start.12 = (bf16[256,512]{1,0:T(8,128)(2,1)S(1)}, bf16[256,512]{1,0:T(8,128)(2,1)S(1)}, u32[]{:S(2)}, u32[]{:S(2)}) collective-permute-start(bf16[256,512]{1,0:T(8,128)(2,1)S(1)} %get-tuple-element.78), channel_id=1, source_target_pairs={{0,64},{64,128},{128,192},{192,0},{1,65},{65,129},{129,193},{193,1... | collective-permute-start | bytes 786440 | tf_op jit(solution)/shard_map/ppermute | solution.py:438
  94.4 13.3 %collective-permute-start.13 = (bf16[256,512]{1,0:T(8,128)(2,1)S(1)}, bf16[256,512]{1,0:T(8,128)(2,1)S(1)}, u32[]{:S(2)}, u32[]{:S(2)}) collective-permute-start(bf16[256,512]{1,0:T(8,128)(2,1)S(1)} %get-tuple-element.79), channel_id=1, source_target_pairs={{0,192},{64,0},{128,64},{192,128},{1,193},{65,1},{129,65},{193,129... | collective-permute-start | bytes 786440 | tf_op jit(solution)/shard_map/ppermute | solution.py:438
  96.1 17.2 %collective-permute-start.15 = (bf16[256,512]{1,0:T(8,128)(2,1)S(1)}, bf16[256,512]{1,0:T(8,128)(2,1)S(1)}, u32[]{:S(2)}, u32[]{:S(2)}) collective-permute-start(bf16[256,512]{1,0:T(8,128)(2,1)S(1)} %get-tuple-element.83), channel_id=1, source_target_pairs={{0,64},{64,128},{128,192},{192,0},{1,65},{65,129},{129,193},{193,1... | collective-permute-start | bytes 786440 | tf_op jit(solution)/shard_map/ppermute | solution.py:438
  102.1 11.2 %collective-permute-start.16 = (bf16[256,512]{1,0:T(8,128)(2,1)S(1)}, bf16[256,512]{1,0:T(8,128)(2,1)S(1)}, u32[]{:S(2)}, u32[]{:S(2)}) collective-permute-start(bf16[256,512]{1,0:T(8,128)(2,1)S(1)} %get-tuple-element.84), channel_id=1, source_target_pairs={{0,192},{64,0},{128,64},{192,128},{1,193},{65,1},{129,65},{193,129... | collective-permute-start | bytes 786440 | tf_op jit(solution)/shard_map/ppermute | solution.py:438
  107.9 11.1 %collective-permute-start.14 = (bf16[256,512]{1,0:T(8,128)(2,1)S(1)}, bf16[256,512]{1,0:T(8,128)(2,1)S(1)}, u32[]{:S(2)}, u32[]{:S(2)}) collective-permute-start(bf16[256,512]{1,0:T(8,128)(2,1)S(1)} %get-tuple-element.82), channel_id=1, source_target_pairs={{0,64},{64,128},{128,192},{192,0},{1,65},{65,129},{129,193},{193,1... | collective-permute-start | bytes 786440 | tf_op jit(solution)/shard_map/ppermute | solution.py:438
  108.9 15.7 %collective-permute-start.18 = (bf16[256,512]{1,0:T(8,128)(2,1)S(1)}, bf16[256,512]{1,0:T(8,128)(2,1)S(1)}, u32[]{:S(2)}, u32[]{:S(2)}) collective-permute-start(bf16[256,512]{1,0:T(8,128)(2,1)S(1)} %get-tuple-element.85), channel_id=1, source_target_pairs={{0,192},{64,0},{128,64},{192,128},{1,193},{65,1},{129,65},{193,129... | collective-permute-start | bytes 786440 | tf_op jit(solution)/shard_map/ppermute | solution.py:438
  113.5 11.1 %collective-permute-start.17 = (bf16[256,512]{1,0:T(8,128)(2,1)S(1)}, bf16[256,512]{1,0:T(8,128)(2,1)S(1)}, u32[]{:S(2)}, u32[]{:S(2)}) collective-permute-start(bf16[256,512]{1,0:T(8,128)(2,1)S(1)} %get-tuple-element.88), channel_id=1, source_target_pairs={{0,64},{64,128},{128,192},{192,0},{1,65},{65,129},{129,193},{193,1... | collective-permute-start | bytes 786440 | tf_op jit(solution)/shard_map/ppermute | solution.py:438
  114.5 10.1 %collective-permute-start.19 = (bf16[256,512]{1,0:T(8,128)(2,1)S(1)}, bf16[256,512]{1,0:T(8,128)(2,1)S(1)}, u32[]{:S(2)}, u32[]{:S(2)}) collective-permute-start(bf16[256,512]{1,0:T(8,128)(2,1)S(1)} %get-tuple-element.89), channel_id=1, source_target_pairs={{0,192},{64,0},{128,64},{192,128},{1,193},{65,1},{129,65},{193,129... | collective-permute-start | bytes 786440 | tf_op jit(solution)/shard_map/ppermute | solution.py:438

commit v6 on v5

--- a/solution.py
+++ b/solution.py
@@ -137,24 +137,30 @@
         )
         for h in range(groups):
             place = slice((k * groups + h) * HD, (k * groups + h + 1) * HD)
-            carry_ref[0:requests, place] = (
+            carry_ref[:, place] = (
                 residual[:, place] + attended[h * requests : (h + 1) * requests]
             )
     rank = lax.axis_index("ep")
-    summed = carry_ref[0:requests]
+    summed = carry_ref[:, : heads * HD]
+    notes = heads * HD + heads * HD // COLS
     row_number = iota(summed.shape, 0)
     for d, (distance, row_ref) in enumerate(zip(distances(ep_count), (row0_ref, row1_ref))):
         slot = find_slot(plan_ref, 1, lax.rem(rank + distance, ep_count), requests, ep_count)
         row_ref[...] = jnp.sum(jnp.where(row_number == slot, summed, 0.0), axis=0, keepdims=True)
         origin = lax.rem(rank + ep_count - distance, ep_count)
         arrival = find_slot(plan_ref, 0, origin, requests, ep_count)
-        carry_ref[2 * requests : 3 * requests, (2 + d) * HD : (3 + d) * HD] = jnp.where(
+        carry_ref[:, notes + (2 + d) * HD : notes + (3 + d) * HD] = jnp.where(
             iota((requests, HD), 0) == arrival, 1.0, 0.0
         )
-    carry_ref[requests : 2 * requests] = jnp.broadcast_to(gain_ref[...], summed.shape)
+    gain = gain_ref[...]
+    part = heads * HD // COLS
+    carry_ref[:, heads * HD : notes] = jnp.concatenate(
+        [gain[:, c * part : (c + 1) * part] for c in range(COLS)], axis=0
+    )
     chosen, _, earlier = routes(ids_ref[...], None, ep_count)
-    carry_ref[2 * requests : 3 * requests, 0:ep_count] = chosen
-    carry_ref[2 * requests : 3 * requests, HD : HD + ep_count] = earlier
+    blank = jnp.zeros((requests, HD - ep_count), F32)
+    carry_ref[:, notes : notes + HD] = jnp.concatenate([chosen, blank], axis=1)
+    carry_ref[:, notes + HD : notes + 2 * HD] = jnp.concatenate([earlier, blank], axis=1)
 
 
 def routes(ids, gates, experts):
@@ -177,20 +183,21 @@
 
 def place_kernel(ep_count, carry_ref, row0_ref, row1_ref, summed_out_ref, slots_ref):
     rows, model_width = summed_out_ref.shape
-    summed = carry_ref[0:rows]
-    notes = slice(2 * rows, 3 * rows)
+    summed = carry_ref[:, :model_width]
+    part = model_width // COLS
+    notes = model_width + part
     for d, row_ref in enumerate((row0_ref, row1_ref)):
-        arrival = carry_ref[notes, (2 + d) * HD : (2 + d) * HD + 1]
+        arrival = carry_ref[:, notes + (2 + d) * HD : notes + (3 + d) * HD][:, 0:1]
         summed = jnp.where(arrival > 0.5, row_ref[...], summed)
     summed_out_ref[...] = summed
     scale = lax.rsqrt(jnp.mean(summed * summed, axis=1, keepdims=True) + 1e-06)
-    normed = summed * scale * carry_ref[rows : 2 * rows]
-    part = model_width // COLS
+    scaled = summed * scale
+    gain = carry_ref[:, model_width:notes]
     pieces = jnp.concatenate(
-        [normed[:, c * part : (c + 1) * part] for c in range(COLS)], axis=0
+        [scaled[:, c * part : (c + 1) * part] * gain[c : c + 1] for c in range(COLS)], axis=0
     ).astype(BF16)
-    chosen = carry_ref[notes, 0:ep_count]
-    earlier = carry_ref[notes, HD : HD + ep_count]
+    chosen = carry_ref[:, notes : notes + HD][:, :ep_count]
+    earlier = carry_ref[:, notes + HD : notes + 2 * HD][:, :ep_count]
     deep = MOST * COLS
     wide = (ep_count * deep, ep_count)
     spread = one_hot(lax.div(iota(wide, 0), deep) == iota(wide, 1))
@@ -547,7 +554,7 @@
 
     carry, row0, row1 = call(
         attend,
-        (shape_of((3 * requests, model_width), F32), row, row),
+        (shape_of((requests, model_width + model_width // COLS + 4 * HD), F32), row, row),
         (cache_lengths, plan),
         (
             queries,

time: 162 us -> 162 us (level)
  no operation moved by 1% of the time
where the time goes in v6:
time: 162 us
  blocking collectives  73.6 us (45%)
  starting transfers between devices  34.9 us (22%)
  waiting for transfers between devices  28.4 us (18%)
  Pallas kernels  19.7 us (12%)
  local copies, waits for them, and re-layouts  4.81 us (3%)
    all_to_all x2, blocking collectives, exchange(): cut = lax.all_to_all(cut, 'ep', split_axis=0, concat_axis=0, tiled=True)  73.6 us
    ppermute x20, starting transfers between devices, rotate(): lax.ppermute(member, axis, [(s, (s + distance) % count) for s in range(co...  34.9 us
    ppermute x20, waiting for transfers between devices, rotate(): lax.ppermute(member, axis, [(s, (s + distance) % count) for s in range(co...  28.4 us
    pallas_call x11, Pallas kernels, call(): pl.pallas_call(body, out_shape=outs, grid_spec=pltpu.PrefetchScalarGridSp...  18.4 us
    unnamed x24, local copies, waits for them, and re-layouts  4.74 us
  transfers between devices with their start and end apart: 20, of which 8 were waited for; matrix products, arithmetic and copies ran while one was open for 0% of the time, Pallas kernels for 8%

profile of v6, /device:TPU:1, one launch (start us, length us, event | category | flops | bytes accessed | tf_op | source)
XLA Modules:
  0.0 162.1 jit_solution(10358306539701225386)
XLA Ops:
  0.6 0.0 copy-start.9
  0.6 0.0 copy-start.7
  0.7 0.0 copy-start.3
  0.7 0.0 copy-start.5
  0.7 3.5 %shard_map.157 = (f32[8,5120]{1,0:T(8,128)}, f32[1,4096]{1,0:T(1,128)}, f32[1,4096]{1,0:T(1,128)}) custom-call(s32[8]{0:T(128)} %refs_0_.4, s32[2,8]{1,0:T(2,128)} %bitcast.12, bf16[8,4096]{1,0:T(8,128)(2,1)} %refs_2_.3, bf16[8,64,256]{2,1,0:T(8,128)(2,1)} %refs_2_.5, bf16[8,256]{1,0:T(8,128)(2,1)} %refs_4_.5, bf16[8,64,256]{2,1,0:T(8,128)(2,1)} %refs_3_.6, ...), custom_call_target="tpu_custom_call" | custom-call | flops 100000000 | bytes 3000000 | tf_op jit(solution)/shard_map/pallas_call | solution.py:405
  4.2 2.7 %collective-permute-start = (f32[1,4096]{1,0:T(1,128)}, f32[1,4096]{1,0:T(1,128)S(1)}, u32[]{:S(2)}, u32[]{:S(2)}) collective-permute-start(f32[1,4096]{1,0:T(1,128)} %get-tuple-element.51), channel_id=1, source_target_pairs={{0,1},{1,2},{2,3},{3,4},{4,5},{5,6},{6,7},{7,8},{8,9},{9,10},{10,1... | collective-permute-start | bytes 49160 | tf_op jit(solution)/shard_map/ppermute | solution.py:445
  6.9 6.9 %collective-permute-start.1 = (f32[1,4096]{1,0:T(1,128)}, f32[1,4096]{1,0:T(1,128)S(1)}, u32[]{:S(2)}, u32[]{:S(2)}) collective-permute-start(f32[1,4096]{1,0:T(1,128)} %get-tuple-element.52), channel_id=1, source_target_pairs={{0,32},{1,33},{2,34},{3,35},{4,36},{5,37},{6,38},{7,39},{8,40},{9,... | collective-permute-start | bytes 49160 | tf_op jit(solution)/shard_map/ppermute | solution.py:445
  13.8 0.0 collective-permute-done.refs_1_
  13.8 1.3 collective-permute-done.1.refs_2_
  15.2 0.9 copy-done.10
  16.1 0.7 shard_map.158
  16.8 37.9 %all_to_all.10 = bf16[64,16,512]{2,1,0:T(8,128)(2,1)S(1)} all-to-all(bf16[64,16,512]{2,1,0:T(8,128)(2,1)S(1)} %bitcast.11), channel_id=1, replica_groups=mesh['dp'=4,'ep'=64] {'ep'}, dimensions={0} | all-to-all | bytes 2097152 | tf_op jit(solution)/shard_map/all_to_all | solution.py:451
  54.8 0.1 fusion
  54.8 1.4 collective-permute-start.2
  56.2 1.5 collective-permute-start.3
  57.7 0.0 collective-permute-start.5
  57.7 2.7 %collective-permute-start.6 = (bf16[512,512]{1,0:T(8,128)(2,1)S(1)}, bf16[512,512]{1,0:T(8,128)(2,1)S(1)}, u32[]{:S(2)}, u32[]{:S(2)}) collective-permute-start(bf16[512,512]{1,0:T(8,128)(2,1)S(1)} %bitcast.16), channel_id=1, source_target_pairs={{0,192},{64,0},{128,64},{192,128},{1,193},{65,1},{129,65},{193,129... | collective-permute-start | bytes 1572872 | tf_op jit(solution)/shard_map/ppermute | solution.py:445
  60.5 1.5 shard_map.161
  62.0 3.5 %collective-permute-start.4 = (bf16[128,256]{1,0:T(8,128)(2,1)S(1)}, bf16[128,256]{1,0:T(8,128)(2,1)S(1)}, u32[]{:S(2)}, u32[]{:S(2)}) collective-permute-start(bf16[128,256]{1,0:T(8,128)(2,1)S(1)} %get-tuple-element.61), channel_id=1, source_target_pairs={{0,1},{1,2},{2,3},{3,4},{4,5},{5,6},{6,7},{7,8},{8,9},{9,10},{10,1... | collective-permute-start | bytes 196616 | tf_op jit(solution)/shard_map/ppermute | solution.py:445
  65.5 1.9 %copy-done.1 = bf16[1,4096,384]{2,1,0:T(8,128)(2,1)S(1)} copy-done((bf16[1,4096,384]{2,1,0:T(8,128)(2,1)S(1)}, bf16[1,4096,384]{2,1,0:T(8,128)(2,1)}, u32[]{:S(2)}) %copy-start.1) | copy-done | bytes 3145752
  67.4 1.9 %copy-done.2 = bf16[1,384,4096]{2,1,0:T(8,128)(2,1)S(1)} copy-done((bf16[1,384,4096]{2,1,0:T(8,128)(2,1)S(1)}, bf16[1,384,4096]{2,1,0:T(8,128)(2,1)}, u32[]{:S(2)}) %copy-start.2) | copy-done | bytes 3145752
  69.2 2.5 %shard_map.160 = (bf16[512,512]{1,0:T(8,128)(2,1)S(1)}, bf16[512,512]{1,0:T(8,128)(2,1)S(1)}) custom-call(bf16[1024,512]{1,0:T(8,128)(2,1)S(1)} %bitcast.8, bf16[1,4096,384]{2,1,0:T(8,128)(2,1)S(1)} %copy-done, bf16[1,4096,384]{2,1,0:T(8,128)(2,1)S(1)} %copy-done.1, bf16[1,384,4096]{2,1,0:T(8,128)(2,1)S(1)} %copy-done.2), custom_call_target="tpu_custom_call" | custom-call | flops 1207959552 | bytes 11534336 | tf_op jit(solution)/shard_map/pallas_call | solution.py:405
  71.7 0.0 collective-permute-done.4.refs_1_
  71.7 0.0 collective-permute-done.2.refs_0_
  71.7 0.0 collective-permute-done.3.refs_3_
  71.7 0.9 collective-permute-start.7
  72.7 0.0 collective-permute-start.10
  72.7 2.7 %collective-permute-start.11 = (bf16[512,512]{1,0:T(8,128)(2,1)S(1)}, bf16[512,512]{1,0:T(8,128)(2,1)S(1)}, u32[]{:S(2)}, u32[]{:S(2)}) collective-permute-start(bf16[512,512]{1,0:T(8,128)(2,1)S(1)} %collective-permute-done.3.refs_3_), channel_id=1, source_target_pairs={{0,192},{64,0},{128,64},{192,128},{1,193},{65,1},{129,65},{193,129... | collective-permute-start | bytes 1572872 | tf_op jit(solution)/shard_map/ppermute | solution.py:445
  75.3 4.2 %collective-permute-done.5.refs_1_ = bf16[512,512]{1,0:T(8,128)(2,1)S(1)} collective-permute-done((bf16[512,512]{1,0:T(8,128)(2,1)S(1)}, bf16[512,512]{1,0:T(8,128)(2,1)S(1)}, u32[]{:S(2)}, u32[]{:S(2)}) %collective-permute-start.5) | collective-permute-done | bytes 524320 | tf_op jit(solution)/shard_map/ppermute | solution.py:445
  79.6 0.0 collective-permute-done.6.refs_2_
  79.6 0.0 collective-permute-done.7.refs_2_
  79.6 4.6 %shard_map.162 = (bf16[512,512]{1,0:T(8,128)(2,1)S(1)}, bf16[512,512]{1,0:T(8,128)(2,1)S(1)}, bf16[512,512]{1,0:T(8,128)(2,1)S(1)}, bf16[512,512]{1,0:T(8,128)(2,1)S(1)}) custom-call(bf16[512,512]{1,0:T(8,128)(2,1)S(1)} %collective-permute-done.2.refs_0_, bf16[512,512]{1,0:T(8,128)(2,1)S(1)} %collective-permute-done.5.refs_1_, ...), custom_call_target="tpu_custom_call" | custom-call | flops 2415919104 | bytes 13631488 | tf_op jit(solution)/shard_map/pallas_call | solution.py:405
  84.2 1.0 collective-permute-start.8
  85.2 1.7 %collective-permute-start.9 = (bf16[512,512]{1,0:T(8,128)(2,1)S(1)}, bf16[512,512]{1,0:T(8,128)(2,1)S(1)}, u32[]{:S(2)}, u32[]{:S(2)}) collective-permute-start(bf16[512,512]{1,0:T(8,128)(2,1)S(1)} %get-tuple-element.71), channel_id=1, source_target_pairs={{0,192},{64,0},{128,64},{192,128},{1,193},{65,1},{129,65},{193,129... | collective-permute-start | bytes 1572872 | tf_op jit(solution)/shard_map/ppermute | solution.py:445
  86.9 3.9 %collective-permute-done.10.refs_0_ = bf16[512,512]{1,0:T(8,128)(2,1)S(1)} collective-permute-done((bf16[512,512]{1,0:T(8,128)(2,1)S(1)}, bf16[512,512]{1,0:T(8,128)(2,1)S(1)}, u32[]{:S(2)}, u32[]{:S(2)}) %collective-permute-start.10) | collective-permute-done | bytes 524320 | tf_op jit(solution)/shard_map/ppermute | solution.py:445
  90.8 0.0 collective-permute-done.11.refs_1_
  90.8 2.5 %shard_map.163 = (bf16[256,512]{1,0:T(8,128)(2,1)S(1)}, bf16[256,512]{1,0:T(8,128)(2,1)S(1)}, bf16[256,512]{1,0:T(8,128)(2,1)S(1)}, bf16[256,512]{1,0:T(8,128)(2,1)S(1)}) custom-call(bf16[512,512]{1,0:T(8,128)(2,1)S(1)} %collective-permute-done.10.refs_0_, bf16[512,512]{1,0:T(8,128)(2,1)S(1)} %collective-permute-done.11.refs_1_, ...), custom_call_target="tpu_custom_call" | custom-call | flops 1207959552 | bytes 11534336 | tf_op jit(solution)/shard_map/pallas_call | solution.py:405
  93.3 0.0 copy-start.8
  93.3 0.0 copy-start.11
  93.3 1.0 collective-permute-start.12
  94.3 1.7 %collective-permute-start.13 = (bf16[256,512]{1,0:T(8,128)(2,1)S(1)}, bf16[256,512]{1,0:T(8,128)(2,1)S(1)}, u32[]{:S(2)}, u32[]{:S(2)}) collective-permute-start(bf16[256,512]{1,0:T(8,128)(2,1)S(1)} %get-tuple-element.79), channel_id=1, source_target_pairs={{0,192},{64,0},{128,64},{192,128},{1,193},{65,1},{129,65},{193,129... | collective-permute-start | bytes 786440 | tf_op jit(solution)/shard_map/ppermute | solution.py:445
  96.0 0.0 collective-permute-start.15
  96.0 6.0 %collective-permute-done.8.refs_2_ = bf16[512,512]{1,0:T(8,128)(2,1)S(1)} collective-permute-done((bf16[512,512]{1,0:T(8,128)(2,1)S(1)}, bf16[512,512]{1,0:T(8,128)(2,1)S(1)}, u32[]{:S(2)}, u32[]{:S(2)}) %collective-permute-start.8) | collective-permute-done | bytes 524320 | tf_op jit(solution)/shard_map/ppermute | solution.py:445
  102.0 1.4 collective-permute-start.16
  103.4 0.0 collective-permute-done.9.refs_3_
  103.4 4.2 %collective-permute-done.12.refs_2_ = bf16[256,512]{1,0:T(8,128)(2,1)S(1)} collective-permute-done((bf16[256,512]{1,0:T(8,128)(2,1)S(1)}, bf16[256,512]{1,0:T(8,128)(2,1)S(1)}, u32[]{:S(2)}, u32[]{:S(2)}) %collective-permute-start.12) | collective-permute-done | bytes 262176 | tf_op jit(solution)/shard_map/ppermute | solution.py:445
  107.6 0.0 collective-permute-done.13.refs_3_
  107.6 0.1 shard_map.164
  107.8 1.0 collective-permute-start.14
  108.8 1.9 %collective-permute-start.18 = (bf16[256,512]{1,0:T(8,128)(2,1)S(1)}, bf16[256,512]{1,0:T(8,128)(2,1)S(1)}, u32[]{:S(2)}, u32[]{:S(2)}) collective-permute-start(bf16[256,512]{1,0:T(8,128)(2,1)S(1)} %get-tuple-element.85), channel_id=1, source_target_pairs={{0,192},{64,0},{128,64},{192,128},{1,193},{65,1},{129,65},{193,129... | collective-permute-start | bytes 786440 | tf_op jit(solution)/shard_map/ppermute | solution.py:445
  110.7 2.5 %collective-permute-done.15.refs_2_ = bf16[256,512]{1,0:T(8,128)(2,1)S(1)} collective-permute-done((bf16[256,512]{1,0:T(8,128)(2,1)S(1)}, bf16[256,512]{1,0:T(8,128)(2,1)S(1)}, u32[]{:S(2)}, u32[]{:S(2)}) %collective-permute-start.15) | collective-permute-done | bytes 262176 | tf_op jit(solution)/shard_map/ppermute | solution.py:445
  113.3 0.0 collective-permute-done.16.refs_3_
  113.3 0.1 shard_map.165
  113.4 1.0 collective-permute-start.17
  114.4 1.7 %collective-permute-start.19 = (bf16[256,512]{1,0:T(8,128)(2,1)S(1)}, bf16[256,512]{1,0:T(8,128)(2,1)S(1)}, u32[]{:S(2)}, u32[]{:S(2)}) collective-permute-start(bf16[256,512]{1,0:T(8,128)(2,1)S(1)} %get-tuple-element.89), channel_id=1, source_target_pairs={{0,192},{64,0},{128,64},{192,128},{1,193},{65,1},{129,65},{193,129... | collective-permute-start | bytes 786440 | tf_op jit(solution)/shard_map/ppermute | solution.py:445
  116.1 0.9 shard_map.159
  117.0 1.3 shard_map.167
  118.3 0.6 collective-permute-done.14.refs_4_
  118.9 5.6 %collective-permute-done.17.refs_5_ = bf16[256,512]{1,0:T(8,128)(2,1)S(1)} collective-permute-done((bf16[256,512]{1,0:T(8,128)(2,1)S(1)}, bf16[256,512]{1,0:T(8,128)(2,1)S(1)}, u32[]{:S(2)}, u32[]{:S(2)}) %collective-permute-start.17) | collective-permute-done | bytes 262176 | tf_op jit(solution)/shard_map/ppermute | solution.py:445
  124.5 0.0 collective-permute-done.18.refs_6_
  124.5 0.0 collective-permute-done.19.refs_7_
  124.5 0.9 shard_map.166
  125.4 35.6 %all_to_all.11 = bf16[64,16,512]{2,1,0:T(8,128)(2,1)S(1)} all-to-all(bf16[64,16,512]{2,1,0:T(8,128)(2,1)S(1)} %bitcast.10), channel_id=1, replica_groups=mesh['dp'=4,'ep'=64] {'ep'}, dimensions={0} | all-to-all | bytes 2097152 | tf_op jit(solution)/shard_map/all_to_all | solution.py:451
  161.0 1.1 shard_map.168
  (15 shorter events, 0.0 us)
Async XLA Ops:
  0.6 59.8 %copy-start.9 = (s32[8]{0:T(128)S(1)}, s32[8]{0:T(128)}, u32[]{:S(2)}) copy-start(s32[8]{0:T(128)} %refs_0_.4) | copy-start | bytes 100
  0.6 59.8 %copy-start.7 = (s32[8,2]{0,1:T(2,128)S(1)}, s32[8,2]{0,1:T(2,128)}, u32[]{:S(2)}) copy-start(s32[8,2]{0,1:T(2,128)} %param.21) | copy-start | bytes 196
  0.7 59.8 %copy-start.3 = (bf16[8,64,256]{2,1,0:T(8,128)(2,1)S(1)}, bf16[8,64,256]{2,1,0:T(8,128)(2,1)}, u32[]{:S(2)}) copy-start(bf16[8,64,256]{2,1,0:T(8,128)(2,1)} %refs_2_.5) | copy-start | bytes 786436
  0.7 59.8 %copy-start.5 = (bf16[8,256]{1,0:T(8,128)(2,1)S(1)}, bf16[8,256]{1,0:T(8,128)(2,1)}, u32[]{:S(2)}) copy-start(bf16[8,256]{1,0:T(8,128)(2,1)} %refs_4_.5) | copy-start | bytes 12292
  0.7 59.8 %copy-start.4 = (bf16[8,64,256]{2,1,0:T(8,128)(2,1)S(1)}, bf16[8,64,256]{2,1,0:T(8,128)(2,1)}, u32[]{:S(2)}) copy-start(bf16[8,64,256]{2,1,0:T(8,128)(2,1)} %refs_3_.6) | copy-start | bytes 786436
  0.7 59.8 %copy-start.6 = (bf16[8,256]{1,0:T(8,128)(2,1)S(1)}, bf16[8,256]{1,0:T(8,128)(2,1)}, u32[]{:S(2)}) copy-start(bf16[8,256]{1,0:T(8,128)(2,1)} %refs_5_.4) | copy-start | bytes 12292
  0.7 64.8 %copy-start = (bf16[1,4096,384]{2,1,0:T(8,128)(2,1)S(1)}, bf16[1,4096,384]{2,1,0:T(8,128)(2,1)}, u32[]{:S(2)}) copy-start(bf16[1,4096,384]{2,1,0:T(8,128)(2,1)} %refs_2_.6) | copy-start | bytes 9437188
  4.2 9.6 %collective-permute-start = (f32[1,4096]{1,0:T(1,128)}, f32[1,4096]{1,0:T(1,128)S(1)}, u32[]{:S(2)}, u32[]{:S(2)}) collective-permute-start(f32[1,4096]{1,0:T(1,128)} %get-tuple-element.51), channel_id=1, source_target_pairs={{0,1},{1,2},{2,3},{3,4},{4,5},{5,6},{6,7},{7,8},{8,9},{9,10},{10,1... | collective-permute-start | bytes 49160 | tf_op jit(solution)/shard_map/ppermute | solution.py:445
  6.9 8.2 %collective-permute-start.1 = (f32[1,4096]{1,0:T(1,128)}, f32[1,4096]{1,0:T(1,128)S(1)}, u32[]{:S(2)}, u32[]{:S(2)}) collective-permute-start(f32[1,4096]{1,0:T(1,128)} %get-tuple-element.52), channel_id=1, source_target_pairs={{0,32},{1,33},{2,34},{3,35},{4,36},{5,37},{6,38},{7,39},{8,40},{9,... | collective-permute-start | bytes 49160 | tf_op jit(solution)/shard_map/ppermute | solution.py:445
  15.2 0.9 copy-start.10
  54.8 16.9 %collective-permute-start.2 = (bf16[512,512]{1,0:T(8,128)(2,1)S(1)}, bf16[512,512]{1,0:T(8,128)(2,1)S(1)}, u32[]{:S(2)}, u32[]{:S(2)}) collective-permute-start(bf16[512,512]{1,0:T(8,128)(2,1)S(1)} %bitcast.15), channel_id=1, source_target_pairs={{0,64},{64,128},{128,192},{192,0},{1,65},{65,129},{129,193},{193,1... | collective-permute-start | bytes 1572872 | tf_op jit(solution)/shard_map/ppermute | solution.py:445
  56.2 15.5 %collective-permute-start.3 = (bf16[512,512]{1,0:T(8,128)(2,1)S(1)}, bf16[512,512]{1,0:T(8,128)(2,1)S(1)}, u32[]{:S(2)}, u32[]{:S(2)}) collective-permute-start(bf16[512,512]{1,0:T(8,128)(2,1)S(1)} %bitcast.17), channel_id=1, source_target_pairs={{0,192},{64,0},{128,64},{192,128},{1,193},{65,1},{129,65},{193,129... | collective-permute-start | bytes 1572872 | tf_op jit(solution)/shard_map/ppermute | solution.py:445
  57.7 21.8 %collective-permute-start.5 = (bf16[512,512]{1,0:T(8,128)(2,1)S(1)}, bf16[512,512]{1,0:T(8,128)(2,1)S(1)}, u32[]{:S(2)}, u32[]{:S(2)}) collective-permute-start(bf16[512,512]{1,0:T(8,128)(2,1)S(1)} %bitcast.18), channel_id=1, source_target_pairs={{0,64},{64,128},{128,192},{192,0},{1,65},{65,129},{129,193},{193,1... | collective-permute-start | bytes 1572872 | tf_op jit(solution)/shard_map/ppermute | solution.py:445
  57.7 21.8 %collective-permute-start.6 = (bf16[512,512]{1,0:T(8,128)(2,1)S(1)}, bf16[512,512]{1,0:T(8,128)(2,1)S(1)}, u32[]{:S(2)}, u32[]{:S(2)}) collective-permute-start(bf16[512,512]{1,0:T(8,128)(2,1)S(1)} %bitcast.16), channel_id=1, source_target_pairs={{0,192},{64,0},{128,64},{192,128},{1,193},{65,1},{129,65},{193,129... | collective-permute-start | bytes 1572872 | tf_op jit(solution)/shard_map/ppermute | solution.py:445
  62.0 9.7 %collective-permute-start.4 = (bf16[128,256]{1,0:T(8,128)(2,1)S(1)}, bf16[128,256]{1,0:T(8,128)(2,1)S(1)}, u32[]{:S(2)}, u32[]{:S(2)}) collective-permute-start(bf16[128,256]{1,0:T(8,128)(2,1)S(1)} %get-tuple-element.61), channel_id=1, source_target_pairs={{0,1},{1,2},{2,3},{3,4},{4,5},{5,6},{6,7},{7,8},{8,9},{9,10},{10,1... | collective-permute-start | bytes 196616 | tf_op jit(solution)/shard_map/ppermute | solution.py:445
  65.5 1.9 %copy-start.1 = (bf16[1,4096,384]{2,1,0:T(8,128)(2,1)S(1)}, bf16[1,4096,384]{2,1,0:T(8,128)(2,1)}, u32[]{:S(2)}) copy-start(bf16[1,4096,384]{2,1,0:T(8,128)(2,1)} %refs_3_.7) | copy-start | bytes 9437188
  67.3 1.9 %copy-start.2 = (bf16[1,384,4096]{2,1,0:T(8,128)(2,1)S(1)}, bf16[1,384,4096]{2,1,0:T(8,128)(2,1)}, u32[]{:S(2)}) copy-start(bf16[1,384,4096]{2,1,0:T(8,128)(2,1)} %refs_4_.7) | copy-start | bytes 9437188
  71.7 7.8 %collective-permute-start.7 = (bf16[128,256]{1,0:T(8,128)(2,1)S(1)}, bf16[128,256]{1,0:T(8,128)(2,1)S(1)}, u32[]{:S(2)}, u32[]{:S(2)}) collective-permute-start(bf16[128,256]{1,0:T(8,128)(2,1)S(1)} %get-tuple-element.66), channel_id=1, source_target_pairs={{0,32},{1,33},{2,34},{3,35},{4,36},{5,37},{6,38},{7,39},{8,40},{9,... | collective-permute-start | bytes 196616 | tf_op jit(solution)/shard_map/ppermute | solution.py:445
  72.7 18.1 %collective-permute-start.10 = (bf16[512,512]{1,0:T(8,128)(2,1)S(1)}, bf16[512,512]{1,0:T(8,128)(2,1)S(1)}, u32[]{:S(2)}, u32[]{:S(2)}) collective-permute-start(bf16[512,512]{1,0:T(8,128)(2,1)S(1)} %collective-permute-done.2.refs_0_), channel_id=1, source_target_pairs={{0,64},{64,128},{128,192},{192,0},{1,65},{65,129},{129,193},{193,1... | collective-permute-start | bytes 1572872 | tf_op jit(solution)/shard_map/ppermute | solution.py:445
  72.7 18.1 %collective-permute-start.11 = (bf16[512,512]{1,0:T(8,128)(2,1)S(1)}, bf16[512,512]{1,0:T(8,128)(2,1)S(1)}, u32[]{:S(2)}, u32[]{:S(2)}) collective-permute-start(bf16[512,512]{1,0:T(8,128)(2,1)S(1)} %collective-permute-done.3.refs_3_), channel_id=1, source_target_pairs={{0,192},{64,0},{128,64},{192,128},{1,193},{65,1},{129,65},{193,129... | collective-permute-start | bytes 1572872 | tf_op jit(solution)/shard_map/ppermute | solution.py:445
  84.2 17.9 %collective-permute-start.8 = (bf16[512,512]{1,0:T(8,128)(2,1)S(1)}, bf16[512,512]{1,0:T(8,128)(2,1)S(1)}, u32[]{:S(2)}, u32[]{:S(2)}) collective-permute-start(bf16[512,512]{1,0:T(8,128)(2,1)S(1)} %get-tuple-element.70), channel_id=1, source_target_pairs={{0,64},{64,128},{128,192},{192,0},{1,65},{65,129},{129,193},{193,1... | collective-permute-start | bytes 1572872 | tf_op jit(solution)/shard_map/ppermute | solution.py:445
  85.2 18.2 %collective-permute-start.9 = (bf16[512,512]{1,0:T(8,128)(2,1)S(1)}, bf16[512,512]{1,0:T(8,128)(2,1)S(1)}, u32[]{:S(2)}, u32[]{:S(2)}) collective-permute-start(bf16[512,512]{1,0:T(8,128)(2,1)S(1)} %get-tuple-element.71), channel_id=1, source_target_pairs={{0,192},{64,0},{128,64},{192,128},{1,193},{65,1},{129,65},{193,129... | collective-permute-start | bytes 1572872 | tf_op jit(solution)/shard_map/ppermute | solution.py:445
  93.3 22.9 %copy-start.8 = (s32[8,8]{1,0:T(8,128)S(1)}, s32[8,8]{1,0:T(8,128)}, u32[]{:S(2)}) copy-start(s32[8,8]{1,0:T(8,128)} %refs_0_.3) | copy-start | bytes 772
  93.3 22.9 %copy-start.11 = (f32[8,8]{1,0:T(8,128)S(1)}, f32[8,8]{1,0:T(8,128)}, u32[]{:S(2)}) copy-start(f32[8,8]{1,0:T(8,128)} %refs_1_.2) | copy-start | bytes 772
  93.3 14.4 %collective-permute-start.12 = (bf16[256,512]{1,0:T(8,128)(2,1)S(1)}, bf16[256,512]{1,0:T(8,128)(2,1)S(1)}, u32[]{:S(2)}, u32[]{:S(2)}) collective-permute-start(bf16[256,512]{1,0:T(8,128)(2,1)S(1)} %get-tuple-element.78), channel_id=1, source_target_pairs={{0,64},{64,128},{128,192},{192,0},{1,65},{65,129},{129,193},{193,1... | collective-permute-start | bytes 786440 | tf_op jit(solution)/shard_map/ppermute | solution.py:445
  94.3 13.3 %collective-permute-start.13 = (bf16[256,512]{1,0:T(8,128)(2,1)S(1)}, bf16[256,512]{1,0:T(8,128)(2,1)S(1)}, u32[]{:S(2)}, u32[]{:S(2)}) collective-permute-start(bf16[256,512]{1,0:T(8,128)(2,1)S(1)} %get-tuple-element.79), channel_id=1, source_target_pairs={{0,192},{64,0},{128,64},{192,128},{1,193},{65,1},{129,65},{193,129... | collective-permute-start | bytes 786440 | tf_op jit(solution)/shard_map/ppermute | solution.py:445
  96.0 17.2 %collective-permute-start.15 = (bf16[256,512]{1,0:T(8,128)(2,1)S(1)}, bf16[256,512]{1,0:T(8,128)(2,1)S(1)}, u32[]{:S(2)}, u32[]{:S(2)}) collective-permute-start(bf16[256,512]{1,0:T(8,128)(2,1)S(1)} %get-tuple-element.83), channel_id=1, source_target_pairs={{0,64},{64,128},{128,192},{192,0},{1,65},{65,129},{129,193},{193,1... | collective-permute-start | bytes 786440 | tf_op jit(solution)/shard_map/ppermute | solution.py:445
  102.0 11.2 %collective-permute-start.16 = (bf16[256,512]{1,0:T(8,128)(2,1)S(1)}, bf16[256,512]{1,0:T(8,128)(2,1)S(1)}, u32[]{:S(2)}, u32[]{:S(2)}) collective-permute-start(bf16[256,512]{1,0:T(8,128)(2,1)S(1)} %get-tuple-element.84), channel_id=1, source_target_pairs={{0,192},{64,0},{128,64},{192,128},{1,193},{65,1},{129,65},{193,129... | collective-permute-start | bytes 786440 | tf_op jit(solution)/shard_map/ppermute | solution.py:445
  107.8 11.1 %collective-permute-start.14 = (bf16[256,512]{1,0:T(8,128)(2,1)S(1)}, bf16[256,512]{1,0:T(8,128)(2,1)S(1)}, u32[]{:S(2)}, u32[]{:S(2)}) collective-permute-start(bf16[256,512]{1,0:T(8,128)(2,1)S(1)} %get-tuple-element.82), channel_id=1, source_target_pairs={{0,64},{64,128},{128,192},{192,0},{1,65},{65,129},{129,193},{193,1... | collective-permute-start | bytes 786440 | tf_op jit(solution)/shard_map/ppermute | solution.py:445
  108.8 15.7 %collective-permute-start.18 = (bf16[256,512]{1,0:T(8,128)(2,1)S(1)}, bf16[256,512]{1,0:T(8,128)(2,1)S(1)}, u32[]{:S(2)}, u32[]{:S(2)}) collective-permute-start(bf16[256,512]{1,0:T(8,128)(2,1)S(1)} %get-tuple-element.85), channel_id=1, source_target_pairs={{0,192},{64,0},{128,64},{192,128},{1,193},{65,1},{129,65},{193,129... | collective-permute-start | bytes 786440 | tf_op jit(solution)/shard_map/ppermute | solution.py:445
  113.4 11.1 %collective-permute-start.17 = (bf16[256,512]{1,0:T(8,128)(2,1)S(1)}, bf16[256,512]{1,0:T(8,128)(2,1)S(1)}, u32[]{:S(2)}, u32[]{:S(2)}) collective-permute-start(bf16[256,512]{1,0:T(8,128)(2,1)S(1)} %get-tuple-element.88), channel_id=1, source_target_pairs={{0,64},{64,128},{128,192},{192,0},{1,65},{65,129},{129,193},{193,1... | collective-permute-start | bytes 786440 | tf_op jit(solution)/shard_map/ppermute | solution.py:445
  114.4 10.1 %collective-permute-start.19 = (bf16[256,512]{1,0:T(8,128)(2,1)S(1)}, bf16[256,512]{1,0:T(8,128)(2,1)S(1)}, u32[]{:S(2)}, u32[]{:S(2)}) collective-permute-start(bf16[256,512]{1,0:T(8,128)(2,1)S(1)} %get-tuple-element.89), channel_id=1, source_target_pairs={{0,192},{64,0},{128,64},{192,128},{1,193},{65,1},{129,65},{193,129... | collective-permute-start | bytes 786440 | tf_op jit(solution)/shard_map/ppermute | solution.py:445
